TPU v7x, 128 devices: a whole 4x4x4 slice. The times are simulated.
128 devices in a mesh: lat: 8 (over x_hi, y), lon: 16 (over x_lo, z, core).
Axes of the slice: x: 4 (x_hi: 2, x_lo: 2; x = x_hi * 2 + x_lo), y: 4, z: 4, core: 2. Of those that a mesh axis runs over, the one named last changes fastest.
Arguments:
- tokens: bfloat16 [32768, 1024], P(('lat', 'lon')), may hold values from -8 to 8
- attn_gain: float32 [1024], replicated, may hold values from 0.1 to 1.9
- w_query: bfloat16 [1024, 1024], replicated, may hold values from -1 to 1
- w_key: bfloat16 [1024, 256], replicated, may hold values from -4 to 4
- w_value: bfloat16 [1024, 256], replicated, may hold values from -0.1875 to 0.1875
- w_out: bfloat16 [1024, 1024], replicated, may hold values from -0.1875 to 0.1875
- head_rate: float32 [16], replicated, may hold values from 0.00024414062 to 0.05
- obs_values: bfloat16 [16384, 128, 32], P(('lat', 'lon')), may hold values from -6 to 6
- tile_owner: int32 [16384, 1], P(('lat', 'lon')), may hold values from 0 to 127; in each aligned block of 128 rows (0 to 127, 128 to 255, ...) at most 2 rows name the same one
- tile_cell: int32 [16384], P(('lat', 'lon')), may hold values from 0 to 255
- tile_count: int32 [16384], P(('lat', 'lon')), may hold values from 1 to 128
- w_obs_in: bfloat16 [32, 1024], replicated, may hold values from -1 to 1
- w_obs_out: bfloat16 [1024, 1024], replicated, may hold values from -0.1875 to 0.1875
- mlp_gain: float32 [1024], replicated, may hold values from 0.1 to 1.9
- w_up: bfloat16 [1024, 4096], replicated, may hold values from -0.1875 to 0.1875
- w_down: bfloat16 [4096, 1024], replicated, may hold values from -0.09375 to 0.09375
Outputs:
- updated: bfloat16 [32768, 1024], P(('lat', 'lon'))
Inputs may be any that keep to these rules, and one draw needn't show every extreme that they name: `tile_owner`: the 128 tiles of one device name one owner at most 2 times; some owner is named exactly 2 times by some device.
All inputs are finite; a program needn't handle non-finite values.
Results may differ from a plain program's by a relative error of at most 0.0095.
The roundings to bfloat16 on the way count: a program that leaves them out, or rounds other values in their place, can miss the bound.
Values may be sent and summed in bfloat16 or wider, within the bound.
No kernel may reach another device: no remote copies, remote signals or barrier semaphores. Data moves between devices by JAX's collectives and lax.ppermute only.
A program may use at most 128 MiB of HBM per device.

v0:
```python
import math

import jax
import jax.numpy as jnp
from jax import lax
from jax.sharding import PartitionSpec as P


def scaled_rows(row_data, row_gain):
    as_float = row_data.astype(jnp.float32)
    mean_square = jnp.mean(as_float * as_float, axis=-1, keepdims=True)
    return (as_float * lax.rsqrt(mean_square + 1e-05) * row_gain).astype(jnp.bfloat16)


def pool_tiles(obs_tiles, tile_counts, w_obs_in):
    tile_total, tile_rows, feature_count = obs_tiles.shape
    block_rows = math.gcd(tile_total, 32)

    def one_block(block_args):
        value_block, count_block = block_args
        activity = jax.nn.gelu(
            jnp.dot(
                value_block.reshape(block_rows * tile_rows, feature_count),
                w_obs_in,
                preferred_element_type=jnp.float32,
            )
        )
        activity = activity.reshape(block_rows, tile_rows, -1)
        live_rows = (jnp.arange(tile_rows, dtype=jnp.int32)[None, :] < count_block[:, None]).astype(
            jnp.float32
        )
        summed = jnp.sum(activity * live_rows[:, :, None], axis=1)
        return (summed / jnp.maximum(count_block, 1).astype(jnp.float32)[:, None]).astype(
            jnp.bfloat16
        )

    pooled = lax.map(
        one_block,
        (
            obs_tiles.reshape(tile_total // block_rows, block_rows, tile_rows, feature_count),
            tile_counts.reshape(tile_total // block_rows, block_rows),
        ),
    )
    return pooled.reshape(tile_total, -1)


def observation_update(
    obs_values, tile_owner, tile_cell, tile_count, w_obs_in, w_obs_out, tok_rows
):
    owners = lax.axis_size("lat") * lax.axis_size("lon")
    tiles_here = obs_values.shape[0]
    capacity = max(2, 2 * tiles_here // owners)
    owner_index = tile_owner[:, 0]
    owner_hits = (owner_index[:, None] == jnp.arange(owners, dtype=jnp.int32)[None, :]).astype(
        jnp.int32
    )
    before = jnp.cumsum(owner_hits, axis=0) - owner_hits
    order_rank = jnp.sum(before * owner_hits, axis=1)
    slot_index = owner_index * capacity + order_rank
    slot_count = owners * capacity
    cell_index = jnp.zeros((slot_count,), jnp.int32).at[slot_index].set(tile_cell)
    packed = (
        jnp.zeros((slot_count,) + obs_values.shape[1:], jnp.bfloat16).at[slot_index].set(obs_values)
    )
    count_slots = jnp.zeros((slot_count,), jnp.int32).at[slot_index].set(tile_count)
    arrived, arrived_cells, arrived_counts = (
        lax.all_to_all(packed, ("lat", "lon"), split_axis=0, concat_axis=0, tiled=True),
        lax.all_to_all(cell_index, ("lat", "lon"), split_axis=0, concat_axis=0, tiled=True),
        lax.all_to_all(count_slots, ("lat", "lon"), split_axis=0, concat_axis=0, tiled=True),
    )
    pooled = pool_tiles(arrived, arrived_counts, w_obs_in)
    increment = jnp.dot(pooled, w_obs_out, preferred_element_type=jnp.float32)
    return jax.ops.segment_sum(increment, arrived_cells, num_segments=tok_rows)


def cycle_attention(
    query_rows, key_rows, value_rows, head_rate, tok_rows, band_rows, head_size, kv_heads
):
    head_count = head_rate.shape[0]
    group_size = head_count // kv_heads
    inv_scale = 1.0 / math.sqrt(head_size)
    rate_table = head_rate.reshape(kv_heads, group_size)
    query_position = lax.axis_index("lon") * tok_rows + jnp.arange(tok_rows, dtype=jnp.int32)
    grouped = query_rows.reshape(tok_rows, kv_heads, group_size, head_size)
    start_state = (
        jnp.full((kv_heads, group_size, tok_rows), -jnp.inf, jnp.float32),
        jnp.zeros((kv_heads, group_size, tok_rows), jnp.float32),
        jnp.zeros((kv_heads, group_size, tok_rows, head_size), jnp.float32),
    )
    running = start_state
    piece = (
        lax.all_gather(key_rows, "lon", axis=0, tiled=True),
        lax.all_gather(value_rows, "lon", axis=0, tiled=True),
    )
    piece_rows = piece[0].shape[0]
    sub_rows = math.gcd(piece_rows, 512)
    key_blocks = piece[0].reshape(piece_rows // sub_rows, sub_rows, kv_heads, head_size)
    value_blocks = piece[1].reshape(piece_rows // sub_rows, sub_rows, kv_heads, head_size)
    offsets = jnp.arange(piece_rows // sub_rows, dtype=jnp.int32) * sub_rows

    def inner_step(carry_state, block_item):
        row_top, weight_sum, weighted = carry_state
        key_block, value_block, block_first = block_item
        scores = (
            jnp.einsum("qkgd,skd->kgqs", grouped, key_block, preferred_element_type=jnp.float32)
            * inv_scale
        )
        distance = jnp.abs(
            query_position[:, None] - (block_first + jnp.arange(sub_rows, dtype=jnp.int32))[None, :]
        )
        distance = jnp.minimum(distance, band_rows - distance).astype(jnp.float32)
        scores = scores - rate_table[:, :, None, None] * distance[None, None]
        new_top = jnp.maximum(row_top, jnp.max(scores, axis=-1))
        shrink = jnp.exp(row_top - new_top)
        weights = jnp.exp(scores - new_top[..., None])
        weight_sum = weight_sum * shrink + jnp.sum(weights, axis=-1)
        weighted = weighted * shrink[..., None] + jnp.einsum(
            "kgqs,skd->kgqd",
            weights.astype(jnp.bfloat16),
            value_block,
            preferred_element_type=jnp.float32,
        )
        return ((new_top, weight_sum, weighted), None)

    running, _ = lax.scan(inner_step, running, (key_blocks, value_blocks, offsets))
    row_top, weight_sum, weighted = running
    context = weighted / weight_sum[..., None]
    return (
        jnp.transpose(context, (2, 0, 1, 3))
        .reshape(tok_rows, head_count * head_size)
        .astype(jnp.bfloat16)
    )


def shards(
    tokens,
    attn_gain,
    w_query,
    w_key,
    w_value,
    w_out,
    head_rate,
    obs_values,
    tile_owner,
    tile_cell,
    tile_count,
    w_obs_in,
    w_obs_out,
    mlp_gain,
    w_up,
    w_down,
):
    tok_rows = tokens.shape[0]
    head_count = head_rate.shape[0]
    head_size = w_query.shape[1] // head_count
    kv_heads = w_key.shape[1] // head_size
    band_rows = tok_rows * lax.axis_size("lon")
    update = observation_update(
        obs_values, tile_owner, tile_cell, tile_count, w_obs_in, w_obs_out, tok_rows
    )
    normed = scaled_rows(tokens, attn_gain)
    query_rows = jnp.dot(normed, w_query, preferred_element_type=jnp.float32).astype(jnp.bfloat16)
    key_rows = jnp.dot(normed, w_key, preferred_element_type=jnp.float32).astype(jnp.bfloat16)
    value_rows = jnp.dot(normed, w_value, preferred_element_type=jnp.float32).astype(jnp.bfloat16)
    context = cycle_attention(
        query_rows, key_rows, value_rows, head_rate, tok_rows, band_rows, head_size, kv_heads
    )
    attended = jnp.dot(context, w_out, preferred_element_type=jnp.float32)
    mixed_rows = (tokens.astype(jnp.float32) + attended + update).astype(jnp.bfloat16)
    mixed_rows = lax.optimization_barrier(mixed_rows)
    normed_mlp = scaled_rows(mixed_rows, mlp_gain)
    hidden = jax.nn.gelu(jnp.dot(normed_mlp, w_up, preferred_element_type=jnp.float32)).astype(
        jnp.bfloat16
    )
    return (
        mixed_rows.astype(jnp.float32) + jnp.dot(hidden, w_down, preferred_element_type=jnp.float32)
    ).astype(jnp.bfloat16)


def solution(mesh):
    return jax.shard_map(
        shards,
        mesh=mesh,
        in_specs=(
            P(("lat", "lon"), None),
            P(),
            P(),
            P(),
            P(),
            P(),
            P(),
            P(("lat", "lon"), None, None),
            P(("lat", "lon"), None),
            P(("lat", "lon")),
            P(("lat", "lon")),
            P(),
            P(),
            P(),
            P(),
            P(),
        ),
        out_specs=P(("lat", "lon"), None),
        check_vma=False,
    )
```

profile of v0, /device:TPU:0, one launch (start us, length us, event | category | flops | bytes accessed | tf_op | source)
XLA Modules:
  0.0 382.7 jit_solution(10926604440558221850)
XLA Ops:
  14.5 11.1 %all-to-all-start.2 = ((s32[128,2,1]{1,2,0:T(1,128)}), s32[128,2,1]{1,2,0:T(1,128)S(1)}, u32[]{:S(2)}, u32[]{:S(2)}) async-start(s32[128,2,1]{1,2,0:T(1,128)} %bitcast.12), calls=%async_computation.2 | async-start | bytes 131072 | tf_op jit(solution)/shard_map/all_to_all | solution.py:69
  27.5 7.6 %all-to-all-done.2 = s32[128,2,1]{1,2,0:T(1,128)S(1)} async-done(((s32[128,2,1]{1,2,0:T(1,128)}), s32[128,2,1]{1,2,0:T(1,128)S(1)}, u32[]{:S(2)}, u32[]{:S(2)}) %all-to-all-start.2) | async-done | bytes 1056 | tf_op jit(solution)/shard_map/all_to_all | solution.py:69
  41.2 15.4 %scatter_fusion = bf16[256,128,32]{1,2,0:T(8,128)(2,1)} fusion(bf16[256,128,32]{1,2,0:T(8,128)(2,1)} %broadcast_in_dim.23, s32[128]{0:T(128)S(1)} %fusion.67, bf16[128,128,32]{1,2,0:T(8,128)(2,1)} %param.27), kind=kCustom, calls=%fused_computation.1 | custom fusion | bytes 3146240 | tf_op jit(solution)/shard_map/scatter | solution.py:63
  56.6 10.3 %all-to-all-start.1 = ((bf16[256,128,32]{1,2,0:T(8,128)(2,1)}), bf16[256,128,32]{1,2,0:T(8,128)(2,1)}, u32[]{:S(2)}, u32[]{:S(2)}) async-start(bf16[256,128,32]{1,2,0:T(8,128)(2,1)} %scatter_fusion), calls=%async_computation.1 | async-start | bytes 4194304 | tf_op jit(solution)/shard_map/all_to_all | solution.py:67
  71.5 26.0 %all-to-all-done.1 = bf16[256,128,32]{1,2,0:T(8,128)(2,1)} async-done(((bf16[256,128,32]{1,2,0:T(8,128)(2,1)}), bf16[256,128,32]{1,2,0:T(8,128)(2,1)}, u32[]{:S(2)}, u32[]{:S(2)}) %all-to-all-start.1) | async-done | bytes 2097184 | tf_op jit(solution)/shard_map/all_to_all | solution.py:67
  97.5 85.8 %while.25 = (s32[]{:T(128)}, bf16[8,32,1024]{2,1,0:T(8,128)(2,1)}, bf16[8,32,128,32]{2,3,1,0:T(8,128)(2,1)}, bf16[32,1024]{1,0:T(8,128)(2,1)S(1)}, s32[8,32]{1,0:T(8,128)S(1)}, /*index=5*/s32[]{:T(128)}) while((s32[]{:T(128)}, bf16[8,32,1024]{2,1,0:T(8,128)(2,1)}, bf16[8,32,128,32]{2,3,1,0:T(8,128)(2,1)}, bf16[32,1024]{1,0:T(8,128)(2,1)S(1)}, ...), condition=%wide.region_12.13_spmd, body=%wide.region_10.12_spmd.sunk | while | flops 310419520 | bytes 1737933 | solution.py:37
  99.9 7.6 %multiply_reduce_fusion.2 = f32[32,1024]{1,0:T(8,128)S(1)} fusion(f32[32,128]{1,0:T(8,128)S(1)} %fusion.107, bf16[4096,32]{1,0:T(8,128)(2,1)} %bitcast.92, bf16[32,1024]{1,0:T(8,128)(2,1)S(1)} %get-tuple-element.360), kind=kOutput, calls=%fused_computation.13.clone.1 | convolution fusion | flops 310345728 | bytes 475136 | tf_op jit(solution)/shard_map/while/body/eval_jaxpr/dot_general | solution.py:22
  110.6 7.6 %multiply_reduce_fusion.2 = f32[32,1024]{1,0:T(8,128)S(1)} fusion(f32[32,128]{1,0:T(8,128)S(1)} %fusion.107, bf16[4096,32]{1,0:T(8,128)(2,1)} %bitcast.92, bf16[32,1024]{1,0:T(8,128)(2,1)S(1)} %get-tuple-element.360), kind=kOutput, calls=%fused_computation.13.clone.1 | convolution fusion | flops 310345728 | bytes 475136 | tf_op jit(solution)/shard_map/while/body/eval_jaxpr/dot_general | solution.py:22
  121.3 7.6 %multiply_reduce_fusion.2 = f32[32,1024]{1,0:T(8,128)S(1)} fusion(f32[32,128]{1,0:T(8,128)S(1)} %fusion.107, bf16[4096,32]{1,0:T(8,128)(2,1)} %bitcast.92, bf16[32,1024]{1,0:T(8,128)(2,1)S(1)} %get-tuple-element.360), kind=kOutput, calls=%fused_computation.13.clone.1 | convolution fusion | flops 310345728 | bytes 475136 | tf_op jit(solution)/shard_map/while/body/eval_jaxpr/dot_general | solution.py:22
  132.1 7.6 %multiply_reduce_fusion.2 = f32[32,1024]{1,0:T(8,128)S(1)} fusion(f32[32,128]{1,0:T(8,128)S(1)} %fusion.107, bf16[4096,32]{1,0:T(8,128)(2,1)} %bitcast.92, bf16[32,1024]{1,0:T(8,128)(2,1)S(1)} %get-tuple-element.360), kind=kOutput, calls=%fused_computation.13.clone.1 | convolution fusion | flops 310345728 | bytes 475136 | tf_op jit(solution)/shard_map/while/body/eval_jaxpr/dot_general | solution.py:22
  142.8 7.6 %multiply_reduce_fusion.2 = f32[32,1024]{1,0:T(8,128)S(1)} fusion(f32[32,128]{1,0:T(8,128)S(1)} %fusion.107, bf16[4096,32]{1,0:T(8,128)(2,1)} %bitcast.92, bf16[32,1024]{1,0:T(8,128)(2,1)S(1)} %get-tuple-element.360), kind=kOutput, calls=%fused_computation.13.clone.1 | convolution fusion | flops 310345728 | bytes 475136 | tf_op jit(solution)/shard_map/while/body/eval_jaxpr/dot_general | solution.py:22
  153.5 7.6 %multiply_reduce_fusion.2 = f32[32,1024]{1,0:T(8,128)S(1)} fusion(f32[32,128]{1,0:T(8,128)S(1)} %fusion.107, bf16[4096,32]{1,0:T(8,128)(2,1)} %bitcast.92, bf16[32,1024]{1,0:T(8,128)(2,1)S(1)} %get-tuple-element.360), kind=kOutput, calls=%fused_computation.13.clone.1 | convolution fusion | flops 310345728 | bytes 475136 | tf_op jit(solution)/shard_map/while/body/eval_jaxpr/dot_general | solution.py:22
  164.2 7.6 %multiply_reduce_fusion.2 = f32[32,1024]{1,0:T(8,128)S(1)} fusion(f32[32,128]{1,0:T(8,128)S(1)} %fusion.107, bf16[4096,32]{1,0:T(8,128)(2,1)} %bitcast.92, bf16[32,1024]{1,0:T(8,128)(2,1)S(1)} %get-tuple-element.360), kind=kOutput, calls=%fused_computation.13.clone.1 | convolution fusion | flops 310345728 | bytes 475136 | tf_op jit(solution)/shard_map/while/body/eval_jaxpr/dot_general | solution.py:22
  174.9 7.6 %multiply_reduce_fusion.2 = f32[32,1024]{1,0:T(8,128)S(1)} fusion(f32[32,128]{1,0:T(8,128)S(1)} %fusion.107, bf16[4096,32]{1,0:T(8,128)(2,1)} %bitcast.92, bf16[32,1024]{1,0:T(8,128)(2,1)S(1)} %get-tuple-element.360), kind=kOutput, calls=%fused_computation.13.clone.1 | convolution fusion | flops 310345728 | bytes 475136 | tf_op jit(solution)/shard_map/while/body/eval_jaxpr/dot_general | solution.py:22
  186.7 7.1 %reshape.192 = bf16[8,512,4,64]{3,2,1,0:T(4,128)(2,1)} reshape(bf16[4096,256]{1,0:T(8,128)(2,1)} %all-gather.3.cloned.1.call-done) | data formatting | bytes 4194304 | tf_op jit(solution)/shard_map/reshape | solution.py:97
  193.8 7.0 %copy.33 = bf16[8,512,4,64]{1,3,2,0:T(8,128)(2,1)} copy(bf16[8,512,4,64]{3,2,1,0:T(4,128)(2,1)} %reshape.192) | data formatting | bytes 4194304
  200.7 7.1 %reshape.193 = bf16[8,512,4,64]{3,2,1,0:T(4,128)(2,1)} reshape(bf16[4096,256]{1,0:T(8,128)(2,1)} %all-gather.5.cloned.1.call-done) | data formatting | bytes 4194304 | tf_op jit(solution)/shard_map/reshape | solution.py:98
  207.8 7.0 %copy.34 = bf16[8,512,4,64]{1,3,2,0:T(8,128)(2,1)} copy(bf16[8,512,4,64]{3,2,1,0:T(4,128)(2,1)} %reshape.193) | data formatting | bytes 4194304
  214.8 140.9 %while.26 = (s32[]{:T(128)}, f32[4,4,256]{2,1,0:T(4,128)S(1)}, f32[4,4,256]{2,1,0:T(4,128)S(1)}, f32[4,4,256,64]{2,3,1,0:T(8,128)}, bf16[8,512,4,64]{1,3,2,0:T(8...) while((s32[]{:T(128)}, f32[4,4,256]{2,1,0:T(4,128)S(1)}, ...), condition=%wide.region_4.5_spmd.clone, body=%wide.region_1.0_spmd.clone.sunk | while | flops 567694080 | bytes 64232944 | solution.py:125
  233.6 5.7 %fusion.113 = (f32[4,4,256]{2,1,0:T(4,128)S(1)}, f32[4,512,256,4]{2,1,3,0:T(8,128)}) fusion(f32[256,512]{0,1:T(8,128)S(1)} %fusion.112, f32[4,4]{1,0:T(4,128)S(1)} %mul.398, bf16[256,4,4,64]{0,3,2,1:T(8,128)(2,1)S(1)} %get-tuple-element.338, bf16[8,512,4,64]{1,3,2,0:T(8,128)(2,1)} %get-tuple-element.337, s32[]{:T(128)} %get-tuple-element.321), kind=kOutput, calls=%fused_computation.27.clone.1 | convolution fusion | flops 276819968 | bytes 9716288 | tf_op jit(solution)/shard_map/while/body/eval_jaxpr/qkgd,skd->kgqs/dot_general | solution.py:105
  251.3 5.7 %fusion.113 = (f32[4,4,256]{2,1,0:T(4,128)S(1)}, f32[4,512,256,4]{2,1,3,0:T(8,128)}) fusion(f32[256,512]{0,1:T(8,128)S(1)} %fusion.112, f32[4,4]{1,0:T(4,128)S(1)} %mul.398, bf16[256,4,4,64]{0,3,2,1:T(8,128)(2,1)S(1)} %get-tuple-element.338, bf16[8,512,4,64]{1,3,2,0:T(8,128)(2,1)} %get-tuple-element.337, s32[]{:T(128)} %get-tuple-element.321), kind=kOutput, calls=%fused_computation.27.clone.1 | convolution fusion | flops 276819968 | bytes 9716288 | tf_op jit(solution)/shard_map/while/body/eval_jaxpr/qkgd,skd->kgqs/dot_general | solution.py:105
  268.9 5.7 %fusion.113 = (f32[4,4,256]{2,1,0:T(4,128)S(1)}, f32[4,512,256,4]{2,1,3,0:T(8,128)}) fusion(f32[256,512]{0,1:T(8,128)S(1)} %fusion.112, f32[4,4]{1,0:T(4,128)S(1)} %mul.398, bf16[256,4,4,64]{0,3,2,1:T(8,128)(2,1)S(1)} %get-tuple-element.338, bf16[8,512,4,64]{1,3,2,0:T(8,128)(2,1)} %get-tuple-element.337, s32[]{:T(128)} %get-tuple-element.321), kind=kOutput, calls=%fused_computation.27.clone.1 | convolution fusion | flops 276819968 | bytes 9716288 | tf_op jit(solution)/shard_map/while/body/eval_jaxpr/qkgd,skd->kgqs/dot_general | solution.py:105
  286.6 5.7 %fusion.113 = (f32[4,4,256]{2,1,0:T(4,128)S(1)}, f32[4,512,256,4]{2,1,3,0:T(8,128)}) fusion(f32[256,512]{0,1:T(8,128)S(1)} %fusion.112, f32[4,4]{1,0:T(4,128)S(1)} %mul.398, bf16[256,4,4,64]{0,3,2,1:T(8,128)(2,1)S(1)} %get-tuple-element.338, bf16[8,512,4,64]{1,3,2,0:T(8,128)(2,1)} %get-tuple-element.337, s32[]{:T(128)} %get-tuple-element.321), kind=kOutput, calls=%fused_computation.27.clone.1 | convolution fusion | flops 276819968 | bytes 9716288 | tf_op jit(solution)/shard_map/while/body/eval_jaxpr/qkgd,skd->kgqs/dot_general | solution.py:105
  364.2 11.7 %fusion.47 = bf16[256,1024]{1,0:T(8,128)(2,1)} fusion(bf16[4096,1024]{1,0:T(8,128)(2,1)} %param.35, bf16[256,1024]{1,0:T(8,128)(2,1)} %copy-done.2, bf16[1024,4096]{1,0:T(8,128)(2,1)} %param.34, f32[1024]{0:T(1024)S(1)} %copy-done.8, f32[256]{0:T(256)S(1)} %add_rsqrt_fusion), kind=kOutput, calls=%fused_computation.67 | convolution fusion | flops 4306239488 | bytes 17830912 | tf_op jit(solution)/shard_map/dot_general | solution.py:176
  (196 shorter events, 174.9 us)
Async XLA Ops:
  6.5 61.7 %copy-start = (bf16[1024,1024]{1,0:T(8,128)(2,1)S(1)}, bf16[1024,1024]{1,0:T(8,128)(2,1)}, u32[]{:S(2)}) copy-start(bf16[1024,1024]{1,0:T(8,128)(2,1)} %param.22) | copy-start | bytes 6291460
  6.5 180.2 %all-gather.3.cloned.1.call-start = ((), (), s32[]{:S(2)}) async-start(), calls=%async_computation.3 | async-start | bytes 2228224 | tf_op jit(solution)/shard_map/all_gather | solution.py:92
  14.5 20.6 %all-to-all-start.2 = ((s32[128,2,1]{1,2,0:T(1,128)}), s32[128,2,1]{1,2,0:T(1,128)S(1)}, u32[]{:S(2)}, u32[]{:S(2)}) async-start(s32[128,2,1]{1,2,0:T(1,128)} %bitcast.12), calls=%async_computation.2 | async-start | bytes 131072 | tf_op jit(solution)/shard_map/all_to_all | solution.py:69
  35.1 21.6 %all-to-all-start = ((s32[128,2,1]{1,2,0:T(1,128)}), s32[128,2,1]{1,2,0:T(1,128)S(1)}, u32[]{:S(2)}, u32[]{:S(2)}) async-start(s32[128,2,1]{1,2,0:T(1,128)} %bitcast.10), calls=%async_computation | async-start | bytes 131072 | tf_op jit(solution)/shard_map/all_to_all | solution.py:68
  41.2 25.9 %copy-start.3 = (bf16[256,1024]{1,0:T(8,128)(2,1)S(1)}, bf16[256,1024]{1,0:T(8,128)(2,1)}, u32[]{:S(2)}) copy-start(bf16[256,1024]{1,0:T(8,128)(2,1)} %param.20) | copy-start | bytes 1572868
  41.2 25.9 %copy-start.5 = (bf16[1024,256]{1,0:T(8,128)(2,1)S(1)}, bf16[1024,256]{1,0:T(8,128)(2,1)}, u32[]{:S(2)}) copy-start(bf16[1024,256]{1,0:T(8,128)(2,1)} %param.24) | copy-start | bytes 1572868
  41.2 26.0 %copy-start.7 = (f32[1024]{0:T(1024)S(1)}, f32[1024]{0:T(1024)}, u32[]{:S(2)}) copy-start(f32[1024]{0:T(1024)} %param.21) | copy-start | bytes 12292
  56.6 40.8 %copy-start.6 = (bf16[32,1024]{1,0:T(8,128)(2,1)S(1)}, bf16[32,1024]{1,0:T(8,128)(2,1)}, u32[]{:S(2)}) copy-start(bf16[32,1024]{1,0:T(8,128)(2,1)} %param.31) | copy-start | bytes 196612
  56.6 40.8 %all-to-all-start.1 = ((bf16[256,128,32]{1,2,0:T(8,128)(2,1)}), bf16[256,128,32]{1,2,0:T(8,128)(2,1)}, u32[]{:S(2)}, u32[]{:S(2)}) async-start(bf16[256,128,32]{1,2,0:T(8,128)(2,1)} %scatter_fusion), calls=%async_computation.1 | async-start | bytes 4194304 | tf_op jit(solution)/shard_map/all_to_all | solution.py:67
  66.9 133.8 %all-gather.5.cloned.1.call-start = ((), (), s32[]{:S(2)}) async-start(), calls=%async_computation.4 | async-start | bytes 2228224 | tf_op jit(solution)/shard_map/all_gather | solution.py:93
  193.8 21.0 %copy-start.4 = (f32[16]{0:T(128)S(1)}, f32[16]{0:T(128)}, u32[]{:S(2)}) copy-start(f32[16]{0:T(128)} %param.26) | copy-start | bytes 196
  222.0 5.8 %copy-start.1 = (f32[4,512,256,4]{2,1,3,0:T(8,128)S(1)}, f32[4,512,256,4]{2,1,3,0:T(8,128)}, u32[]{:S(2)}) copy-start(f32[4,512,256,4]{2,1,3,0:T(8,128)} %get-tuple-element.306) | copy-start | bytes 25165828 | tf_op jit(solution)/shard_map/while
  239.3 5.8 %copy-start.1 = (f32[4,512,256,4]{2,1,3,0:T(8,128)S(1)}, f32[4,512,256,4]{2,1,3,0:T(8,128)}, u32[]{:S(2)}) copy-start(f32[4,512,256,4]{2,1,3,0:T(8,128)} %get-tuple-element.306) | copy-start | bytes 25165828 | tf_op jit(solution)/shard_map/while
  257.0 5.8 %copy-start.1 = (f32[4,512,256,4]{2,1,3,0:T(8,128)S(1)}, f32[4,512,256,4]{2,1,3,0:T(8,128)}, u32[]{:S(2)}) copy-start(f32[4,512,256,4]{2,1,3,0:T(8,128)} %get-tuple-element.306) | copy-start | bytes 25165828 | tf_op jit(solution)/shard_map/while
  274.7 5.8 %copy-start.1 = (f32[4,512,256,4]{2,1,3,0:T(8,128)S(1)}, f32[4,512,256,4]{2,1,3,0:T(8,128)}, u32[]{:S(2)}) copy-start(f32[4,512,256,4]{2,1,3,0:T(8,128)} %get-tuple-element.306) | copy-start | bytes 25165828 | tf_op jit(solution)/shard_map/while
  292.3 5.8 %copy-start.1 = (f32[4,512,256,4]{2,1,3,0:T(8,128)S(1)}, f32[4,512,256,4]{2,1,3,0:T(8,128)}, u32[]{:S(2)}) copy-start(f32[4,512,256,4]{2,1,3,0:T(8,128)} %get-tuple-element.306) | copy-start | bytes 25165828 | tf_op jit(solution)/shard_map/while
  310.0 5.8 %copy-start.1 = (f32[4,512,256,4]{2,1,3,0:T(8,128)S(1)}, f32[4,512,256,4]{2,1,3,0:T(8,128)}, u32[]{:S(2)}) copy-start(f32[4,512,256,4]{2,1,3,0:T(8,128)} %get-tuple-element.306) | copy-start | bytes 25165828 | tf_op jit(solution)/shard_map/while
  327.6 5.8 %copy-start.1 = (f32[4,512,256,4]{2,1,3,0:T(8,128)S(1)}, f32[4,512,256,4]{2,1,3,0:T(8,128)}, u32[]{:S(2)}) copy-start(f32[4,512,256,4]{2,1,3,0:T(8,128)} %get-tuple-element.306) | copy-start | bytes 25165828 | tf_op jit(solution)/shard_map/while
  345.3 5.8 %copy-start.1 = (f32[4,512,256,4]{2,1,3,0:T(8,128)S(1)}, f32[4,512,256,4]{2,1,3,0:T(8,128)}, u32[]{:S(2)}) copy-start(f32[4,512,256,4]{2,1,3,0:T(8,128)} %get-tuple-element.306) | copy-start | bytes 25165828 | tf_op jit(solution)/shard_map/while
  359.4 4.8 %copy-start.8 = (f32[1024]{0:T(1024)S(1)}, f32[1024]{0:T(1024)}, u32[]{:S(2)}) copy-start(f32[1024]{0:T(1024)} %param.33) | copy-start | bytes 12292
  363.3 0.8 copy-start.2
Sparse Core Ops, SparseCore 0:
  10.3 37.0 all-gather.2
  69.5 45.1 all-gather.4
where the time goes:
time: 385 us; the launch traced here: 383 us
  matrix products  164 us (43%)
  local copies, waits for them, and re-layouts  83.4 us (22%)
  other arithmetic  61.2 us (16%)
  waiting for transfers between devices  33.6 us (9%)
  starting transfers between devices  26.2 us (7%)
  between operations  13.6 us (4%)
    dot_general x8, matrix products, one_block(): jnp.dot(value_block.reshape(block_rows * tile_rows, feature_count), w_obs...  60.8 us
    dot_general x8, matrix products, inner_step(): jnp.einsum('qkgd,skd->kgqs', grouped, key_block, preferred_element_type=j...  45.7 us
    reduce_sum x8, other arithmetic, inner_step(): weight_sum = weight_sum * shrink + jnp.sum(weights, axis=-1)  37.2 us
    dot_general x8, matrix products, inner_step(): jnp.einsum('kgqs,skd->kgqd', weights.astype(jnp.bfloat16), value_block, p...  36.2 us
    all_to_all x1, waiting for transfers between devices, observation_update(): lax.all_to_all(packed, ('lat', 'lon'), split_axis=0, concat_axis=0, tiled...  26 us
    dynamic_slice x16, local copies, waits for them, and re-layouts, pool_tiles(): lax.map(one_block, (obs_tiles.reshape(tile_total // block_rows, block_row...  18.5 us
    scatter x1, local copies, waits for them, and re-layouts, observation_update(): jnp.zeros((slot_count,) + obs_values.shape[1:], jnp.bfloat16).at[slot_index]  15.4 us
    unnamed x18, local copies, waits for them, and re-layouts  14.7 us
  transfers between devices with their start and end apart: 5, of which 2 were waited for; matrix products, arithmetic and copies ran while one was open for 34% of the time, Pallas kernels for 0%

commit v1 on v0

v1 whole, which is shorter than its diff:
```python
import functools
import math

import jax
import jax.numpy as jnp
from jax import lax
from jax.experimental import pallas as pl
from jax.experimental.pallas import tpu as pltpu
from jax.sharding import PartitionSpec as P

BF = jnp.bfloat16
F32 = jnp.float32
I32 = jnp.int32

D = 1024
HEADS = 16
HD = 64
KVH = 4
FF = 4096
ROWS = 256
TILES = 128
TROWS = 128
F_OBS = 32
LON = 16
BAND = ROWS * LON
SLOTS = 256
PAY = D + 128
LOG2E = 1.4426950408889634
VT = HD + 16
MIB = 2**20
VMEM = pl.BlockSpec(memory_space=pltpu.VMEM)
SMEM = pl.BlockSpec(memory_space=pltpu.SMEM)
ANY = pl.BlockSpec(memory_space=pl.ANY)


def iota(shape, dim):
    return lax.broadcasted_iota(I32, shape, dim)


def params(mib):
    return pltpu.CompilerParams(vmem_limit_bytes=mib * MIB)


def cost(micros):
    return pl.CostEstimate(
        flops=int(micros * 1.0e9), bytes_accessed=int(micros * 1.0e6), transcendentals=0
    )


def dot(a, b):
    return jnp.dot(a, b, preferred_element_type=F32)


def normed_rows(rows, gain):
    mean_square = jnp.mean(rows * rows, axis=-1, keepdims=True)
    return (rows * lax.rsqrt(mean_square + 1e-05) * gain).astype(BF)


def twice_gelu(x):
    k0 = math.sqrt(2.0 / math.pi)
    k1 = k0 * 0.044715
    inner = x * (x * x * k1 + k0)
    return jnp.tanh(inner) * x + x


def kv_kernel(tok_ref, gain_ref, wk_ref, wv_ref, normed_ref, kv_ref):
    normed = normed_rows(tok_ref[...].astype(F32), gain_ref[...])
    normed_ref[...] = normed
    kv_ref[0:ROWS, :] = dot(normed, wk_ref[...]).astype(BF)
    kv_ref[ROWS : 2 * ROWS, :] = dot(normed, wv_ref[...]).T.astype(BF)


def kv_call(tokens, gain, w_key, w_value):
    return pl.pallas_call(
        kv_kernel,
        out_shape=(
            jax.ShapeDtypeStruct((ROWS, D), BF),
            jax.ShapeDtypeStruct((2 * ROWS, KVH * HD), BF),
        ),
        in_specs=[VMEM] * 4,
        out_specs=(VMEM, VMEM),
        compiler_params=params(16),
        cost_estimate=cost(3),
        name="norm_keys_values",
    )(tokens, gain.reshape(1, D), w_key, w_value)


def pool_kernel(cnt_s, obs_ref, cnt_ref, own_ref, cell_ref, w_ref, pay_ref, live_ref, acc_ref):
    def put(tile, first):
        live_ref[pl.ds(pl.multiple_of(first, 16), TROWS), :] = obs_ref[tile]
        return first + ((cnt_s[tile] + 15) // 16) * 16

    total = lax.fori_loop(0, TILES, put, jnp.int32(0))
    live_ref[pl.ds(pl.multiple_of(total, 16), ROWS), :] = jnp.zeros((ROWS, F_OBS), BF)

    square = (TILES, TILES)
    cnt = jnp.broadcast_to(cnt_ref[...].astype(F32), square).T
    groups = jnp.floor((cnt + 15.0) * (1.0 / 16.0))
    earlier = (iota(square, 1) < iota(square, 0)).astype(F32)
    start = dot(earlier.astype(BF), groups.astype(BF)) * 16.0
    start = jnp.concatenate([start, start], axis=1).astype(I32)
    live = jnp.concatenate([cnt, cnt], axis=1).astype(I32)

    acc_ref[...] = jnp.zeros_like(acc_ref)

    @pl.loop(0, (total + ROWS - 1) // ROWS)
    def _(block):
        first = pl.multiple_of(block * ROWS, ROWS)
        rows = live_ref[pl.ds(first, ROWS), :]
        place = iota((TILES, ROWS), 1) + first - start
        member = ((place >= 0) & (place < live)).astype(F32).astype(BF)
        for c in range(0, D, 256):
            x = dot(rows, w_ref[:, c : c + 256]).astype(BF)
            acc_ref[:, c : c + 256] += dot(member, twice_gelu(x))

    pooled = acc_ref[...] * (0.5 / cnt[:, 0:1])
    own = jnp.broadcast_to(own_ref[...].astype(F32), square)
    own_t = own.T
    rank = jnp.sum(
        jnp.where((own == own_t) & (iota(square, 0) < iota(square, 1)), 1.0, 0.0),
        axis=0,
        keepdims=True,
    )
    slot = (2.0 * own_t[0:1, :] + rank).astype(I32)
    place = (iota((SLOTS, TILES), 0) == slot).astype(F32).astype(BF)
    cell = jnp.broadcast_to(cell_ref[...].astype(F32), square).T + 1.0
    pay_ref[:, 0:D] = dot(place, pooled.astype(BF)).astype(BF)
    pay_ref[:, D:PAY] = dot(place, cell.astype(BF)).astype(BF)


def pool_call(obs_values, tile_owner, tile_cell, tile_count, w_obs_in):
    return pl.pallas_call(
        pool_kernel,
        out_shape=jax.ShapeDtypeStruct((SLOTS, PAY), BF),
        in_specs=[SMEM] + [VMEM] * 5,
        out_specs=VMEM,
        scratch_shapes=[
            pltpu.VMEM((TILES * TROWS + ROWS, F_OBS), BF),
            pltpu.VMEM((TILES, D), F32),
        ],
        compiler_params=params(32),
        cost_estimate=cost(12),
        name="pool_tiles",
    )(
        tile_count,
        obs_values,
        tile_count.reshape(1, TILES),
        tile_owner,
        tile_cell.reshape(1, TILES),
        w_obs_in,
    )


def three(x):
    hi = x.astype(BF)
    rest = x - hi.astype(F32)
    mid = rest.astype(BF)
    lo = (rest - mid.astype(F32)).astype(BF)
    return [hi.astype(F32), mid.astype(F32), lo.astype(F32)]


def stacked(rows, count):
    place = iota((count, ROWS), 0)
    out = jnp.zeros((count, ROWS), F32)
    for i, row in enumerate(rows):
        out = jnp.where(place == i, jnp.broadcast_to(row, out.shape), out)
    return out


def value_rows(kv_ref, group):
    first = ROWS + group * HD
    return jnp.concatenate([kv_ref[first : first + HD, :], jnp.ones((VT - HD, ROWS), BF)], axis=0)


def first_kernel(rate_s, normed_ref, wq_ref, kv_ref, q_ref, out_ref, dist_ref):
    q = (dot(normed_ref[...], wq_ref[...]) * (0.125 * LOG2E)).T
    dist_ref[...] = jnp.abs(iota((ROWS, ROWS), 0) - iota((ROWS, ROWS), 1)).astype(F32)
    lane = iota((ROWS, 128), 1)
    at = iota((1, ROWS), 1).astype(F32)
    for group in range(KVH):
        even = group % 2 == 0
        pair = kv_ref[0:ROWS, (group // 2) * 128 : (group // 2) * 128 + 128]
        keys = jnp.where((lane < HD) == even, pair, jnp.zeros_like(pair))
        values = value_rows(kv_ref, group)
        for head in range(4 * group, 4 * group + 4):
            rate = rate_s[head] * LOG2E
            own = q[head * HD : head * HD + HD, :].astype(BF)
            blank = jnp.zeros((HD, ROWS), BF)
            scores = dot(keys, jnp.concatenate([own, blank] if even else [blank, own], axis=0))
            scores = scores - rate * dist_ref[...]
            top = jnp.max(scores, axis=0, keepdims=True)
            out_ref[head] = dot(values, jnp.exp2(scores - top).astype(BF))
            rates = three(jnp.full((1, ROWS), rate, F32))
            extra = stacked(
                rates + rates + three(rate * at - top) + three(-rate * at - top) + three(-top), 16
            ).astype(BF)
            extra = jnp.concatenate([extra, jnp.zeros((HD - 16, ROWS), BF)], axis=0)
            q_ref[head] = jnp.concatenate([own, extra] if even else [extra, own], axis=0)


def first_call(head_rate, normed, w_query, kv):
    return pl.pallas_call(
        first_kernel,
        out_shape=(
            jax.ShapeDtypeStruct((HEADS, 128, ROWS), BF),
            jax.ShapeDtypeStruct((HEADS, VT, ROWS), F32),
        ),
        in_specs=[SMEM] + [VMEM] * 3,
        out_specs=(VMEM, VMEM),
        scratch_shapes=[pltpu.VMEM((ROWS, ROWS), F32)],
        compiler_params=params(24),
        cost_estimate=cost(5),
        name="queries_own_rows",
    )(head_rate, normed, w_query, kv)


def place_lanes(ahead, first):
    lane = iota((ROWS, 128), 1) - first
    row = iota((ROWS, 128), 0)
    plus = jnp.where(ahead < 8, 1, 0)
    minus = jnp.where(ahead > 8, 1, 0)
    blocks = jnp.where(ahead == 8, 0, jnp.where(ahead < 8, ahead, LON - ahead))
    out = jnp.where(lane < 3, row * (minus - plus), -ROWS * blocks)
    out = jnp.where(lane < 6, out, jnp.where(lane < 9, plus, jnp.where(lane < 12, minus, 1 - plus - minus)))
    out = jnp.where((lane >= 0) & (lane < 15), out, 0)
    return out.astype(F32).astype(BF)


def other_kernel(count, half_way, chunk, ahead_s, rate_s, q_ref, part_ref, *rest):
    blocks = rest[:count]
    out_ref, key_ref, value_ref = rest[count:]
    lane = iota((ROWS, 128), 1)
    for b in range(count):
        here = pl.ds(b * ROWS, ROWS)
        extra = (place_lanes(ahead_s[b], HD), place_lanes(ahead_s[b], 0))
        for group in range(KVH):
            odd = group % 2
            pair = blocks[b][0:ROWS, (group // 2) * 128 : (group // 2) * 128 + 128]
            key_ref[group, here, :] = jnp.where((lane < HD) == (odd == 0), pair, extra[odd])
            value_ref[group, :, here] = value_rows(blocks[b], group)
    if half_way is not None:
        gap = LON // 2 * ROWS - jnp.abs(iota((ROWS, ROWS), 0) - iota((ROWS, ROWS), 1))
        gap = gap.astype(F32)

    @pl.loop(0, KVH)
    def _(group):
        for i in range(4):
            head = group * 4 + i
            total = part_ref[head]
            for first in range(0, count, chunk):
                size = min(chunk, count - first)
                here = pl.ds(first * ROWS, size * ROWS)
                scores = dot(key_ref[group, here, :], q_ref[head])
                if half_way is not None and first <= half_way < first + size:
                    at = (half_way - first) * ROWS
                    far = scores[at : at + ROWS] - (rate_s[head] * LOG2E) * gap
                    pieces = [scores[:at], far, scores[at + ROWS :]]
                    scores = jnp.concatenate([x for x in pieces if x.shape[0]], axis=0)
                total = total + dot(value_ref[group, :, here], jnp.exp2(scores).astype(BF))
            out_ref[head] = total


def other_call(ahead, head_rate, q, part, blocks, half_way, chunk, name):
    count = len(blocks)
    return pl.pallas_call(
        functools.partial(other_kernel, count, half_way, chunk),
        out_shape=jax.ShapeDtypeStruct((HEADS, VT, ROWS), F32),
        in_specs=[SMEM] * 2 + [VMEM] * (2 + count),
        out_specs=VMEM,
        scratch_shapes=[
            pltpu.VMEM((KVH, count * ROWS, 128), BF),
            pltpu.VMEM((KVH, VT, count * ROWS), BF),
        ],
        compiler_params=params(40),
        cost_estimate=cost(2 + 1.3 * count),
        name=name,
    )(ahead, head_rate, q, part, *blocks)


def careful(ahead_s, rate_s, q_ref, blocks, kvs_ref, context_ref, top_ref, sum_ref, acc_ref, sem):
    for b, block in enumerate(blocks):
        copy = pltpu.make_async_copy(block, kvs_ref.at[b], sem)
        copy.start()
        copy.wait()
    lane = iota((ROWS, 128), 1)
    for group in range(KVH):

        @pl.loop(0, 4)
        def _(i):
            head = group * 4 + i
            top_ref[...] = jnp.full((1, ROWS), -jnp.inf, F32)
            sum_ref[...] = jnp.zeros((1, ROWS), F32)
            acc_ref[...] = jnp.zeros((HD, ROWS), F32)

            @pl.loop(0, LON)
            def _(b):
                pair = kvs_ref[b, 0:ROWS, (group // 2) * 128 : (group // 2) * 128 + 128]
                keys = jnp.where((lane < HD) == (group % 2 == 0), pair, jnp.zeros_like(pair))
                gap = jnp.abs(
                    ahead_s[b] * ROWS + iota((ROWS, ROWS), 0) - iota((ROWS, ROWS), 1)
                )
                gap = jnp.minimum(gap, BAND - gap).astype(F32)
                scores = dot(keys, q_ref[head]) - (rate_s[head] * LOG2E) * gap
                top = jnp.maximum(top_ref[...], jnp.max(scores, axis=0, keepdims=True))
                shrink = jnp.exp2(top_ref[...] - top)
                weights = jnp.exp2(scores - top)
                first = ROWS + group * HD
                top_ref[...] = top
                sum_ref[...] = sum_ref[...] * shrink + jnp.sum(weights, axis=0, keepdims=True)
                acc_ref[...] = acc_ref[...] * shrink + dot(
                    kvs_ref[b, first : first + HD, :], weights.astype(BF)
                )

            context_ref[pl.ds(pl.multiple_of(head * HD, HD), HD), :] = acc_ref[...] / sum_ref[...]


STEP = 512


def last_kernel(
    ahead_s,
    rate_s,
    tok_ref,
    gain_ref,
    q_ref,
    part_ref,
    pay_ref,
    w_out_hbm,
    w_obs_hbm,
    w_up_hbm,
    w_down_hbm,
    *rest,
):
    blocks = rest[:LON]
    (
        out_ref,
        w_out_ref,
        w_obs_ref,
        w_up_ref,
        w_down_ref,
        context_ref,
        kvs_ref,
        top_ref,
        sum_ref,
        acc_ref,
        sem,
        spare,
    ) = rest[LON:]
    steps = FF // STEP
    copies = [
        pltpu.make_async_copy(w_out_hbm, w_out_ref, sem.at[0]),
        pltpu.make_async_copy(w_obs_hbm, w_obs_ref, sem.at[1]),
    ]
    for s in range(steps):
        here = pl.ds(s * STEP, STEP)
        copies.append(pltpu.make_async_copy(w_up_hbm.at[:, here], w_up_ref.at[s], sem.at[2 + 2 * s]))
        copies.append(
            pltpu.make_async_copy(w_down_hbm.at[here, :], w_down_ref.at[s], sem.at[3 + 2 * s])
        )
    for copy in copies:
        copy.start()

    largest = jnp.zeros((1, ROWS), F32)
    for head in range(HEADS):
        weight_sum = part_ref[head, HD : HD + 1, :]
        largest = jnp.maximum(largest, weight_sum)
        context_ref[head * HD : head * HD + HD, :] = part_ref[head, 0:HD, :] * (1.0 / weight_sum)

    @pl.when(jnp.logical_not(jnp.max(largest) < 2.0**100))
    def _():
        careful(
            ahead_s, rate_s, q_ref, blocks, kvs_ref, context_ref, top_ref, sum_ref, acc_ref, spare
        )

    cell = pay_ref[:, D:PAY].astype(F32).T
    cell = jnp.broadcast_to(cell[0:1, :], (ROWS, SLOTS)).astype(I32)
    place = (iota((ROWS, SLOTS), 0) + 1 == cell).astype(F32).astype(BF)
    pooled = dot(place, pay_ref[:, 0:D]).astype(BF)
    context = context_ref[...].T.astype(BF)
    copies[0].wait()
    mixed = tok_ref[...].astype(F32) + dot(context, w_out_ref[...])
    copies[1].wait()
    mixed = (mixed + dot(pooled, w_obs_ref[...])).astype(BF).astype(F32)
    normed = normed_rows(mixed, gain_ref[...])
    for s in range(steps):
        copies[2 + 2 * s].wait()
        hidden = (0.5 * twice_gelu(dot(normed, w_up_ref[s]))).astype(BF)
        copies[3 + 2 * s].wait()
        mixed = mixed + dot(hidden, w_down_ref[s])
    out_ref[...] = mixed.astype(BF)


def last_call(ahead, head_rate, tokens, gain, q, part, pay, w_out, w_obs_out, w_up, w_down, blocks):
    steps = FF // STEP
    return pl.pallas_call(
        last_kernel,
        out_shape=jax.ShapeDtypeStruct((ROWS, D), BF),
        in_specs=[SMEM] * 2 + [VMEM] * 5 + [ANY] * (4 + LON),
        out_specs=VMEM,
        scratch_shapes=[
            pltpu.VMEM((D, D), BF),
            pltpu.VMEM((D, D), BF),
            pltpu.VMEM((steps, D, STEP), BF),
            pltpu.VMEM((steps, STEP, D), BF),
            pltpu.VMEM((D, ROWS), F32),
            pltpu.VMEM((LON, 2 * ROWS, KVH * HD), BF),
            pltpu.VMEM((1, ROWS), F32),
            pltpu.VMEM((1, ROWS), F32),
            pltpu.VMEM((HD, ROWS), F32),
            pltpu.SemaphoreType.DMA((2 + 2 * steps,)),
            pltpu.SemaphoreType.DMA,
        ],
        compiler_params=params(48),
        cost_estimate=cost(9),
        name="project_update_mlp",
    )(
        ahead,
        head_rate,
        tokens,
        gain.reshape(1, D),
        q,
        part,
        pay,
        w_out,
        w_obs_out,
        w_up,
        w_down,
        *blocks,
    )


def lon_of(x, z, core):
    return x * 8 + (z % 4) * 2 + core


def send(block, flip_x, step_z, flip_core):
    pairs = [
        (lon_of(x, z, core), lon_of(x ^ flip_x, z + step_z, core ^ flip_core))
        for x in range(2)
        for z in range(4)
        for core in range(2)
    ]
    return lax.ppermute(block, "lon", pairs)


def ahead_of(moves):
    me = lax.axis_index("lon")
    x, z, core = me // 8, (me // 2) % 4, me % 2
    sources = [
        lax.rem(x + fx, 2) * 8 + lax.rem(z + 4 - dz, 4) * 2 + lax.rem(core + fc, 2)
        for fx, dz, fc in moves
    ]
    return jnp.stack([lax.rem(s - me + LON, LON) for s in sources]).astype(I32)


def shards(
    tokens,
    attn_gain,
    w_query,
    w_key,
    w_value,
    w_out,
    head_rate,
    obs_values,
    tile_owner,
    tile_cell,
    tile_count,
    w_obs_in,
    w_obs_out,
    mlp_gain,
    w_up,
    w_down,
):
    normed, kv = kv_call(tokens, attn_gain, w_key, w_value)
    up = send(kv, 0, 1, 0)
    down = send(kv, 0, 3, 0)
    across = send(kv, 1, 0, 0)
    far = send(kv, 0, 2, 0)
    sibling = send(kv, 0, 0, 1)
    pay = pool_call(obs_values, tile_owner, tile_cell, tile_count, w_obs_in)
    pay = lax.all_to_all(pay, ("lat", "lon"), split_axis=0, concat_axis=0, tiled=True)
    q, part = first_call(head_rate, normed, w_query, kv)

    near = [across, up, down, far]
    near_moves = [(1, 0, 0), (0, 1, 0), (0, 3, 0), (0, 2, 0)]
    late = [send(across, 0, 1, 0), send(across, 0, 3, 0), send(far, 1, 0, 0)]
    late_moves = [(1, 1, 0), (1, 3, 0), (1, 2, 0)]
    flip = lambda moves: [(x, z, 1) for x, z, _ in moves]
    near_twin = [send(b, 0, 0, 1) for b in near]
    late_twin = [send(b, 0, 0, 1) for b in late]

    stage_one = near + [sibling] + near_twin
    stage_two = late + late_twin
    moves_one = near_moves + [(0, 0, 1)] + flip(near_moves)
    moves_two = late_moves + flip(late_moves)
    part = other_call(
        ahead_of(moves_one), head_rate, q, part, stage_one, 0, 3, "near_rows"
    )
    part = other_call(
        ahead_of(moves_two), head_rate, q, part, stage_two, None, 3, "late_rows"
    )
    return last_call(
        ahead_of([(0, 0, 0)] + moves_one + moves_two),
        head_rate,
        tokens,
        mlp_gain,
        q,
        part,
        pay,
        w_out,
        w_obs_out,
        w_up,
        w_down,
        [kv] + stage_one + stage_two,
    )


def solution(mesh):
    shard = P(("lat", "lon"))
    rows = P(("lat", "lon"), None)
    return jax.shard_map(
        shards,
        mesh=mesh,
        in_specs=(rows,)
        + (P(),) * 6
        + (P(("lat", "lon"), None, None), rows, shard, shard)
        + (P(),) * 5,
        out_specs=rows,
        check_vma=False,
    )
```

time: 385 us -> 253 us (0.66)
  Pallas kernels: 0 us -> 190 us
  matrix products: 164 us -> 0 us
  other arithmetic: 61.2 us -> 0 us
  local copies, waits for them, and re-layouts: 83.4 us -> 23.9 us
  waiting for transfers between devices: 33.6 us -> 5.82 us
  between operations: 13.6 us -> 0.73 us
    pallas_call x0 -> x6, Pallas kernels: none -> 190 us  [the longest x1 123 us: last_call(): pl.pallas_call(last_kernel, out_shape=jax.ShapeDtypeStruct((ROWS, D), BF)...]
    dot_general x30 -> x0, matrix products: 164 us -> none  [the longest x8 60.8 us: one_block(): jnp.dot(value_block.reshape(block_rows * tile_rows, feature_count), w_obs...]
    reduce_sum x11 -> x0, other arithmetic: 39.5 us -> none  [the longest x8 37.2 us: inner_step(): weight_sum = weight_sum * shrink + jnp.sum(weights, axis=-1)]
    all_to_all x3 -> x1, waiting for transfers between devices: 33.6 us -> 0.01 us  [shards(): lax.all_to_all(pay, ('lat', 'lon'), split_axis=0, concat_axis=0, tiled=True)]
    dynamic_slice x24 -> x0, local copies, waits for them, and re-layouts: 23.1 us -> none  [the longest x16 18.5 us: pool_tiles(): lax.map(one_block, (obs_tiles.reshape(tile_total // block_rows, block_row...]
    scatter x3 -> x0, local copies, waits for them, and re-layouts: 17.6 us -> none  [the longest x1 15.4 us: observation_update(): jnp.zeros((slot_count,) + obs_values.shape[1:], jnp.bfloat16).at[slot_index]]
    reshape x3 -> x0, local copies, waits for them, and re-layouts: 14.2 us -> none  [the longest x1 7.07 us: cycle_attention(): piece[0].reshape(piece_rows // sub_rows, sub_rows, kv_heads, head_size)]
    ppermute x0 -> x15, starting transfers between devices: none -> 12 us  [send(): return lax.ppermute(block, 'lon', pairs)]
  transfers between devices with their start and end apart: 5 -> 16, of which waited for: 2 -> 2; matrix products, arithmetic and copies ran while one was open for 34% -> 2% of each run, Pallas kernels for 0% -> 22%
where the time goes in v1:
time: 253 us; the launch traced here: 250 us
  Pallas kernels  190 us (75%)
  starting transfers between devices  29.8 us (12%)
  local copies, waits for them, and re-layouts  23.9 us (9%)
  waiting for transfers between devices  5.82 us (2%)
    pallas_call x1, Pallas kernels, last_call(): pl.pallas_call(last_kernel, out_shape=jax.ShapeDtypeStruct((ROWS, D), BF)...  123 us
    pallas_call x1, Pallas kernels, pool_call(): pl.pallas_call(pool_kernel, out_shape=jax.ShapeDtypeStruct((SLOTS, PAY),...  36.7 us
    pallas_call x2, Pallas kernels, other_call(): pl.pallas_call(functools.partial(other_kernel, count, half_way, chunk), o...  23.5 us
    unnamed x54, local copies, waits for them, and re-layouts  20.6 us
    all_to_all x1, starting transfers between devices, shards(): lax.all_to_all(pay, ('lat', 'lon'), split_axis=0, concat_axis=0, tiled=True)  17.7 us
    ppermute x15, starting transfers between devices, send(): return lax.ppermute(block, 'lon', pairs)  12 us
    ppermute x15, waiting for transfers between devices, send(): return lax.ppermute(block, 'lon', pairs)  5.82 us
    pallas_call x1, Pallas kernels, first_call(): pl.pallas_call(first_kernel, out_shape=(jax.ShapeDtypeStruct((HEADS, 128,...  5.64 us
  transfers between devices with their start and end apart: 16, of which 2 were waited for; matrix products, arithmetic and copies ran while one was open for 2% of the time, Pallas kernels for 22%

profile of v1, /device:TPU:0, one launch (start us, length us, event | category | flops | bytes accessed | tf_op | source)
XLA Modules:
  0.0 250.2 jit_solution(10283980125144466281)
XLA Ops:
  0.0 1.0 copy-done.2
  1.0 1.0 copy-done.3
  2.1 1.0 copy-done.4
  5.2 4.0 %collective-permute-start.3 = (bf16[512,256]{1,0:T(8,128)(2,1)S(1)}, bf16[512,256]{1,0:T(8,128)(2,1)S(1)}, u32[]{:S(2)}, u32[]{:S(2)}) collective-permute-start(bf16[512,256]{1,0:T(8,128)(2,1)S(1)} %get-tuple-element.10.kv_ref.rest_0_), channel_id=1, source_target_pairs={{0,4},{1,5},{2,6},{3,7},{4,0},{5,1},{6,2},{7,3},{8,12},{9,13},{10,... | collective-permute-start | bytes 786440 | tf_op jit(solution)/shard_map/ppermute | solution.py:443
  9.9 1.3 collective-permute-start.1
  11.2 1.5 collective-permute-start
  12.9 4.6 %copy.17.obs_ref = bf16[128,128,32]{2,1,0:T(8,128)(2,1)} copy(bf16[128,128,32]{1,2,0:T(8,128)(2,1)} %param.23) | data formatting | bytes 2097152 | tf_op args[7]
  18.1 2.2 copy-done
  20.3 36.7 %pool_tiles.1 = bf16[256,1152]{1,0:T(8,128)(2,1)S(1)} custom-call(s32[128]{0:T(128)S(1)} %copy-done.15, bf16[128,128,32]{2,1,0:T(8,128)(2,1)S(1)} %copy-done, s32[1,128]{1,0:T(1,128)S(1)} %bitcast.22, s32[128,1]{1,0:T(8,128)S(1)} %copy.18.own_ref, s32[1,128]{1,0:T(1,128)S(1)} %bitcast.23, bf16[32,1024]{1,0:T(8,128)(2,1)S(1)} %copy-done.12), custom_call_target="tpu_custom_call" | custom-call | flops 12000000000 | bytes 12000000 | tf_op jit(solution)/shard_map/pool_tiles/pallas_call | solution.py:132
  57.0 1.0 all_to_all.7
  58.1 17.7 %all-to-all-start = ((bf16[128,2,1152]{2,1,0:T(2,128)(2,1)}), bf16[128,2,1152]{2,1,0:T(2,128)(2,1)}, u32[]{:S(2)}, u32[]{:S(2)}) async-start(bf16[128,2,1152]{2,1,0:T(2,128)(2,1)} %all_to_all.7), calls=%async_computation | async-start | bytes 1179648 | tf_op jit(solution)/shard_map/all_to_all | solution.py:481
  76.4 2.8 %collective-permute-start.10 = (bf16[512,256]{1,0:T(8,128)(2,1)}, bf16[512,256]{1,0:T(8,128)(2,1)}, u32[]{:S(2)}, u32[]{:S(2)}) collective-permute-start(bf16[512,256]{1,0:T(8,128)(2,1)} %collective-permute-done.rest_0_.rest_1_), channel_id=1, source_target_pairs={{0,6},{1,7},{2,0},{3,1},{4,2},{5,3},{6,4},{7,5},{8,14},{9,15},{10,... | collective-permute-start | bytes 786440 | tf_op jit(solution)/shard_map/ppermute | solution.py:443
  79.9 1.0 copy-done.22
  81.0 5.6 %queries_own_rows.1 = (bf16[16,128,256]{2,1,0:T(8,128)(2,1)S(1)}, f32[16,80,256]{2,1,0:T(8,128)S(1)}) custom-call(f32[16]{0:T(128)S(1)} %copy-done.17, bf16[256,1024]{1,0:T(8,128)(2,1)S(1)} %copy-done.22, bf16[1024,1024]{1,0:T(8,128)(2,1)S(1)} %copy-done.1, bf16[512,256]{1,0:T(8,128)(2,1)S(1)} %get-tuple-element.10.kv_ref.rest_0_), custom_call_target="tpu_custom_call" | custom-call | flops 5000000000 | bytes 5000000 | tf_op jit(solution)/shard_map/queries_own_rows/pallas_call | solution.py:202
  87.1 3.1 %collective-permute-done.10.rest_1_.rest_11_ = bf16[512,256]{1,0:T(8,128)(2,1)} collective-permute-done((bf16[512,256]{1,0:T(8,128)(2,1)}, bf16[512,256]{1,0:T(8,128)(2,1)}, u32[]{:S(2)}, u32[]{:S(2)}) %collective-permute-start.10) | collective-permute-done | bytes 262176 | tf_op jit(solution)/shard_map/ppermute | solution.py:443
  90.2 2.7 %collective-permute-done.9.rest_0_.rest_10_ = bf16[512,256]{1,0:T(8,128)(2,1)} collective-permute-done((bf16[512,256]{1,0:T(8,128)(2,1)}, bf16[512,256]{1,0:T(8,128)(2,1)}, u32[]{:S(2)}, u32[]{:S(2)}) %collective-permute-start.9) | collective-permute-done | bytes 262176 | tf_op jit(solution)/shard_map/ppermute | solution.py:443
  92.9 13.2 %near_rows.1.part_ref = f32[16,80,256]{2,1,0:T(8,128)S(1)} custom-call(s32[9]{0:T(128)S(1)} %stack.90.ahead_s, f32[16]{0:T(128)S(1)} %copy-done.17, bf16[16,128,256]{2,1,0:T(8,128)(2,1)S(1)} %get-tuple-element.11.q_ref, f32[16,80,256]{2,1,0:T(8,128)S(1)} %get-tuple-element.12.part_ref, bf16[512,256]{1,0:T(8,128)(2,1)} %collective-permute-done.rest_0_.rest_1_, ...), custom_call_target="tpu_custom_call" | custom-call | flops 13699999744 | bytes 13700000 | tf_op jit(solution)/shard_map/near_rows/pallas_call | solution.py:265
  109.3 1.1 copy-done.23
  110.4 2.0 all_to_all.9.pay_ref
  112.5 1.3 copy-done.20
  113.8 1.3 copy-done.24
  115.1 10.3 %late_rows.1.part_ref = f32[16,80,256]{2,1,0:T(8,128)S(1)} custom-call(s32[6]{0:T(128)S(1)} %stack.89.ahead_s, f32[16]{0:T(128)S(1)} %copy-done.17, bf16[16,128,256]{2,1,0:T(8,128)(2,1)S(1)} %copy-done.20, f32[16,80,256]{2,1,0:T(8,128)S(1)} %copy-done.24, bf16[512,256]{1,0:T(8,128)(2,1)} %collective-permute-done.9.rest_0_.rest_10_, ...), custom_call_target="tpu_custom_call" | custom-call | flops 9799999488 | bytes 9800000 | tf_op jit(solution)/shard_map/late_rows/pallas_call | solution.py:265
  125.4 1.1 copy-done.18
  126.5 123.5 %project_update_mlp.1 = bf16[256,1024]{1,0:T(8,128)(2,1)} custom-call(s32[16]{0:T(128)S(1)} %stack.88.ahead_s, f32[16]{0:T(128)S(1)} %copy-done.17, bf16[256,1024]{1,0:T(8,128)(2,1)S(1)} %copy-done.5, f32[1,1024]{1,0:T(1,128)S(1)} %bitcast.21, bf16[16,128,256]{2,1,0:T(8,128)(2,1)} %copy-done.19, f32[16,80,256]{2,1,0:T(8,128)} %copy-done.18, ...), custom_call_target="tpu_custom_call" | custom-call | flops 8999999488 | bytes 9000000 | tf_op jit(solution)/shard_map/project_update_mlp/pallas_call | solution.py:395
  (73 shorter events, 8.1 us)
Async XLA Ops:
  3.8 8.9 %copy-start.25 = (s32[128,1]{0,1:T(1,128)S(1)}, s32[128,1]{0,1:T(1,128)}, u32[]{:S(2)}) copy-start(s32[128,1]{0,1:T(1,128)} %param.24) | copy-start | bytes 1540
  5.2 12.3 %collective-permute-start.3 = (bf16[512,256]{1,0:T(8,128)(2,1)S(1)}, bf16[512,256]{1,0:T(8,128)(2,1)S(1)}, u32[]{:S(2)}, u32[]{:S(2)}) collective-permute-start(bf16[512,256]{1,0:T(8,128)(2,1)S(1)} %get-tuple-element.10.kv_ref.rest_0_), channel_id=1, source_target_pairs={{0,4},{1,5},{2,6},{3,7},{4,0},{5,1},{6,2},{7,3},{8,12},{9,13},{10,... | collective-permute-start | bytes 786440 | tf_op jit(solution)/shard_map/ppermute | solution.py:443
  9.2 8.8 %collective-permute-start.4 = (bf16[512,256]{1,0:T(8,128)(2,1)S(1)}, bf16[512,256]{1,0:T(8,128)(2,1)S(1)}, u32[]{:S(2)}, u32[]{:S(2)}) collective-permute-start(bf16[512,256]{1,0:T(8,128)(2,1)S(1)} %get-tuple-element.10.kv_ref.rest_0_), channel_id=1, source_target_pairs={{0,1},{1,0},{2,3},{3,2},{4,5},{5,4},{6,7},{7,6},{8,9},{9,8},{10,11... | collective-permute-start | bytes 786440 | tf_op jit(solution)/shard_map/ppermute | solution.py:443
  9.2 70.0 %collective-permute-start.2 = (bf16[512,256]{1,0:T(8,128)(2,1)S(1)}, bf16[512,256]{1,0:T(8,128)(2,1)}, u32[]{:S(2)}, u32[]{:S(2)}) collective-permute-start(bf16[512,256]{1,0:T(8,128)(2,1)S(1)} %get-tuple-element.10.kv_ref.rest_0_), channel_id=1, source_target_pairs={{0,6},{1,7},{2,0},{3,1},{4,2},{5,3},{6,4},{7,5},{8,14},{9,15},{10,... | collective-permute-start | bytes 786440 | tf_op jit(solution)/shard_map/ppermute | solution.py:443
  9.9 69.3 %collective-permute-start.1 = (bf16[512,256]{1,0:T(8,128)(2,1)S(1)}, bf16[512,256]{1,0:T(8,128)(2,1)}, u32[]{:S(2)}, u32[]{:S(2)}) collective-permute-start(bf16[512,256]{1,0:T(8,128)(2,1)S(1)} %get-tuple-element.10.kv_ref.rest_0_), channel_id=1, source_target_pairs={{0,2},{1,3},{2,4},{3,5},{4,6},{5,7},{6,0},{7,1},{8,10},{9,11},{10,... | collective-permute-start | bytes 786440 | tf_op jit(solution)/shard_map/ppermute | solution.py:443
  11.2 65.1 %collective-permute-start = (bf16[512,256]{1,0:T(8,128)(2,1)S(1)}, bf16[512,256]{1,0:T(8,128)(2,1)}, u32[]{:S(2)}, u32[]{:S(2)}) collective-permute-start(bf16[512,256]{1,0:T(8,128)(2,1)S(1)} %get-tuple-element.10.kv_ref.rest_0_), channel_id=1, source_target_pairs={{0,8},{1,9},{2,10},{3,11},{4,12},{5,13},{6,14},{7,15},{8,0},{9,1},... | collective-permute-start | bytes 786440 | tf_op jit(solution)/shard_map/ppermute | solution.py:443
  17.5 61.8 %collective-permute-start.11 = (bf16[512,256]{1,0:T(8,128)(2,1)S(1)}, bf16[512,256]{1,0:T(8,128)(2,1)}, u32[]{:S(2)}, u32[]{:S(2)}) collective-permute-start(bf16[512,256]{1,0:T(8,128)(2,1)S(1)} %collective-permute-done.3.rest_3_.rest_4_), channel_id=1, source_target_pairs={{0,8},{1,9},{2,10},{3,11},{4,12},{5,13},{6,14},{7,15},{8,0},{9,1},... | collective-permute-start | bytes 786440 | tf_op jit(solution)/shard_map/ppermute | solution.py:443
  18.0 61.8 %collective-permute-start.8 = (bf16[512,256]{1,0:T(8,128)(2,1)S(1)}, bf16[512,256]{1,0:T(8,128)(2,1)}, u32[]{:S(2)}, u32[]{:S(2)}) collective-permute-start(bf16[512,256]{1,0:T(8,128)(2,1)S(1)} %collective-permute-done.3.rest_3_.rest_4_), channel_id=1, source_target_pairs={{0,1},{1,0},{2,3},{3,2},{4,5},{5,4},{6,7},{7,6},{8,9},{9,8},{10,11... | collective-permute-start | bytes 786440 | tf_op jit(solution)/shard_map/ppermute | solution.py:443
  57.0 22.9 %copy-start.1 = (bf16[1024,1024]{1,0:T(8,128)(2,1)S(1)}, bf16[1024,1024]{1,0:T(8,128)(2,1)}, u32[]{:S(2)}) copy-start(bf16[1024,1024]{1,0:T(8,128)(2,1)} %wq_ref.1) | copy-start | bytes 6291460
  57.0 22.9 %copy-start.17 = (f32[16]{0:T(128)S(1)}, f32[16]{0:T(128)}, u32[]{:S(2)}) copy-start(f32[16]{0:T(128)} %rate_s.7) | copy-start | bytes 196
  58.1 52.3 %all-to-all-start = ((bf16[128,2,1152]{2,1,0:T(2,128)(2,1)}), bf16[128,2,1152]{2,1,0:T(2,128)(2,1)}, u32[]{:S(2)}, u32[]{:S(2)}) async-start(bf16[128,2,1152]{2,1,0:T(2,128)(2,1)} %all_to_all.7), calls=%async_computation | async-start | bytes 1179648 | tf_op jit(solution)/shard_map/all_to_all | solution.py:481
  76.4 13.8 %collective-permute-start.10 = (bf16[512,256]{1,0:T(8,128)(2,1)}, bf16[512,256]{1,0:T(8,128)(2,1)}, u32[]{:S(2)}, u32[]{:S(2)}) collective-permute-start(bf16[512,256]{1,0:T(8,128)(2,1)} %collective-permute-done.rest_0_.rest_1_), channel_id=1, source_target_pairs={{0,6},{1,7},{2,0},{3,1},{4,2},{5,3},{6,4},{7,5},{8,14},{9,15},{10,... | collective-permute-start | bytes 786440 | tf_op jit(solution)/shard_map/ppermute | solution.py:443
  79.2 13.7 %collective-permute-start.9 = (bf16[512,256]{1,0:T(8,128)(2,1)}, bf16[512,256]{1,0:T(8,128)(2,1)}, u32[]{:S(2)}, u32[]{:S(2)}) collective-permute-start(bf16[512,256]{1,0:T(8,128)(2,1)} %collective-permute-done.rest_0_.rest_1_), channel_id=1, source_target_pairs={{0,2},{1,3},{2,4},{3,5},{4,6},{5,7},{6,0},{7,1},{8,10},{9,11},{10,... | collective-permute-start | bytes 786440 | tf_op jit(solution)/shard_map/ppermute | solution.py:443
  79.2 13.7 %collective-permute-start.5 = (bf16[512,256]{1,0:T(8,128)(2,1)}, bf16[512,256]{1,0:T(8,128)(2,1)S(1)}, u32[]{:S(2)}, u32[]{:S(2)}) collective-permute-start(bf16[512,256]{1,0:T(8,128)(2,1)} %collective-permute-done.rest_0_.rest_1_), channel_id=1, source_target_pairs={{0,1},{1,0},{2,3},{3,2},{4,5},{5,4},{6,7},{7,6},{8,9},{9,8},{10,11... | collective-permute-start | bytes 786440 | tf_op jit(solution)/shard_map/ppermute | solution.py:443
  79.3 7.3 %collective-permute-start.7 = (bf16[512,256]{1,0:T(8,128)(2,1)}, bf16[512,256]{1,0:T(8,128)(2,1)S(1)}, u32[]{:S(2)}, u32[]{:S(2)}) collective-permute-start(bf16[512,256]{1,0:T(8,128)(2,1)} %collective-permute-done.2.rest_2_.rest_3_), channel_id=1, source_target_pairs={{0,1},{1,0},{2,3},{3,2},{4,5},{5,4},{6,7},{7,6},{8,9},{9,8},{10,11... | collective-permute-start | bytes 786440 | tf_op jit(solution)/shard_map/ppermute | solution.py:443
  79.8 13.1 %collective-permute-start.6 = (bf16[512,256]{1,0:T(8,128)(2,1)}, bf16[512,256]{1,0:T(8,128)(2,1)S(1)}, u32[]{:S(2)}, u32[]{:S(2)}) collective-permute-start(bf16[512,256]{1,0:T(8,128)(2,1)} %collective-permute-done.1.rest_1_.rest_2_), channel_id=1, source_target_pairs={{0,1},{1,0},{2,3},{3,2},{4,5},{5,4},{6,7},{7,6},{8,9},{9,8},{10,11... | collective-permute-start | bytes 786440 | tf_op jit(solution)/shard_map/ppermute | solution.py:443
  86.6 25.8 %collective-permute-start.14 = (bf16[512,256]{1,0:T(8,128)(2,1)}, bf16[512,256]{1,0:T(8,128)(2,1)S(1)}, u32[]{:S(2)}, u32[]{:S(2)}) collective-permute-start(bf16[512,256]{1,0:T(8,128)(2,1)} %collective-permute-done.11.rest_2_.rest_12_), channel_id=1, source_target_pairs={{0,1},{1,0},{2,3},{3,2},{4,5},{5,4},{6,7},{7,6},{8,9},{9,8},{10,11... | collective-permute-start | bytes 786440 | tf_op jit(solution)/shard_map/ppermute | solution.py:443
  90.2 22.3 %collective-permute-start.13 = (bf16[512,256]{1,0:T(8,128)(2,1)}, bf16[512,256]{1,0:T(8,128)(2,1)S(1)}, u32[]{:S(2)}, u32[]{:S(2)}) collective-permute-start(bf16[512,256]{1,0:T(8,128)(2,1)} %collective-permute-done.10.rest_1_.rest_11_), channel_id=1, source_target_pairs={{0,1},{1,0},{2,3},{3,2},{4,5},{5,4},{6,7},{7,6},{8,9},{9,8},{10,11... | collective-permute-start | bytes 786440 | tf_op jit(solution)/shard_map/ppermute | solution.py:443
  92.9 19.5 %collective-permute-start.12 = (bf16[512,256]{1,0:T(8,128)(2,1)}, bf16[512,256]{1,0:T(8,128)(2,1)S(1)}, u32[]{:S(2)}, u32[]{:S(2)}) collective-permute-start(bf16[512,256]{1,0:T(8,128)(2,1)} %collective-permute-done.9.rest_0_.rest_10_), channel_id=1, source_target_pairs={{0,1},{1,0},{2,3},{3,2},{4,5},{5,4},{6,7},{7,6},{8,9},{9,8},{10,11... | collective-permute-start | bytes 786440 | tf_op jit(solution)/shard_map/ppermute | solution.py:443
  112.4 14.1 %copy-start.5 = (bf16[256,1024]{1,0:T(8,128)(2,1)S(1)}, bf16[256,1024]{1,0:T(8,128)(2,1)}, u32[]{:S(2)}) copy-start(bf16[256,1024]{1,0:T(8,128)(2,1)} %tok_ref.3) | copy-start | bytes 1572868
  112.4 14.1 %copy-start.7 = (bf16[512,256]{1,0:T(8,128)(2,1)S(1)}, bf16[512,256]{1,0:T(8,128)(2,1)}, u32[]{:S(2)}) copy-start(bf16[512,256]{1,0:T(8,128)(2,1)} %copy-done.6) | copy-start | bytes 786436
  112.4 14.1 %copy-start.9 = (bf16[512,256]{1,0:T(8,128)(2,1)S(1)}, bf16[512,256]{1,0:T(8,128)(2,1)}, u32[]{:S(2)}) copy-start(bf16[512,256]{1,0:T(8,128)(2,1)} %copy-done.8) | copy-start | bytes 786436
  112.4 14.1 %copy-start.11 = (bf16[512,256]{1,0:T(8,128)(2,1)S(1)}, bf16[512,256]{1,0:T(8,128)(2,1)}, u32[]{:S(2)}) copy-start(bf16[512,256]{1,0:T(8,128)(2,1)} %copy-done.10) | copy-start | bytes 786436
  112.4 14.1 %copy-start.14 = (f32[1024]{0:T(1024)S(1)}, f32[1024]{0:T(1024)}, u32[]{:S(2)}) copy-start(f32[1024]{0:T(1024)} %param.29) | copy-start | bytes 12292
  (18 other events, 31.4 us)

commit v2 on v1

--- a/solution.py
+++ b/solution.py
@@ -79,45 +79,75 @@
         ),
         in_specs=[VMEM] * 4,
         out_specs=(VMEM, VMEM),
-        compiler_params=params(16),
+        compiler_params=params(60),
         cost_estimate=cost(3),
         name="norm_keys_values",
     )(tokens, gain.reshape(1, D), w_key, w_value)
 
 
-def pool_kernel(cnt_s, obs_ref, cnt_ref, own_ref, cell_ref, w_ref, pay_ref, live_ref, acc_ref):
-    def put(tile, first):
-        live_ref[pl.ds(pl.multiple_of(first, 16), TROWS), :] = obs_ref[tile]
-        return first + ((cnt_s[tile] + 15) // 16) * 16
-
-    total = lax.fori_loop(0, TILES, put, jnp.int32(0))
-    live_ref[pl.ds(pl.multiple_of(total, 16), ROWS), :] = jnp.zeros((ROWS, F_OBS), BF)
-
+BLOCK = 512
+HALF = BLOCK // 2
+COLS = 512
+
+
+def pool_kernel(
+    cnt_s, obs_ref, cnt_ref, own_ref, cell_ref, w_ref, pay_ref, live_ref, acc_ref, act_ref, member_ref
+):
     square = (TILES, TILES)
+    source = iota(square, 1) // F_OBS
+    row = iota(square, 0)
+
+    def put(step, first):
+        for u in range(2):
+            four = step * 2 + u
+            rows = obs_ref[pl.ds(pl.multiple_of(four * TILES, TILES), TILES), :].T
+            for k in range(4):
+                count = cnt_s[four * 4 + k]
+                live_ref[pl.ds(pl.multiple_of(first, 32), TROWS), :] = jnp.where(
+                    (source == k) & (row < count), rows, jnp.zeros_like(rows)
+                )
+                first = first + ((count + 31) // 32) * 32
+        return first
+
+    total = lax.fori_loop(0, TILES // 8, put, jnp.int32(0))
+    for i in range(0, 2 * BLOCK, 128):
+        live_ref[pl.ds(pl.multiple_of(total + i, 32), 128), :] = jnp.zeros(square, BF)
+
+    weights = jnp.concatenate([w_ref[...]] * 4, axis=0)
     cnt = jnp.broadcast_to(cnt_ref[...].astype(F32), square).T
-    groups = jnp.floor((cnt + 15.0) * (1.0 / 16.0))
+    groups = jnp.floor((cnt + 31.0) * (1.0 / 32.0))
     earlier = (iota(square, 1) < iota(square, 0)).astype(F32)
     start = dot(earlier.astype(BF), groups.astype(BF)) * 16.0
-    start = jnp.concatenate([start, start], axis=1).astype(I32)
-    live = jnp.concatenate([cnt, cnt], axis=1).astype(I32)
+    start = jnp.concatenate([start] * (HALF // 128), axis=1)
+    length = jnp.concatenate([groups * 16.0] * (HALF // 128), axis=1)
 
     acc_ref[...] = jnp.zeros_like(acc_ref)
-
-    @pl.loop(0, (total + ROWS - 1) // ROWS)
-    def _(block):
-        first = pl.multiple_of(block * ROWS, ROWS)
-        rows = live_ref[pl.ds(first, ROWS), :]
-        place = iota((TILES, ROWS), 1) + first - start
-        member = ((place >= 0) & (place < live)).astype(F32).astype(BF)
-        for c in range(0, D, 256):
-            x = dot(rows, w_ref[:, c : c + 256]).astype(BF)
-            acc_ref[:, c : c + 256] += dot(member, twice_gelu(x))
-
-    pooled = acc_ref[...] * (0.5 / cnt[:, 0:1])
-    own = jnp.broadcast_to(own_ref[...].astype(F32), square)
-    own_t = own.T
+    act_ref[...] = jnp.zeros_like(act_ref)
+    member_ref[...] = jnp.zeros_like(member_ref)
+
+    def one_block(block, now):
+        old = 1 - now
+        rows = live_ref[pl.ds(pl.multiple_of(block * BLOCK, BLOCK), BLOCK), :]
+        place = (iota((TILES, HALF), 1) + block * HALF).astype(F32) - start
+        member_ref[now] = ((place >= 0) & (place < length)).astype(F32).astype(BF)
+        for c in range(0, D, COLS):
+            here = slice(c, c + COLS)
+            x = dot(rows, weights[:, here])
+            acc_ref[:, here] += dot(member_ref[old], act_ref[old, :, here])
+            act = twice_gelu(x.astype(BF))
+            act_ref[now, :, here] = jnp.concatenate(
+                [act[i : i + 16] + act[i + 16 : i + 32] for i in range(0, BLOCK, 32)], axis=0
+            )
+
+    @pl.loop(0, (total + 2 * BLOCK - 1) // (2 * BLOCK))
+    def _(pair):
+        one_block(2 * pair, 0)
+        one_block(2 * pair + 1, 1)
+
+    pooled = (acc_ref[...] + dot(member_ref[1], act_ref[1])) * (0.5 / cnt[:, 0:1])
+    own_t = jnp.broadcast_to(own_ref[...].astype(F32), square)
     rank = jnp.sum(
-        jnp.where((own == own_t) & (iota(square, 0) < iota(square, 1)), 1.0, 0.0),
+        jnp.where((own_t.T == own_t) & (iota(square, 0) < iota(square, 1)), 1.0, 0.0),
         axis=0,
         keepdims=True,
     )
@@ -135,17 +165,19 @@
         in_specs=[SMEM] + [VMEM] * 5,
         out_specs=VMEM,
         scratch_shapes=[
-            pltpu.VMEM((TILES * TROWS + ROWS, F_OBS), BF),
+            pltpu.VMEM((TILES * TROWS + 2 * BLOCK, 128), BF),
             pltpu.VMEM((TILES, D), F32),
+            pltpu.VMEM((2, HALF, D), BF),
+            pltpu.VMEM((2, TILES, HALF), BF),
         ],
-        compiler_params=params(32),
-        cost_estimate=cost(12),
+        compiler_params=params(60),
+        cost_estimate=cost(15),
         name="pool_tiles",
     )(
         tile_count,
-        obs_values,
+        jnp.transpose(obs_values, (0, 2, 1)).reshape(TILES * F_OBS, TROWS),
         tile_count.reshape(1, TILES),
-        tile_owner,
+        tile_owner.reshape(1, TILES),
         tile_cell.reshape(1, TILES),
         w_obs_in,
     )
@@ -208,7 +240,7 @@
         in_specs=[SMEM] + [VMEM] * 3,
         out_specs=(VMEM, VMEM),
         scratch_shapes=[pltpu.VMEM((ROWS, ROWS), F32)],
-        compiler_params=params(24),
+        compiler_params=params(60),
         cost_estimate=cost(5),
         name="queries_own_rows",
     )(head_rate, normed, w_query, kv)
@@ -226,62 +258,9 @@
     return out.astype(F32).astype(BF)
 
 
-def other_kernel(count, half_way, chunk, ahead_s, rate_s, q_ref, part_ref, *rest):
-    blocks = rest[:count]
-    out_ref, key_ref, value_ref = rest[count:]
-    lane = iota((ROWS, 128), 1)
-    for b in range(count):
-        here = pl.ds(b * ROWS, ROWS)
-        extra = (place_lanes(ahead_s[b], HD), place_lanes(ahead_s[b], 0))
-        for group in range(KVH):
-            odd = group % 2
-            pair = blocks[b][0:ROWS, (group // 2) * 128 : (group // 2) * 128 + 128]
-            key_ref[group, here, :] = jnp.where((lane < HD) == (odd == 0), pair, extra[odd])
-            value_ref[group, :, here] = value_rows(blocks[b], group)
-    if half_way is not None:
-        gap = LON // 2 * ROWS - jnp.abs(iota((ROWS, ROWS), 0) - iota((ROWS, ROWS), 1))
-        gap = gap.astype(F32)
-
-    @pl.loop(0, KVH)
-    def _(group):
-        for i in range(4):
-            head = group * 4 + i
-            total = part_ref[head]
-            for first in range(0, count, chunk):
-                size = min(chunk, count - first)
-                here = pl.ds(first * ROWS, size * ROWS)
-                scores = dot(key_ref[group, here, :], q_ref[head])
-                if half_way is not None and first <= half_way < first + size:
-                    at = (half_way - first) * ROWS
-                    far = scores[at : at + ROWS] - (rate_s[head] * LOG2E) * gap
-                    pieces = [scores[:at], far, scores[at + ROWS :]]
-                    scores = jnp.concatenate([x for x in pieces if x.shape[0]], axis=0)
-                total = total + dot(value_ref[group, :, here], jnp.exp2(scores).astype(BF))
-            out_ref[head] = total
-
-
-def other_call(ahead, head_rate, q, part, blocks, half_way, chunk, name):
-    count = len(blocks)
-    return pl.pallas_call(
-        functools.partial(other_kernel, count, half_way, chunk),
-        out_shape=jax.ShapeDtypeStruct((HEADS, VT, ROWS), F32),
-        in_specs=[SMEM] * 2 + [VMEM] * (2 + count),
-        out_specs=VMEM,
-        scratch_shapes=[
-            pltpu.VMEM((KVH, count * ROWS, 128), BF),
-            pltpu.VMEM((KVH, VT, count * ROWS), BF),
-        ],
-        compiler_params=params(40),
-        cost_estimate=cost(2 + 1.3 * count),
-        name=name,
-    )(ahead, head_rate, q, part, *blocks)
-
-
-def careful(ahead_s, rate_s, q_ref, blocks, kvs_ref, context_ref, top_ref, sum_ref, acc_ref, sem):
-    for b, block in enumerate(blocks):
-        copy = pltpu.make_async_copy(block, kvs_ref.at[b], sem)
-        copy.start()
-        copy.wait()
+def careful(ahead, rate_s, q_ref, key_ref, value_ref, ahead_ref, context_ref, top_ref, sum_ref, acc_ref):
+    for b in range(LON):
+        ahead_ref[b] = ahead[b]
     lane = iota((ROWS, 128), 1)
     for group in range(KVH):
 
@@ -294,31 +273,31 @@
 
             @pl.loop(0, LON)
             def _(b):
-                pair = kvs_ref[b, 0:ROWS, (group // 2) * 128 : (group // 2) * 128 + 128]
-                keys = jnp.where((lane < HD) == (group % 2 == 0), pair, jnp.zeros_like(pair))
-                gap = jnp.abs(
-                    ahead_s[b] * ROWS + iota((ROWS, ROWS), 0) - iota((ROWS, ROWS), 1)
-                )
+                here = pl.ds(pl.multiple_of(b * ROWS, ROWS), ROWS)
+                keys = key_ref[group, here, :]
+                keys = jnp.where((lane < HD) == (group % 2 == 0), keys, jnp.zeros_like(keys))
+                gap = jnp.abs(ahead_ref[b] * ROWS + iota((ROWS, ROWS), 0) - iota((ROWS, ROWS), 1))
                 gap = jnp.minimum(gap, BAND - gap).astype(F32)
                 scores = dot(keys, q_ref[head]) - (rate_s[head] * LOG2E) * gap
                 top = jnp.maximum(top_ref[...], jnp.max(scores, axis=0, keepdims=True))
                 shrink = jnp.exp2(top_ref[...] - top)
                 weights = jnp.exp2(scores - top)
-                first = ROWS + group * HD
                 top_ref[...] = top
                 sum_ref[...] = sum_ref[...] * shrink + jnp.sum(weights, axis=0, keepdims=True)
                 acc_ref[...] = acc_ref[...] * shrink + dot(
-                    kvs_ref[b, first : first + HD, :], weights.astype(BF)
+                    value_ref[group, 0:HD, here], weights.astype(BF)
                 )
 
             context_ref[pl.ds(pl.multiple_of(head * HD, HD), HD), :] = acc_ref[...] / sum_ref[...]
 
 
-STEP = 512
+STEP = 1024
+STEPS = FF // STEP
+CHUNK = 5
 
 
 def last_kernel(
-    ahead_s,
+    moves,
     rate_s,
     tok_ref,
     gain_ref,
@@ -338,20 +317,21 @@
         w_obs_ref,
         w_up_ref,
         w_down_ref,
+        key_ref,
+        value_ref,
         context_ref,
-        kvs_ref,
+        largest_ref,
+        ahead_ref,
         top_ref,
         sum_ref,
         acc_ref,
         sem,
-        spare,
     ) = rest[LON:]
-    steps = FF // STEP
     copies = [
         pltpu.make_async_copy(w_out_hbm, w_out_ref, sem.at[0]),
         pltpu.make_async_copy(w_obs_hbm, w_obs_ref, sem.at[1]),
     ]
-    for s in range(steps):
+    for s in range(STEPS):
         here = pl.ds(s * STEP, STEP)
         copies.append(pltpu.make_async_copy(w_up_hbm.at[:, here], w_up_ref.at[s], sem.at[2 + 2 * s]))
         copies.append(
@@ -360,16 +340,42 @@
     for copy in copies:
         copy.start()
 
-    largest = jnp.zeros((1, ROWS), F32)
-    for head in range(HEADS):
-        weight_sum = part_ref[head, HD : HD + 1, :]
-        largest = jnp.maximum(largest, weight_sum)
-        context_ref[head * HD : head * HD + HD, :] = part_ref[head, 0:HD, :] * (1.0 / weight_sum)
-
-    @pl.when(jnp.logical_not(jnp.max(largest) < 2.0**100))
+    ahead = ahead_of(moves)
+    lane = iota((ROWS, 128), 1)
+    for b in range(LON):
+        here = pl.ds(b * ROWS, ROWS)
+        extra = (place_lanes(ahead[b], HD), place_lanes(ahead[b], 0))
+        for group in range(KVH):
+            odd = group % 2
+            pair = blocks[b][0:ROWS, (group // 2) * 128 : (group // 2) * 128 + 128]
+            key_ref[group, here, :] = jnp.where((lane < HD) == (odd == 0), pair, extra[odd])
+            value_ref[group, :, here] = value_rows(blocks[b], group)
+    gap = LON // 2 * ROWS - jnp.abs(iota((ROWS, ROWS), 0) - iota((ROWS, ROWS), 1))
+    gap = gap.astype(F32)
+    largest_ref[...] = jnp.zeros((1, ROWS), F32)
+
+    @pl.loop(0, KVH)
+    def _(group):
+        for i in range(4):
+            head = group * 4 + i
+            total = part_ref[head]
+            for first in range(1, LON, CHUNK):
+                here = pl.ds(first * ROWS, CHUNK * ROWS)
+                scores = dot(key_ref[group, here, :], q_ref[head])
+                if first == 1:
+                    far = scores[:ROWS] - (rate_s[head] * LOG2E) * gap
+                    scores = jnp.concatenate([far, scores[ROWS:]], axis=0)
+                total = total + dot(value_ref[group, :, here], jnp.exp2(scores).astype(BF))
+            weight_sum = total[HD : HD + 1]
+            largest_ref[...] = jnp.maximum(largest_ref[...], weight_sum)
+            context_ref[pl.ds(pl.multiple_of(head * HD, HD), HD), :] = total[:HD] * (
+                1.0 / weight_sum
+            )
+
+    @pl.when(jnp.logical_not(jnp.max(largest_ref[...]) < 2.0**100))
     def _():
         careful(
-            ahead_s, rate_s, q_ref, blocks, kvs_ref, context_ref, top_ref, sum_ref, acc_ref, spare
+            ahead, rate_s, q_ref, key_ref, value_ref, ahead_ref, context_ref, top_ref, sum_ref, acc_ref
         )
 
     cell = pay_ref[:, D:PAY].astype(F32).T
@@ -382,7 +388,7 @@
     copies[1].wait()
     mixed = (mixed + dot(pooled, w_obs_ref[...])).astype(BF).astype(F32)
     normed = normed_rows(mixed, gain_ref[...])
-    for s in range(steps):
+    for s in range(STEPS):
         copies[2 + 2 * s].wait()
         hidden = (0.5 * twice_gelu(dot(normed, w_up_ref[s]))).astype(BF)
         copies[3 + 2 * s].wait()
@@ -390,31 +396,31 @@
     out_ref[...] = mixed.astype(BF)
 
 
-def last_call(ahead, head_rate, tokens, gain, q, part, pay, w_out, w_obs_out, w_up, w_down, blocks):
-    steps = FF // STEP
+def last_call(moves, head_rate, tokens, gain, q, part, pay, w_out, w_obs_out, w_up, w_down, blocks):
     return pl.pallas_call(
-        last_kernel,
+        functools.partial(last_kernel, moves),
         out_shape=jax.ShapeDtypeStruct((ROWS, D), BF),
-        in_specs=[SMEM] * 2 + [VMEM] * 5 + [ANY] * (4 + LON),
+        in_specs=[SMEM] + [VMEM] * 5 + [ANY] * 4 + [VMEM] * LON,
         out_specs=VMEM,
         scratch_shapes=[
             pltpu.VMEM((D, D), BF),
             pltpu.VMEM((D, D), BF),
-            pltpu.VMEM((steps, D, STEP), BF),
-            pltpu.VMEM((steps, STEP, D), BF),
+            pltpu.VMEM((STEPS, D, STEP), BF),
+            pltpu.VMEM((STEPS, STEP, D), BF),
+            pltpu.VMEM((KVH, BAND, 128), BF),
+            pltpu.VMEM((KVH, VT, BAND), BF),
             pltpu.VMEM((D, ROWS), F32),
-            pltpu.VMEM((LON, 2 * ROWS, KVH * HD), BF),
+            pltpu.VMEM((1, ROWS), F32),
+            pltpu.SMEM((LON,), I32),
             pltpu.VMEM((1, ROWS), F32),
             pltpu.VMEM((1, ROWS), F32),
             pltpu.VMEM((HD, ROWS), F32),
-            pltpu.SemaphoreType.DMA((2 + 2 * steps,)),
-            pltpu.SemaphoreType.DMA,
+            pltpu.SemaphoreType.DMA((2 + 2 * STEPS,)),
         ],
-        compiler_params=params(48),
-        cost_estimate=cost(9),
-        name="project_update_mlp",
+        compiler_params=params(60),
+        cost_estimate=cost(24),
+        name="other_rows_project_update_mlp",
     )(
-        ahead,
         head_rate,
         tokens,
         gain.reshape(1, D),
@@ -450,7 +456,7 @@
         lax.rem(x + fx, 2) * 8 + lax.rem(z + 4 - dz, 4) * 2 + lax.rem(core + fc, 2)
         for fx, dz, fc in moves
     ]
-    return jnp.stack([lax.rem(s - me + LON, LON) for s in sources]).astype(I32)
+    return [lax.rem(s - me + LON, LON) for s in sources]
 
 
 def shards(
@@ -477,30 +483,25 @@
     across = send(kv, 1, 0, 0)
     far = send(kv, 0, 2, 0)
     sibling = send(kv, 0, 0, 1)
+    q, part = first_call(head_rate, normed, w_query, kv)
+    part, tile_count, up, down, across, far, sibling = lax.optimization_barrier(
+        (part, tile_count, up, down, across, far, sibling)
+    )
+    late = [send(across, 0, 1, 0), send(across, 0, 3, 0), send(far, 1, 0, 0)]
+    near = [across, up, down, far]
+    near_twin = [send(b, 0, 0, 1) for b in near]
     pay = pool_call(obs_values, tile_owner, tile_cell, tile_count, w_obs_in)
+    pay, *late = lax.optimization_barrier((pay, *late, *near_twin))
+    late, near_twin = late[:3], late[3:]
+    late_twin = [send(b, 0, 0, 1) for b in late]
     pay = lax.all_to_all(pay, ("lat", "lon"), split_axis=0, concat_axis=0, tiled=True)
-    q, part = first_call(head_rate, normed, w_query, kv)
-
-    near = [across, up, down, far]
+
     near_moves = [(1, 0, 0), (0, 1, 0), (0, 3, 0), (0, 2, 0)]
-    late = [send(across, 0, 1, 0), send(across, 0, 3, 0), send(far, 1, 0, 0)]
     late_moves = [(1, 1, 0), (1, 3, 0), (1, 2, 0)]
-    flip = lambda moves: [(x, z, 1) for x, z, _ in moves]
-    near_twin = [send(b, 0, 0, 1) for b in near]
-    late_twin = [send(b, 0, 0, 1) for b in late]
-
-    stage_one = near + [sibling] + near_twin
-    stage_two = late + late_twin
-    moves_one = near_moves + [(0, 0, 1)] + flip(near_moves)
-    moves_two = late_moves + flip(late_moves)
-    part = other_call(
-        ahead_of(moves_one), head_rate, q, part, stage_one, 0, 3, "near_rows"
-    )
-    part = other_call(
-        ahead_of(moves_two), head_rate, q, part, stage_two, None, 3, "late_rows"
-    )
+    moves = [(0, 0, 0)] + near_moves + late_moves + [(0, 0, 1)]
+    moves = moves + [(x, z, 1) for x, z, _ in near_moves + late_moves]
     return last_call(
-        ahead_of([(0, 0, 0)] + moves_one + moves_two),
+        moves,
         head_rate,
         tokens,
         mlp_gain,
@@ -511,7 +512,7 @@
         w_obs_out,
         w_up,
         w_down,
-        [kv] + stage_one + stage_two,
+        [kv] + near + late + [sibling] + near_twin + late_twin,
     )
 
 

time: 253 us -> 201 us (0.79)
  Pallas kernels: 190 us -> 155 us
  local copies, waits for them, and re-layouts: 23.9 us -> 4.81 us
  waiting for transfers between devices: 5.82 us -> 15.4 us
  starting transfers between devices: 29.8 us -> 23.9 us
    pallas_call x1, Pallas kernels: 36.7 us -> 15.4 us  [pool_call(): pl.pallas_call(pool_kernel, out_shape=jax.ShapeDtypeStruct((SLOTS, PAY),...]
    unnamed x54 -> x28, local copies, waits for them, and re-layouts: 20.6 us -> 0.85 us
    pallas_call x3 -> x1, Pallas kernels: 147 us -> 129 us  [last_call(): pl.pallas_call(functools.partial(last_kernel, moves), out_shape=jax.Shape...]
    all_to_all x1, waiting for transfers between devices: 0.01 us -> 13.4 us  [shards(): lax.all_to_all(pay, ('lat', 'lon'), split_axis=0, concat_axis=0, tiled=True)]
    all_to_all x1, starting transfers between devices: 17.7 us -> 10.8 us  [shards(): lax.all_to_all(pay, ('lat', 'lon'), split_axis=0, concat_axis=0, tiled=True)]
    ppermute x15, waiting for transfers between devices: 5.82 us -> 1.98 us  [send(): return lax.ppermute(block, 'lon', pairs)]
  transfers between devices with their start and end apart: 16 -> 16, of which waited for: 2 -> 2; matrix products, arithmetic and copies ran while one was open for 2% -> 0% of each run, Pallas kernels for 22% -> 12%
where the time goes in v2:
time: 201 us; the launch traced here: 200 us
  Pallas kernels  155 us (77%)
  starting transfers between devices  23.9 us (12%)
  waiting for transfers between devices  15.4 us (8%)
  local copies, waits for them, and re-layouts  4.81 us (2%)
    pallas_call x1, Pallas kernels, last_call(): pl.pallas_call(functools.partial(last_kernel, moves), out_shape=jax.Shape...  129 us
    pallas_call x1, Pallas kernels, pool_call(): pl.pallas_call(pool_kernel, out_shape=jax.ShapeDtypeStruct((SLOTS, PAY),...  15.4 us
    all_to_all x1, waiting for transfers between devices, shards(): lax.all_to_all(pay, ('lat', 'lon'), split_axis=0, concat_axis=0, tiled=True)  13.4 us
    ppermute x15, starting transfers between devices, send(): return lax.ppermute(block, 'lon', pairs)  13.1 us
    all_to_all x1, starting transfers between devices, shards(): lax.all_to_all(pay, ('lat', 'lon'), split_axis=0, concat_axis=0, tiled=True)  10.8 us
    pallas_call x1, Pallas kernels, first_call(): pl.pallas_call(first_kernel, out_shape=(jax.ShapeDtypeStruct((HEADS, 128,...  8.08 us
  transfers between devices with their start and end apart: 16, of which 2 were waited for; matrix products, arithmetic and copies ran while one was open for 0% of the time, Pallas kernels for 12%

profile of v2, /device:TPU:0, one launch (start us, length us, event | category | flops | bytes accessed | tf_op | source)
XLA Modules:
  0.0 199.8 jit_solution(10522207464313085826)
XLA Ops:
  0.0 2.7 %norm_keys_values.1 = (bf16[256,1024]{1,0:T(8,128)(2,1)}, bf16[512,256]{1,0:T(8,128)(2,1)}) custom-call(bf16[256,1024]{1,0:T(8,128)(2,1)} %tok_ref.3, f32[1,1024]{1,0:T(1,128)} %bitcast.9, bf16[1024,256]{1,0:T(8,128)(2,1)} %wk_ref.1, bf16[1024,256]{1,0:T(8,128)(2,1)} %wv_ref.1), custom_call_target="tpu_custom_call" | custom-call | flops 3000000000 | bytes 3000000 | tf_op jit(solution)/shard_map/norm_keys_values/pallas_call | solution.py:74
  2.7 4.0 %collective-permute-start.3 = (bf16[512,256]{1,0:T(8,128)(2,1)}, bf16[512,256]{1,0:T(8,128)(2,1)S(1)}, u32[]{:S(2)}, u32[]{:S(2)}) collective-permute-start(bf16[512,256]{1,0:T(8,128)(2,1)} %get-tuple-element.25.kv_ref.rest_0_), channel_id=1, source_target_pairs={{0,4},{1,5},{2,6},{3,7},{4,0},{5,1},{6,2},{7,3},{8,12},{9,13},{10,... | collective-permute-start | bytes 786440 | tf_op jit(solution)/shard_map/ppermute | solution.py:449
  6.7 1.5 collective-permute-start.2
  8.2 0.7 collective-permute-start.1
  8.9 1.3 collective-permute-start
  10.2 8.1 %queries_own_rows.1 = (bf16[16,128,256]{2,1,0:T(8,128)(2,1)}, f32[16,80,256]{2,1,0:T(8,128)}) custom-call(f32[16]{0:T(128)} %rate_s.3, bf16[256,1024]{1,0:T(8,128)(2,1)} %get-tuple-element.24.normed_ref, bf16[1024,1024]{1,0:T(8,128)(2,1)} %wq_ref.1, bf16[512,256]{1,0:T(8,128)(2,1)} %get-tuple-element.25.kv_ref.rest_0_), custom_call_target="tpu_custom_call" | custom-call | flops 5000000000 | bytes 5000000 | tf_op jit(solution)/shard_map/queries_own_rows/pallas_call | solution.py:234
  18.3 1.9 collective-permute-done.1.rest_3_
  20.3 0.1 collective-permute-start.9
  20.4 0.5 collective-permute-start.10
  20.9 0.1 collective-permute-start.11
  21.0 1.5 collective-permute-start.7
  22.4 0.2 collective-permute-start.8
  22.6 2.6 %collective-permute-start.6 = (bf16[512,256]{1,0:T(8,128)(2,1)S(1)}, bf16[512,256]{1,0:T(8,128)(2,1)S(1)}, u32[]{:S(2)}, u32[]{:S(2)}) collective-permute-start(bf16[512,256]{1,0:T(8,128)(2,1)S(1)} %collective-permute-done.2.rest_1_), channel_id=1, source_target_pairs={{0,6},{1,7},{2,0},{3,1},{4,2},{5,3},{6,4},{7,5},{8,14},{9,15},{10,... | collective-permute-start | bytes 786440 | tf_op jit(solution)/shard_map/ppermute | solution.py:449
  25.3 15.4 %pool_tiles.1 = bf16[256,1152]{1,0:T(8,128)(2,1)} custom-call(s32[128]{0:T(128)} %cnt_s, bf16[4096,128]{1,0:T(8,128)(2,1)} %bitcast.8, s32[1,128]{1,0:T(1,128)} %bitcast.11, s32[1,128]{1,0:T(1,128)} %bitcast.12, s32[1,128]{1,0:T(1,128)} %bitcast.13, bf16[32,1024]{1,0:T(8,128)(2,1)} %w_ref.1), custom_call_target="tpu_custom_call" | custom-call | flops 15000000512 | bytes 15000000 | tf_op jit(solution)/shard_map/pool_tiles/pallas_call | solution.py:162
  40.8 2.9 %all_to_all.7 = bf16[128,2,1152]{2,1,0:T(2,128)(2,1)} reshape(bf16[256,1152]{1,0:T(8,128)(2,1)} %pool_tiles.1) | data formatting | bytes 1179648 | tf_op jit(solution)/shard_map/all_to_all | solution.py:497
  43.7 10.8 %all-to-all-start = ((bf16[128,2,1152]{2,1,0:T(2,128)(2,1)}), bf16[128,2,1152]{2,1,0:T(2,128)(2,1)S(1)}, u32[]{:S(2)}, u32[]{:S(2)}) async-start(bf16[128,2,1152]{2,1,0:T(2,128)(2,1)} %all_to_all.7), calls=%async_computation | async-start | bytes 1179648 | tf_op jit(solution)/shard_map/all_to_all | solution.py:497
  54.5 0.1 collective-permute-start.12
  54.6 0.5 collective-permute-start.13
  55.1 0.1 collective-permute-start.14
  55.2 13.4 %all-to-all-done = bf16[128,2,1152]{2,1,0:T(2,128)(2,1)S(1)} async-done(((bf16[128,2,1152]{2,1,0:T(2,128)(2,1)}), bf16[128,2,1152]{2,1,0:T(2,128)(2,1)S(1)}, u32[]{:S(2)}, u32[]{:S(2)}) %all-to-all-start) | async-done | bytes 589856 | tf_op jit(solution)/shard_map/all_to_all | solution.py:497
  68.6 1.1 all_to_all.9.pay_ref
  69.7 0.6 copy-done.11
  70.3 0.1 copy-done.12
  70.5 129.1 %other_rows_project_update_mlp.1 = bf16[256,1024]{1,0:T(8,128)(2,1)} custom-call(f32[16]{0:T(128)} %rate_s.3, bf16[256,1024]{1,0:T(8,128)(2,1)} %tok_ref.3, f32[1,1024]{1,0:T(1,128)} %bitcast.10, bf16[16,128,256]{2,1,0:T(8,128)(2,1)} %get-tuple-element.26.q_ref, f32[16,80,256]{2,1,0:T(8,128)} %get-tuple-element.28.part_ref, ...), custom_call_target="tpu_custom_call" | custom-call | flops 24000000000 | bytes 24000000 | tf_op jit(solution)/shard_map/other_rows_project_update_mlp/pallas_call | solution.py:400
  (42 shorter events, 0.2 us)
Async XLA Ops:
  2.7 15.6 %collective-permute-start.4 = (bf16[512,256]{1,0:T(8,128)(2,1)}, bf16[512,256]{1,0:T(8,128)(2,1)S(1)}, u32[]{:S(2)}, u32[]{:S(2)}) collective-permute-start(bf16[512,256]{1,0:T(8,128)(2,1)} %get-tuple-element.25.kv_ref.rest_0_), channel_id=1, source_target_pairs={{0,1},{1,0},{2,3},{3,2},{4,5},{5,4},{6,7},{7,6},{8,9},{9,8},{10,11... | collective-permute-start | bytes 786440 | tf_op jit(solution)/shard_map/ppermute | solution.py:449
  2.7 15.6 %collective-permute-start.3 = (bf16[512,256]{1,0:T(8,128)(2,1)}, bf16[512,256]{1,0:T(8,128)(2,1)S(1)}, u32[]{:S(2)}, u32[]{:S(2)}) collective-permute-start(bf16[512,256]{1,0:T(8,128)(2,1)} %get-tuple-element.25.kv_ref.rest_0_), channel_id=1, source_target_pairs={{0,4},{1,5},{2,6},{3,7},{4,0},{5,1},{6,2},{7,3},{8,12},{9,13},{10,... | collective-permute-start | bytes 786440 | tf_op jit(solution)/shard_map/ppermute | solution.py:449
  6.7 11.6 %collective-permute-start.2 = (bf16[512,256]{1,0:T(8,128)(2,1)}, bf16[512,256]{1,0:T(8,128)(2,1)S(1)}, u32[]{:S(2)}, u32[]{:S(2)}) collective-permute-start(bf16[512,256]{1,0:T(8,128)(2,1)} %get-tuple-element.25.kv_ref.rest_0_), channel_id=1, source_target_pairs={{0,8},{1,9},{2,10},{3,11},{4,12},{5,13},{6,14},{7,15},{8,0},{9,1},... | collective-permute-start | bytes 786440 | tf_op jit(solution)/shard_map/ppermute | solution.py:449
  8.2 12.1 %collective-permute-start.1 = (bf16[512,256]{1,0:T(8,128)(2,1)}, bf16[512,256]{1,0:T(8,128)(2,1)S(1)}, u32[]{:S(2)}, u32[]{:S(2)}) collective-permute-start(bf16[512,256]{1,0:T(8,128)(2,1)} %get-tuple-element.25.kv_ref.rest_0_), channel_id=1, source_target_pairs={{0,6},{1,7},{2,0},{3,1},{4,2},{5,3},{6,4},{7,5},{8,14},{9,15},{10,... | collective-permute-start | bytes 786440 | tf_op jit(solution)/shard_map/ppermute | solution.py:449
  8.9 11.4 %collective-permute-start = (bf16[512,256]{1,0:T(8,128)(2,1)}, bf16[512,256]{1,0:T(8,128)(2,1)S(1)}, u32[]{:S(2)}, u32[]{:S(2)}) collective-permute-start(bf16[512,256]{1,0:T(8,128)(2,1)} %get-tuple-element.25.kv_ref.rest_0_), channel_id=1, source_target_pairs={{0,2},{1,3},{2,4},{3,5},{4,6},{5,7},{6,0},{7,1},{8,10},{9,11},{10,... | collective-permute-start | bytes 786440 | tf_op jit(solution)/shard_map/ppermute | solution.py:449
  18.3 22.3 %copy-start = (bf16[512,256]{1,0:T(8,128)(2,1)}, bf16[512,256]{1,0:T(8,128)(2,1)S(1)}, u32[]{:S(2)}) copy-start(bf16[512,256]{1,0:T(8,128)(2,1)S(1)} %collective-permute-done.4.rest_8_) | copy-start | bytes 786436
  18.3 22.3 %copy-start.1 = (bf16[512,256]{1,0:T(8,128)(2,1)}, bf16[512,256]{1,0:T(8,128)(2,1)S(1)}, u32[]{:S(2)}) copy-start(bf16[512,256]{1,0:T(8,128)(2,1)S(1)} %collective-permute-done.3.rest_4_) | copy-start | bytes 786436
  18.3 22.3 %copy-start.2 = (bf16[512,256]{1,0:T(8,128)(2,1)}, bf16[512,256]{1,0:T(8,128)(2,1)S(1)}, u32[]{:S(2)}) copy-start(bf16[512,256]{1,0:T(8,128)(2,1)S(1)} %collective-permute-done.2.rest_1_) | copy-start | bytes 786436
  20.3 20.4 %copy-start.4 = (bf16[512,256]{1,0:T(8,128)(2,1)}, bf16[512,256]{1,0:T(8,128)(2,1)S(1)}, u32[]{:S(2)}) copy-start(bf16[512,256]{1,0:T(8,128)(2,1)S(1)} %collective-permute-done.rest_2_) | copy-start | bytes 786436
  20.3 2.3 %collective-permute-start.9 = (bf16[512,256]{1,0:T(8,128)(2,1)S(1)}, bf16[512,256]{1,0:T(8,128)(2,1)S(1)}, u32[]{:S(2)}, u32[]{:S(2)}) collective-permute-start(bf16[512,256]{1,0:T(8,128)(2,1)S(1)} %collective-permute-done.rest_2_), channel_id=1, source_target_pairs={{0,1},{1,0},{2,3},{3,2},{4,5},{5,4},{6,7},{7,6},{8,9},{9,8},{10,11... | collective-permute-start | bytes 786440 | tf_op jit(solution)/shard_map/ppermute | solution.py:449
  20.4 4.9 %collective-permute-start.10 = (bf16[512,256]{1,0:T(8,128)(2,1)S(1)}, bf16[512,256]{1,0:T(8,128)(2,1)S(1)}, u32[]{:S(2)}, u32[]{:S(2)}) collective-permute-start(bf16[512,256]{1,0:T(8,128)(2,1)S(1)} %collective-permute-done.1.rest_3_), channel_id=1, source_target_pairs={{0,1},{1,0},{2,3},{3,2},{4,5},{5,4},{6,7},{7,6},{8,9},{9,8},{10,11... | collective-permute-start | bytes 786440 | tf_op jit(solution)/shard_map/ppermute | solution.py:449
  20.9 19.8 %collective-permute-start.11 = (bf16[512,256]{1,0:T(8,128)(2,1)S(1)}, bf16[512,256]{1,0:T(8,128)(2,1)S(1)}, u32[]{:S(2)}, u32[]{:S(2)}) collective-permute-start(bf16[512,256]{1,0:T(8,128)(2,1)S(1)} %collective-permute-done.3.rest_4_), channel_id=1, source_target_pairs={{0,1},{1,0},{2,3},{3,2},{4,5},{5,4},{6,7},{7,6},{8,9},{9,8},{10,11... | collective-permute-start | bytes 786440 | tf_op jit(solution)/shard_map/ppermute | solution.py:449
  21.0 19.7 %collective-permute-start.7 = (bf16[512,256]{1,0:T(8,128)(2,1)S(1)}, bf16[512,256]{1,0:T(8,128)(2,1)S(1)}, u32[]{:S(2)}, u32[]{:S(2)}) collective-permute-start(bf16[512,256]{1,0:T(8,128)(2,1)S(1)} %collective-permute-done.3.rest_4_), channel_id=1, source_target_pairs={{0,8},{1,9},{2,10},{3,11},{4,12},{5,13},{6,14},{7,15},{8,0},{9,1},... | collective-permute-start | bytes 786440 | tf_op jit(solution)/shard_map/ppermute | solution.py:449
  22.4 18.3 %collective-permute-start.8 = (bf16[512,256]{1,0:T(8,128)(2,1)S(1)}, bf16[512,256]{1,0:T(8,128)(2,1)S(1)}, u32[]{:S(2)}, u32[]{:S(2)}) collective-permute-start(bf16[512,256]{1,0:T(8,128)(2,1)S(1)} %collective-permute-done.2.rest_1_), channel_id=1, source_target_pairs={{0,1},{1,0},{2,3},{3,2},{4,5},{5,4},{6,7},{7,6},{8,9},{9,8},{10,11... | collective-permute-start | bytes 786440 | tf_op jit(solution)/shard_map/ppermute | solution.py:449
  22.6 18.1 %collective-permute-start.6 = (bf16[512,256]{1,0:T(8,128)(2,1)S(1)}, bf16[512,256]{1,0:T(8,128)(2,1)S(1)}, u32[]{:S(2)}, u32[]{:S(2)}) collective-permute-start(bf16[512,256]{1,0:T(8,128)(2,1)S(1)} %collective-permute-done.2.rest_1_), channel_id=1, source_target_pairs={{0,6},{1,7},{2,0},{3,1},{4,2},{5,3},{6,4},{7,5},{8,14},{9,15},{10,... | collective-permute-start | bytes 786440 | tf_op jit(solution)/shard_map/ppermute | solution.py:449
  25.3 15.5 %collective-permute-start.5 = (bf16[512,256]{1,0:T(8,128)(2,1)S(1)}, bf16[512,256]{1,0:T(8,128)(2,1)}, u32[]{:S(2)}, u32[]{:S(2)}) collective-permute-start(bf16[512,256]{1,0:T(8,128)(2,1)S(1)} %collective-permute-done.2.rest_1_), channel_id=1, source_target_pairs={{0,2},{1,3},{2,4},{3,5},{4,6},{5,7},{6,0},{7,1},{8,10},{9,11},{10,... | collective-permute-start | bytes 786440 | tf_op jit(solution)/shard_map/ppermute | solution.py:449
  40.7 29.0 %copy-start.7 = (bf16[512,256]{1,0:T(8,128)(2,1)}, bf16[512,256]{1,0:T(8,128)(2,1)S(1)}, u32[]{:S(2)}) copy-start(bf16[512,256]{1,0:T(8,128)(2,1)S(1)} %collective-permute-done.11.rest_12_) | copy-start | bytes 786436
  40.7 29.0 %copy-start.8 = (bf16[512,256]{1,0:T(8,128)(2,1)}, bf16[512,256]{1,0:T(8,128)(2,1)S(1)}, u32[]{:S(2)}) copy-start(bf16[512,256]{1,0:T(8,128)(2,1)S(1)} %collective-permute-done.7.rest_7_) | copy-start | bytes 786436
  40.7 29.0 %copy-start.9 = (bf16[512,256]{1,0:T(8,128)(2,1)}, bf16[512,256]{1,0:T(8,128)(2,1)S(1)}, u32[]{:S(2)}) copy-start(bf16[512,256]{1,0:T(8,128)(2,1)S(1)} %collective-permute-done.8.rest_9_) | copy-start | bytes 786436
  40.8 28.9 %copy-start.10 = (bf16[512,256]{1,0:T(8,128)(2,1)}, bf16[512,256]{1,0:T(8,128)(2,1)S(1)}, u32[]{:S(2)}) copy-start(bf16[512,256]{1,0:T(8,128)(2,1)S(1)} %collective-permute-done.6.rest_6_) | copy-start | bytes 786436
  43.7 24.9 %all-to-all-start = ((bf16[128,2,1152]{2,1,0:T(2,128)(2,1)}), bf16[128,2,1152]{2,1,0:T(2,128)(2,1)S(1)}, u32[]{:S(2)}, u32[]{:S(2)}) async-start(bf16[128,2,1152]{2,1,0:T(2,128)(2,1)} %all_to_all.7), calls=%async_computation | async-start | bytes 1179648 | tf_op jit(solution)/shard_map/all_to_all | solution.py:497
  54.5 15.1 %collective-permute-start.12 = (bf16[512,256]{1,0:T(8,128)(2,1)}, bf16[512,256]{1,0:T(8,128)(2,1)S(1)}, u32[]{:S(2)}, u32[]{:S(2)}) collective-permute-start(bf16[512,256]{1,0:T(8,128)(2,1)} %collective-permute-done.5.rest_5_), channel_id=1, source_target_pairs={{0,1},{1,0},{2,3},{3,2},{4,5},{5,4},{6,7},{7,6},{8,9},{9,8},{10,11... | collective-permute-start | bytes 786440 | tf_op jit(solution)/shard_map/ppermute | solution.py:449
  54.6 15.1 %collective-permute-start.13 = (bf16[512,256]{1,0:T(8,128)(2,1)S(1)}, bf16[512,256]{1,0:T(8,128)(2,1)S(1)}, u32[]{:S(2)}, u32[]{:S(2)}) collective-permute-start(bf16[512,256]{1,0:T(8,128)(2,1)S(1)} %collective-permute-done.6.rest_6_), channel_id=1, source_target_pairs={{0,1},{1,0},{2,3},{3,2},{4,5},{5,4},{6,7},{7,6},{8,9},{9,8},{10,11... | collective-permute-start | bytes 786440 | tf_op jit(solution)/shard_map/ppermute | solution.py:449
  55.1 14.6 %collective-permute-start.14 = (bf16[512,256]{1,0:T(8,128)(2,1)S(1)}, bf16[512,256]{1,0:T(8,128)(2,1)S(1)}, u32[]{:S(2)}, u32[]{:S(2)}) collective-permute-start(bf16[512,256]{1,0:T(8,128)(2,1)S(1)} %collective-permute-done.7.rest_7_), channel_id=1, source_target_pairs={{0,1},{1,0},{2,3},{3,2},{4,5},{5,4},{6,7},{7,6},{8,9},{9,8},{10,11... | collective-permute-start | bytes 786440 | tf_op jit(solution)/shard_map/ppermute | solution.py:449
  (6 other events, 56.2 us)

commit v3 on v2

--- a/solution.py
+++ b/solution.py
@@ -152,16 +152,17 @@
         keepdims=True,
     )
     slot = (2.0 * own_t[0:1, :] + rank).astype(I32)
-    place = (iota((SLOTS, TILES), 0) == slot).astype(F32).astype(BF)
-    cell = jnp.broadcast_to(cell_ref[...].astype(F32), square).T + 1.0
-    pay_ref[:, 0:D] = dot(place, pooled.astype(BF)).astype(BF)
-    pay_ref[:, D:PAY] = dot(place, cell.astype(BF)).astype(BF)
+    cell = (jnp.broadcast_to(cell_ref[...].astype(F32), square).T + 1.0).astype(BF)
+    for k in range(2):
+        place = (2 * iota(square, 0) + k == slot).astype(F32).astype(BF)
+        pay_ref[:, k, 0:D] = dot(place, pooled.astype(BF)).astype(BF)
+        pay_ref[:, k, D:PAY] = dot(place, cell).astype(BF)
 
 
 def pool_call(obs_values, tile_owner, tile_cell, tile_count, w_obs_in):
     return pl.pallas_call(
         pool_kernel,
-        out_shape=jax.ShapeDtypeStruct((SLOTS, PAY), BF),
+        out_shape=jax.ShapeDtypeStruct((SLOTS // 2, 2, PAY), BF),
         in_specs=[SMEM] + [VMEM] * 5,
         out_specs=VMEM,
         scratch_shapes=[
@@ -378,10 +379,11 @@
             ahead, rate_s, q_ref, key_ref, value_ref, ahead_ref, context_ref, top_ref, sum_ref, acc_ref
         )
 
-    cell = pay_ref[:, D:PAY].astype(F32).T
+    pay = jnp.concatenate([pay_ref[:, 0, :], pay_ref[:, 1, :]], axis=0)
+    cell = pay[:, D:PAY].astype(F32).T
     cell = jnp.broadcast_to(cell[0:1, :], (ROWS, SLOTS)).astype(I32)
     place = (iota((ROWS, SLOTS), 0) + 1 == cell).astype(F32).astype(BF)
-    pooled = dot(place, pay_ref[:, 0:D]).astype(BF)
+    pooled = dot(place, pay[:, 0:D]).astype(BF)
     context = context_ref[...].T.astype(BF)
     copies[0].wait()
     mixed = tok_ref[...].astype(F32) + dot(context, w_out_ref[...])
@@ -483,18 +485,16 @@
     across = send(kv, 1, 0, 0)
     far = send(kv, 0, 2, 0)
     sibling = send(kv, 0, 0, 1)
-    q, part = first_call(head_rate, normed, w_query, kv)
-    part, tile_count, up, down, across, far, sibling = lax.optimization_barrier(
-        (part, tile_count, up, down, across, far, sibling)
+    pay = pool_call(obs_values, tile_owner, tile_cell, tile_count, w_obs_in)
+    pay, normed, up, down, across, far, sibling = lax.optimization_barrier(
+        (pay, normed, up, down, across, far, sibling)
     )
     late = [send(across, 0, 1, 0), send(across, 0, 3, 0), send(far, 1, 0, 0)]
     near = [across, up, down, far]
     near_twin = [send(b, 0, 0, 1) for b in near]
-    pay = pool_call(obs_values, tile_owner, tile_cell, tile_count, w_obs_in)
-    pay, *late = lax.optimization_barrier((pay, *late, *near_twin))
-    late, near_twin = late[:3], late[3:]
+    pay = lax.all_to_all(pay, ("lat", "lon"), split_axis=0, concat_axis=0, tiled=True)
+    q, part = first_call(head_rate, normed, w_query, kv)
     late_twin = [send(b, 0, 0, 1) for b in late]
-    pay = lax.all_to_all(pay, ("lat", "lon"), split_axis=0, concat_axis=0, tiled=True)
 
     near_moves = [(1, 0, 0), (0, 1, 0), (0, 3, 0), (0, 2, 0)]
     late_moves = [(1, 1, 0), (1, 3, 0), (1, 2, 0)]

time: 201 us -> 185 us (0.920)
  waiting for transfers between devices: 15.4 us -> 3.72 us
  local copies, waits for them, and re-layouts: 4.81 us -> 1.61 us
  starting transfers between devices: 23.9 us -> 20.8 us
    all_to_all x1, waiting for transfers between devices: 13.4 us -> 3.68 us  [shards(): lax.all_to_all(pay, ('lat', 'lon'), split_axis=0, concat_axis=0, tiled=True)]
    all_to_all x2 -> x0, local copies, waits for them, and re-layouts: 3.96 us -> none  [shards(): lax.all_to_all(pay, ('lat', 'lon'), split_axis=0, concat_axis=0, tiled=True)]
    all_to_all x1, starting transfers between devices: 10.8 us -> 7.59 us  [shards(): lax.all_to_all(pay, ('lat', 'lon'), split_axis=0, concat_axis=0, tiled=True)]
  transfers between devices with their start and end apart: 16 -> 16, of which waited for: 2 -> 1; matrix products, arithmetic and copies ran while one was open for 0% -> 0% of each run, Pallas kernels for 12% -> 13%
where the time goes in v3:
time: 185 us; the launch traced here: 184 us
  Pallas kernels  157 us (85%)
  starting transfers between devices  20.8 us (11%)
  waiting for transfers between devices  3.72 us (2%)
    pallas_call x1, Pallas kernels, last_call(): pl.pallas_call(functools.partial(last_kernel, moves), out_shape=jax.Shape...  130 us
    pallas_call x1, Pallas kernels, pool_call(): pl.pallas_call(pool_kernel, out_shape=jax.ShapeDtypeStruct((SLOTS // 2, 2...  16.4 us
    ppermute x15, starting transfers between devices, send(): return lax.ppermute(block, 'lon', pairs)  13.2 us
    pallas_call x1, Pallas kernels, first_call(): pl.pallas_call(first_kernel, out_shape=(jax.ShapeDtypeStruct((HEADS, 128,...  8.08 us
    all_to_all x1, starting transfers between devices, shards(): lax.all_to_all(pay, ('lat', 'lon'), split_axis=0, concat_axis=0, tiled=True)  7.59 us
  transfers between devices with their start and end apart: 16, of which 1 were waited for; matrix products, arithmetic and copies ran while one was open for 0% of the time, Pallas kernels for 13%

profile of v3, /device:TPU:0, one launch (start us, length us, event | category | flops | bytes accessed | tf_op | source)
XLA Modules:
  0.0 183.9 jit_solution(18121217346554765176)
XLA Ops:
  0.0 2.7 %norm_keys_values.1 = (bf16[256,1024]{1,0:T(8,128)(2,1)}, bf16[512,256]{1,0:T(8,128)(2,1)}) custom-call(bf16[256,1024]{1,0:T(8,128)(2,1)} %tok_ref.3, f32[1,1024]{1,0:T(1,128)} %bitcast.9, bf16[1024,256]{1,0:T(8,128)(2,1)} %wk_ref.1, bf16[1024,256]{1,0:T(8,128)(2,1)} %wv_ref.1), custom_call_target="tpu_custom_call" | custom-call | flops 3000000000 | bytes 3000000 | tf_op jit(solution)/shard_map/norm_keys_values/pallas_call | solution.py:74
  2.7 2.0 %collective-permute-start = (bf16[512,256]{1,0:T(8,128)(2,1)}, bf16[512,256]{1,0:T(8,128)(2,1)S(1)}, u32[]{:S(2)}, u32[]{:S(2)}) collective-permute-start(bf16[512,256]{1,0:T(8,128)(2,1)} %get-tuple-element.17.kv_ref.rest_0_), channel_id=1, source_target_pairs={{0,2},{1,3},{2,4},{3,5},{4,6},{5,7},{6,0},{7,1},{8,10},{9,11},{10,... | collective-permute-start | bytes 786440 | tf_op jit(solution)/shard_map/ppermute | solution.py:451
  4.7 2.1 %collective-permute-start.1 = (bf16[512,256]{1,0:T(8,128)(2,1)}, bf16[512,256]{1,0:T(8,128)(2,1)S(1)}, u32[]{:S(2)}, u32[]{:S(2)}) collective-permute-start(bf16[512,256]{1,0:T(8,128)(2,1)} %get-tuple-element.17.kv_ref.rest_0_), channel_id=1, source_target_pairs={{0,6},{1,7},{2,0},{3,1},{4,2},{5,3},{6,4},{7,5},{8,14},{9,15},{10,... | collective-permute-start | bytes 786440 | tf_op jit(solution)/shard_map/ppermute | solution.py:451
  6.8 1.5 collective-permute-start.2
  8.3 1.9 %collective-permute-start.3 = (bf16[512,256]{1,0:T(8,128)(2,1)}, bf16[512,256]{1,0:T(8,128)(2,1)S(1)}, u32[]{:S(2)}, u32[]{:S(2)}) collective-permute-start(bf16[512,256]{1,0:T(8,128)(2,1)} %get-tuple-element.17.kv_ref.rest_0_), channel_id=1, source_target_pairs={{0,4},{1,5},{2,6},{3,7},{4,0},{5,1},{6,2},{7,3},{8,12},{9,13},{10,... | collective-permute-start | bytes 786440 | tf_op jit(solution)/shard_map/ppermute | solution.py:451
  10.2 16.4 %pool_tiles.1 = bf16[128,2,1152]{2,1,0:T(2,128)(2,1)} custom-call(s32[128]{0:T(128)} %cnt_s.1, bf16[4096,128]{1,0:T(8,128)(2,1)} %bitcast.8, s32[1,128]{1,0:T(1,128)} %bitcast.11, s32[1,128]{1,0:T(1,128)} %bitcast.12, s32[1,128]{1,0:T(1,128)} %bitcast.13, bf16[32,1024]{1,0:T(8,128)(2,1)} %w_ref.1), custom_call_target="tpu_custom_call" | custom-call | flops 15000000512 | bytes 15000000 | tf_op jit(solution)/shard_map/pool_tiles/pallas_call | solution.py:163
  26.6 0.0 collective-permute-done.2.rest_1_
  26.6 1.1 collective-permute-start.5
  27.7 2.2 %collective-permute-start.6 = (bf16[512,256]{1,0:T(8,128)(2,1)S(1)}, bf16[512,256]{1,0:T(8,128)(2,1)S(1)}, u32[]{:S(2)}, u32[]{:S(2)}) collective-permute-start(bf16[512,256]{1,0:T(8,128)(2,1)S(1)} %collective-permute-done.2.rest_1_), channel_id=1, source_target_pairs={{0,6},{1,7},{2,0},{3,1},{4,2},{5,3},{6,4},{7,5},{8,14},{9,15},{10,... | collective-permute-start | bytes 786440 | tf_op jit(solution)/shard_map/ppermute | solution.py:451
  30.0 0.5 collective-permute-start.7
  30.5 0.0 collective-permute-start.8
  30.5 0.5 collective-permute-start.9
  31.0 7.6 %all-to-all-start = ((bf16[128,2,1152]{2,1,0:T(2,128)(2,1)}), bf16[128,2,1152]{2,1,0:T(2,128)(2,1)S(1)}, u32[]{:S(2)}, u32[]{:S(2)}) async-start(bf16[128,2,1152]{2,1,0:T(2,128)(2,1)} %pool_tiles.1), calls=%async_computation | async-start | bytes 1179648 | tf_op jit(solution)/shard_map/all_to_all | solution.py:495
  38.6 0.1 collective-permute-start.11
  38.7 0.5 collective-permute-start.10
  39.2 0.1 collective-permute-start.12
  39.3 0.4 collective-permute-start.13
  39.7 0.3 collective-permute-start.14
  40.0 8.1 %queries_own_rows.1 = (bf16[16,128,256]{2,1,0:T(8,128)(2,1)}, f32[16,80,256]{2,1,0:T(8,128)}) custom-call(f32[16]{0:T(128)} %rate_s.3, bf16[256,1024]{1,0:T(8,128)(2,1)} %get-tuple-element.18.normed_ref, bf16[1024,1024]{1,0:T(8,128)(2,1)} %wq_ref.1, bf16[512,256]{1,0:T(8,128)(2,1)} %get-tuple-element.17.kv_ref.rest_0_), custom_call_target="tpu_custom_call" | custom-call | flops 5000000000 | bytes 5000000 | tf_op jit(solution)/shard_map/queries_own_rows/pallas_call | solution.py:235
  48.3 0.6 copy-done.12
  48.9 0.1 copy-done.13
  49.0 3.7 %all-to-all-done.pay_ref = bf16[128,2,1152]{2,1,0:T(2,128)(2,1)S(1)} async-done(((bf16[128,2,1152]{2,1,0:T(2,128)(2,1)}), bf16[128,2,1152]{2,1,0:T(2,128)(2,1)S(1)}, u32[]{:S(2)}, u32[]{:S(2)}) %all-to-all-start) | async-done | bytes 589856 | tf_op jit(solution)/shard_map/all_to_all | solution.py:495
  52.7 0.8 copy-done
  53.5 130.2 %other_rows_project_update_mlp.1 = bf16[256,1024]{1,0:T(8,128)(2,1)} custom-call(f32[16]{0:T(128)} %rate_s.3, bf16[256,1024]{1,0:T(8,128)(2,1)} %tok_ref.3, f32[1,1024]{1,0:T(1,128)} %bitcast.10, bf16[16,128,256]{2,1,0:T(8,128)(2,1)} %get-tuple-element.19.q_ref, f32[16,80,256]{2,1,0:T(8,128)} %get-tuple-element.20.part_ref, bf16[128,2,1152]{2,1,0:T(2,128)(2,1)} %copy-done, ...), custom_call_target="tpu_custom_call" | custom-call | flops 24000000000 | bytes 24000000 | tf_op jit(solution)/shard_map/other_rows_project_update_mlp/pallas_call | solution.py:402
  (40 shorter events, 0.1 us)
Async XLA Ops:
  2.7 23.9 %collective-permute-start = (bf16[512,256]{1,0:T(8,128)(2,1)}, bf16[512,256]{1,0:T(8,128)(2,1)S(1)}, u32[]{:S(2)}, u32[]{:S(2)}) collective-permute-start(bf16[512,256]{1,0:T(8,128)(2,1)} %get-tuple-element.17.kv_ref.rest_0_), channel_id=1, source_target_pairs={{0,2},{1,3},{2,4},{3,5},{4,6},{5,7},{6,0},{7,1},{8,10},{9,11},{10,... | collective-permute-start | bytes 786440 | tf_op jit(solution)/shard_map/ppermute | solution.py:451
  4.7 21.9 %collective-permute-start.1 = (bf16[512,256]{1,0:T(8,128)(2,1)}, bf16[512,256]{1,0:T(8,128)(2,1)S(1)}, u32[]{:S(2)}, u32[]{:S(2)}) collective-permute-start(bf16[512,256]{1,0:T(8,128)(2,1)} %get-tuple-element.17.kv_ref.rest_0_), channel_id=1, source_target_pairs={{0,6},{1,7},{2,0},{3,1},{4,2},{5,3},{6,4},{7,5},{8,14},{9,15},{10,... | collective-permute-start | bytes 786440 | tf_op jit(solution)/shard_map/ppermute | solution.py:451
  6.8 19.8 %collective-permute-start.2 = (bf16[512,256]{1,0:T(8,128)(2,1)}, bf16[512,256]{1,0:T(8,128)(2,1)S(1)}, u32[]{:S(2)}, u32[]{:S(2)}) collective-permute-start(bf16[512,256]{1,0:T(8,128)(2,1)} %get-tuple-element.17.kv_ref.rest_0_), channel_id=1, source_target_pairs={{0,8},{1,9},{2,10},{3,11},{4,12},{5,13},{6,14},{7,15},{8,0},{9,1},... | collective-permute-start | bytes 786440 | tf_op jit(solution)/shard_map/ppermute | solution.py:451
  8.3 18.3 %collective-permute-start.3 = (bf16[512,256]{1,0:T(8,128)(2,1)}, bf16[512,256]{1,0:T(8,128)(2,1)S(1)}, u32[]{:S(2)}, u32[]{:S(2)}) collective-permute-start(bf16[512,256]{1,0:T(8,128)(2,1)} %get-tuple-element.17.kv_ref.rest_0_), channel_id=1, source_target_pairs={{0,4},{1,5},{2,6},{3,7},{4,0},{5,1},{6,2},{7,3},{8,12},{9,13},{10,... | collective-permute-start | bytes 786440 | tf_op jit(solution)/shard_map/ppermute | solution.py:451
  10.2 16.4 %collective-permute-start.4 = (bf16[512,256]{1,0:T(8,128)(2,1)}, bf16[512,256]{1,0:T(8,128)(2,1)S(1)}, u32[]{:S(2)}, u32[]{:S(2)}) collective-permute-start(bf16[512,256]{1,0:T(8,128)(2,1)} %get-tuple-element.17.kv_ref.rest_0_), channel_id=1, source_target_pairs={{0,1},{1,0},{2,3},{3,2},{4,5},{5,4},{6,7},{7,6},{8,9},{9,8},{10,11... | collective-permute-start | bytes 786440 | tf_op jit(solution)/shard_map/ppermute | solution.py:451
  26.6 21.5 %copy-start.1 = (bf16[512,256]{1,0:T(8,128)(2,1)}, bf16[512,256]{1,0:T(8,128)(2,1)S(1)}, u32[]{:S(2)}) copy-start(bf16[512,256]{1,0:T(8,128)(2,1)S(1)} %collective-permute-done.rest_2_) | copy-start | bytes 786436
  26.6 21.5 %copy-start.2 = (bf16[512,256]{1,0:T(8,128)(2,1)}, bf16[512,256]{1,0:T(8,128)(2,1)S(1)}, u32[]{:S(2)}) copy-start(bf16[512,256]{1,0:T(8,128)(2,1)S(1)} %collective-permute-done.1.rest_3_) | copy-start | bytes 786436
  26.6 21.5 %copy-start.3 = (bf16[512,256]{1,0:T(8,128)(2,1)}, bf16[512,256]{1,0:T(8,128)(2,1)S(1)}, u32[]{:S(2)}) copy-start(bf16[512,256]{1,0:T(8,128)(2,1)S(1)} %collective-permute-done.2.rest_1_) | copy-start | bytes 786436
  26.6 21.5 %copy-start.4 = (bf16[512,256]{1,0:T(8,128)(2,1)}, bf16[512,256]{1,0:T(8,128)(2,1)S(1)}, u32[]{:S(2)}) copy-start(bf16[512,256]{1,0:T(8,128)(2,1)S(1)} %collective-permute-done.3.rest_4_) | copy-start | bytes 786436
  26.6 21.5 %copy-start.5 = (bf16[512,256]{1,0:T(8,128)(2,1)}, bf16[512,256]{1,0:T(8,128)(2,1)S(1)}, u32[]{:S(2)}) copy-start(bf16[512,256]{1,0:T(8,128)(2,1)S(1)} %collective-permute-done.4.rest_8_) | copy-start | bytes 786436
  26.6 11.9 %collective-permute-start.5 = (bf16[512,256]{1,0:T(8,128)(2,1)S(1)}, bf16[512,256]{1,0:T(8,128)(2,1)S(1)}, u32[]{:S(2)}, u32[]{:S(2)}) collective-permute-start(bf16[512,256]{1,0:T(8,128)(2,1)S(1)} %collective-permute-done.2.rest_1_), channel_id=1, source_target_pairs={{0,2},{1,3},{2,4},{3,5},{4,6},{5,7},{6,0},{7,1},{8,10},{9,11},{10,... | collective-permute-start | bytes 786440 | tf_op jit(solution)/shard_map/ppermute | solution.py:451
  27.7 11.0 %collective-permute-start.6 = (bf16[512,256]{1,0:T(8,128)(2,1)S(1)}, bf16[512,256]{1,0:T(8,128)(2,1)S(1)}, u32[]{:S(2)}, u32[]{:S(2)}) collective-permute-start(bf16[512,256]{1,0:T(8,128)(2,1)S(1)} %collective-permute-done.2.rest_1_), channel_id=1, source_target_pairs={{0,6},{1,7},{2,0},{3,1},{4,2},{5,3},{6,4},{7,5},{8,14},{9,15},{10,... | collective-permute-start | bytes 786440 | tf_op jit(solution)/shard_map/ppermute | solution.py:451
  30.0 9.3 %collective-permute-start.7 = (bf16[512,256]{1,0:T(8,128)(2,1)S(1)}, bf16[512,256]{1,0:T(8,128)(2,1)S(1)}, u32[]{:S(2)}, u32[]{:S(2)}) collective-permute-start(bf16[512,256]{1,0:T(8,128)(2,1)S(1)} %collective-permute-done.3.rest_4_), channel_id=1, source_target_pairs={{0,8},{1,9},{2,10},{3,11},{4,12},{5,13},{6,14},{7,15},{8,0},{9,1},... | collective-permute-start | bytes 786440 | tf_op jit(solution)/shard_map/ppermute | solution.py:451
  30.5 8.8 %collective-permute-start.8 = (bf16[512,256]{1,0:T(8,128)(2,1)S(1)}, bf16[512,256]{1,0:T(8,128)(2,1)S(1)}, u32[]{:S(2)}, u32[]{:S(2)}) collective-permute-start(bf16[512,256]{1,0:T(8,128)(2,1)S(1)} %collective-permute-done.2.rest_1_), channel_id=1, source_target_pairs={{0,1},{1,0},{2,3},{3,2},{4,5},{5,4},{6,7},{7,6},{8,9},{9,8},{10,11... | collective-permute-start | bytes 786440 | tf_op jit(solution)/shard_map/ppermute | solution.py:451
  30.5 9.2 %collective-permute-start.9 = (bf16[512,256]{1,0:T(8,128)(2,1)S(1)}, bf16[512,256]{1,0:T(8,128)(2,1)S(1)}, u32[]{:S(2)}, u32[]{:S(2)}) collective-permute-start(bf16[512,256]{1,0:T(8,128)(2,1)S(1)} %collective-permute-done.rest_2_), channel_id=1, source_target_pairs={{0,1},{1,0},{2,3},{3,2},{4,5},{5,4},{6,7},{7,6},{8,9},{9,8},{10,11... | collective-permute-start | bytes 786440 | tf_op jit(solution)/shard_map/ppermute | solution.py:451
  31.0 21.7 %all-to-all-start = ((bf16[128,2,1152]{2,1,0:T(2,128)(2,1)}), bf16[128,2,1152]{2,1,0:T(2,128)(2,1)S(1)}, u32[]{:S(2)}, u32[]{:S(2)}) async-start(bf16[128,2,1152]{2,1,0:T(2,128)(2,1)} %pool_tiles.1), calls=%async_computation | async-start | bytes 1179648 | tf_op jit(solution)/shard_map/all_to_all | solution.py:495
  38.6 9.5 %copy-start.6 = (bf16[512,256]{1,0:T(8,128)(2,1)}, bf16[512,256]{1,0:T(8,128)(2,1)S(1)}, u32[]{:S(2)}) copy-start(bf16[512,256]{1,0:T(8,128)(2,1)S(1)} %collective-permute-done.5.rest_5_) | copy-start | bytes 786436
  38.6 9.6 %collective-permute-start.11 = (bf16[512,256]{1,0:T(8,128)(2,1)S(1)}, bf16[512,256]{1,0:T(8,128)(2,1)S(1)}, u32[]{:S(2)}, u32[]{:S(2)}) collective-permute-start(bf16[512,256]{1,0:T(8,128)(2,1)S(1)} %collective-permute-done.3.rest_4_), channel_id=1, source_target_pairs={{0,1},{1,0},{2,3},{3,2},{4,5},{5,4},{6,7},{7,6},{8,9},{9,8},{10,11... | collective-permute-start | bytes 786440 | tf_op jit(solution)/shard_map/ppermute | solution.py:451
  38.7 9.4 %copy-start.7 = (bf16[512,256]{1,0:T(8,128)(2,1)}, bf16[512,256]{1,0:T(8,128)(2,1)S(1)}, u32[]{:S(2)}) copy-start(bf16[512,256]{1,0:T(8,128)(2,1)S(1)} %collective-permute-done.6.rest_6_) | copy-start | bytes 786436
  38.7 9.5 %collective-permute-start.10 = (bf16[512,256]{1,0:T(8,128)(2,1)S(1)}, bf16[512,256]{1,0:T(8,128)(2,1)S(1)}, u32[]{:S(2)}, u32[]{:S(2)}) collective-permute-start(bf16[512,256]{1,0:T(8,128)(2,1)S(1)} %collective-permute-done.1.rest_3_), channel_id=1, source_target_pairs={{0,1},{1,0},{2,3},{3,2},{4,5},{5,4},{6,7},{7,6},{8,9},{9,8},{10,11... | collective-permute-start | bytes 786440 | tf_op jit(solution)/shard_map/ppermute | solution.py:451
  39.2 8.9 %copy-start.8 = (bf16[512,256]{1,0:T(8,128)(2,1)}, bf16[512,256]{1,0:T(8,128)(2,1)S(1)}, u32[]{:S(2)}) copy-start(bf16[512,256]{1,0:T(8,128)(2,1)S(1)} %collective-permute-done.7.rest_7_) | copy-start | bytes 786436
  39.2 9.0 %collective-permute-start.12 = (bf16[512,256]{1,0:T(8,128)(2,1)S(1)}, bf16[512,256]{1,0:T(8,128)(2,1)S(1)}, u32[]{:S(2)}, u32[]{:S(2)}) collective-permute-start(bf16[512,256]{1,0:T(8,128)(2,1)S(1)} %collective-permute-done.5.rest_5_), channel_id=1, source_target_pairs={{0,1},{1,0},{2,3},{3,2},{4,5},{5,4},{6,7},{7,6},{8,9},{9,8},{10,11... | collective-permute-start | bytes 786440 | tf_op jit(solution)/shard_map/ppermute | solution.py:451
  39.3 8.9 %collective-permute-start.13 = (bf16[512,256]{1,0:T(8,128)(2,1)S(1)}, bf16[512,256]{1,0:T(8,128)(2,1)}, u32[]{:S(2)}, u32[]{:S(2)}) collective-permute-start(bf16[512,256]{1,0:T(8,128)(2,1)S(1)} %collective-permute-done.6.rest_6_), channel_id=1, source_target_pairs={{0,1},{1,0},{2,3},{3,2},{4,5},{5,4},{6,7},{7,6},{8,9},{9,8},{10,11... | collective-permute-start | bytes 786440 | tf_op jit(solution)/shard_map/ppermute | solution.py:451
  39.7 9.3 %collective-permute-start.14 = (bf16[512,256]{1,0:T(8,128)(2,1)S(1)}, bf16[512,256]{1,0:T(8,128)(2,1)}, u32[]{:S(2)}, u32[]{:S(2)}) collective-permute-start(bf16[512,256]{1,0:T(8,128)(2,1)S(1)} %collective-permute-done.7.rest_7_), channel_id=1, source_target_pairs={{0,1},{1,0},{2,3},{3,2},{4,5},{5,4},{6,7},{7,6},{8,9},{9,8},{10,11... | collective-permute-start | bytes 786440 | tf_op jit(solution)/shard_map/ppermute | solution.py:451
  (6 other events, 24.0 us)

commit v4 on v3

--- a/solution.py
+++ b/solution.py
@@ -205,7 +205,55 @@
     return jnp.concatenate([kv_ref[first : first + HD, :], jnp.ones((VT - HD, ROWS), BF)], axis=0)
 
 
-def first_kernel(rate_s, normed_ref, wq_ref, kv_ref, q_ref, out_ref, dist_ref):
+def place_lanes(first):
+    lane = iota((ROWS, 128), 1) - first
+    row = iota((ROWS, 128), 0)
+
+    def lanes(low, value):
+        return jnp.where((lane >= low) & (lane < low + 3), value, 0)
+
+    parts = (lanes(0, -row) + lanes(6, 1), lanes(0, row) + lanes(9, 1), lanes(12, 1), lanes(3, -ROWS))
+    return [p.astype(F32).astype(BF) for p in parts]
+
+
+def beside_keys(parts, ahead):
+    blocks = jnp.where(ahead < 8, ahead, LON - ahead).astype(F32)
+    blocks = jnp.full((ROWS, 128), blocks, F32).astype(BF)
+    return jnp.where(ahead < 8, parts[0], parts[1]) + parts[3] * blocks
+
+
+def lay_out(blocks, aheads, half_way, key_ref, value_ref):
+    lane = iota((ROWS, 128), 1)
+    parts = (place_lanes(HD), place_lanes(0))
+    for b, block in enumerate(blocks):
+        here = pl.ds(b * ROWS, ROWS)
+        extra = [p[2] if b == half_way else beside_keys(p, aheads[b]) for p in parts]
+        for group in range(KVH):
+            odd = group % 2
+            pair = block[0:ROWS, (group // 2) * 128 : (group // 2) * 128 + 128]
+            key_ref[group, here, :] = jnp.where((lane < HD) == (odd == 0), pair, extra[odd])
+            value_ref[group, :, here] = value_rows(block, group)
+
+
+def attend(total, group, head, chunks, gap, rate_s, q_ref, key_ref, value_ref):
+    first = 0
+    for size in chunks:
+        here = pl.ds(first * ROWS, size * ROWS)
+        scores = dot(key_ref[group, here, :], q_ref[head])
+        if gap is not None and first == 0:
+            far = scores[:ROWS] - (rate_s[head] * LOG2E) * gap
+            scores = jnp.concatenate([far, scores[ROWS:]], axis=0)
+        total = total + dot(value_ref[group, :, here], jnp.exp2(scores).astype(BF))
+        first = first + size
+    return total
+
+
+NEAR = (5, 4)
+
+
+def first_kernel(moves, rate_s, normed_ref, wq_ref, kv_ref, *rest):
+    blocks = rest[: len(moves)]
+    q_ref, out_ref, dist_ref, key_ref, value_ref = rest[len(moves) :]
     q = (dot(normed_ref[...], wq_ref[...]) * (0.125 * LOG2E)).T
     dist_ref[...] = jnp.abs(iota((ROWS, ROWS), 0) - iota((ROWS, ROWS), 1)).astype(F32)
     lane = iota((ROWS, 128), 1)
@@ -230,38 +278,47 @@
             extra = jnp.concatenate([extra, jnp.zeros((HD - 16, ROWS), BF)], axis=0)
             q_ref[head] = jnp.concatenate([own, extra] if even else [extra, own], axis=0)
 
-
-def first_call(head_rate, normed, w_query, kv):
+    lay_out(blocks, ahead_of(moves), 0, key_ref, value_ref)
+    gap = LON // 2 * ROWS - dist_ref[...]
+
+    @pl.loop(0, KVH)
+    def _(group):
+        for i in range(4):
+            head = group * 4 + i
+            out_ref[head] = attend(
+                out_ref[head], group, head, NEAR, gap, rate_s, q_ref, key_ref, value_ref
+            )
+
+
+def first_call(moves, head_rate, normed, w_query, kv, blocks):
+    count = len(blocks)
     return pl.pallas_call(
-        first_kernel,
+        functools.partial(first_kernel, moves),
         out_shape=(
             jax.ShapeDtypeStruct((HEADS, 128, ROWS), BF),
             jax.ShapeDtypeStruct((HEADS, VT, ROWS), F32),
         ),
-        in_specs=[SMEM] + [VMEM] * 3,
+        in_specs=[SMEM] + [VMEM] * (3 + count),
         out_specs=(VMEM, VMEM),
-        scratch_shapes=[pltpu.VMEM((ROWS, ROWS), F32)],
+        scratch_shapes=[
+            pltpu.VMEM((ROWS, ROWS), F32),
+            pltpu.VMEM((KVH, count * ROWS, 128), BF),
+            pltpu.VMEM((KVH, VT, count * ROWS), BF),
+        ],
         compiler_params=params(60),
-        cost_estimate=cost(5),
-        name="queries_own_rows",
-    )(head_rate, normed, w_query, kv)
-
-
-def place_lanes(ahead, first):
-    lane = iota((ROWS, 128), 1) - first
-    row = iota((ROWS, 128), 0)
-    plus = jnp.where(ahead < 8, 1, 0)
-    minus = jnp.where(ahead > 8, 1, 0)
-    blocks = jnp.where(ahead == 8, 0, jnp.where(ahead < 8, ahead, LON - ahead))
-    out = jnp.where(lane < 3, row * (minus - plus), -ROWS * blocks)
-    out = jnp.where(lane < 6, out, jnp.where(lane < 9, plus, jnp.where(lane < 12, minus, 1 - plus - minus)))
-    out = jnp.where((lane >= 0) & (lane < 15), out, 0)
-    return out.astype(F32).astype(BF)
-
-
-def careful(ahead, rate_s, q_ref, key_ref, value_ref, ahead_ref, context_ref, top_ref, sum_ref, acc_ref):
+        cost_estimate=cost(18),
+        name="queries_near_rows",
+    )(head_rate, normed, w_query, kv, *blocks)
+
+
+def careful(
+    blocks, aheads, rate_s, q_ref, kvs_ref, ahead_ref, context_ref, top_ref, sum_ref, acc_ref, sem
+):
     for b in range(LON):
-        ahead_ref[b] = ahead[b]
+        ahead_ref[b] = aheads[b]
+        copy = pltpu.make_async_copy(blocks[b], kvs_ref.at[b], sem)
+        copy.start()
+        copy.wait()
     lane = iota((ROWS, 128), 1)
     for group in range(KVH):
 
@@ -274,8 +331,7 @@
 
             @pl.loop(0, LON)
             def _(b):
-                here = pl.ds(pl.multiple_of(b * ROWS, ROWS), ROWS)
-                keys = key_ref[group, here, :]
+                keys = kvs_ref[b, 0:ROWS, (group // 2) * 128 : (group // 2) * 128 + 128]
                 keys = jnp.where((lane < HD) == (group % 2 == 0), keys, jnp.zeros_like(keys))
                 gap = jnp.abs(ahead_ref[b] * ROWS + iota((ROWS, ROWS), 0) - iota((ROWS, ROWS), 1))
                 gap = jnp.minimum(gap, BAND - gap).astype(F32)
@@ -286,15 +342,15 @@
                 top_ref[...] = top
                 sum_ref[...] = sum_ref[...] * shrink + jnp.sum(weights, axis=0, keepdims=True)
                 acc_ref[...] = acc_ref[...] * shrink + dot(
-                    value_ref[group, 0:HD, here], weights.astype(BF)
+                    kvs_ref[b, ROWS + group * HD : ROWS + group * HD + HD, :], weights.astype(BF)
                 )
 
             context_ref[pl.ds(pl.multiple_of(head * HD, HD), HD), :] = acc_ref[...] / sum_ref[...]
 
 
-STEP = 1024
+STEP = 2048
 STEPS = FF // STEP
-CHUNK = 5
+LATE = (3, 3)
 
 
 def last_kernel(
@@ -312,6 +368,8 @@
     *rest,
 ):
     blocks = rest[:LON]
+    count = sum(LATE)
+    late = rest[LON : LON + count]
     (
         out_ref,
         w_out_ref,
@@ -326,8 +384,10 @@
         top_ref,
         sum_ref,
         acc_ref,
+        kvs_ref,
         sem,
-    ) = rest[LON:]
+        spare,
+    ) = rest[LON + count :]
     copies = [
         pltpu.make_async_copy(w_out_hbm, w_out_ref, sem.at[0]),
         pltpu.make_async_copy(w_obs_hbm, w_obs_ref, sem.at[1]),
@@ -341,32 +401,17 @@
     for copy in copies:
         copy.start()
 
-    ahead = ahead_of(moves)
-    lane = iota((ROWS, 128), 1)
-    for b in range(LON):
-        here = pl.ds(b * ROWS, ROWS)
-        extra = (place_lanes(ahead[b], HD), place_lanes(ahead[b], 0))
-        for group in range(KVH):
-            odd = group % 2
-            pair = blocks[b][0:ROWS, (group // 2) * 128 : (group // 2) * 128 + 128]
-            key_ref[group, here, :] = jnp.where((lane < HD) == (odd == 0), pair, extra[odd])
-            value_ref[group, :, here] = value_rows(blocks[b], group)
-    gap = LON // 2 * ROWS - jnp.abs(iota((ROWS, ROWS), 0) - iota((ROWS, ROWS), 1))
-    gap = gap.astype(F32)
+    aheads = ahead_of(moves)
+    lay_out(late, aheads[LON - count :], None, key_ref, value_ref)
     largest_ref[...] = jnp.zeros((1, ROWS), F32)
 
     @pl.loop(0, KVH)
     def _(group):
         for i in range(4):
             head = group * 4 + i
-            total = part_ref[head]
-            for first in range(1, LON, CHUNK):
-                here = pl.ds(first * ROWS, CHUNK * ROWS)
-                scores = dot(key_ref[group, here, :], q_ref[head])
-                if first == 1:
-                    far = scores[:ROWS] - (rate_s[head] * LOG2E) * gap
-                    scores = jnp.concatenate([far, scores[ROWS:]], axis=0)
-                total = total + dot(value_ref[group, :, here], jnp.exp2(scores).astype(BF))
+            total = attend(
+                part_ref[head], group, head, LATE, None, rate_s, q_ref, key_ref, value_ref
+            )
             weight_sum = total[HD : HD + 1]
             largest_ref[...] = jnp.maximum(largest_ref[...], weight_sum)
             context_ref[pl.ds(pl.multiple_of(head * HD, HD), HD), :] = total[:HD] * (
@@ -376,7 +421,17 @@
     @pl.when(jnp.logical_not(jnp.max(largest_ref[...]) < 2.0**100))
     def _():
         careful(
-            ahead, rate_s, q_ref, key_ref, value_ref, ahead_ref, context_ref, top_ref, sum_ref, acc_ref
+            blocks,
+            aheads,
+            rate_s,
+            q_ref,
+            kvs_ref,
+            ahead_ref,
+            context_ref,
+            top_ref,
+            sum_ref,
+            acc_ref,
+            spare,
         )
 
     pay = jnp.concatenate([pay_ref[:, 0, :], pay_ref[:, 1, :]], axis=0)
@@ -390,10 +445,10 @@
     copies[1].wait()
     mixed = (mixed + dot(pooled, w_obs_ref[...])).astype(BF).astype(F32)
     normed = normed_rows(mixed, gain_ref[...])
+    for copy in copies[2:]:
+        copy.wait()
     for s in range(STEPS):
-        copies[2 + 2 * s].wait()
         hidden = (0.5 * twice_gelu(dot(normed, w_up_ref[s]))).astype(BF)
-        copies[3 + 2 * s].wait()
         mixed = mixed + dot(hidden, w_down_ref[s])
     out_ref[...] = mixed.astype(BF)
 
@@ -402,26 +457,28 @@
     return pl.pallas_call(
         functools.partial(last_kernel, moves),
         out_shape=jax.ShapeDtypeStruct((ROWS, D), BF),
-        in_specs=[SMEM] + [VMEM] * 5 + [ANY] * 4 + [VMEM] * LON,
+        in_specs=[SMEM] + [VMEM] * 5 + [ANY] * (4 + LON) + [VMEM] * sum(LATE),
         out_specs=VMEM,
         scratch_shapes=[
             pltpu.VMEM((D, D), BF),
             pltpu.VMEM((D, D), BF),
             pltpu.VMEM((STEPS, D, STEP), BF),
             pltpu.VMEM((STEPS, STEP, D), BF),
-            pltpu.VMEM((KVH, BAND, 128), BF),
-            pltpu.VMEM((KVH, VT, BAND), BF),
+            pltpu.VMEM((KVH, sum(LATE) * ROWS, 128), BF),
+            pltpu.VMEM((KVH, VT, sum(LATE) * ROWS), BF),
             pltpu.VMEM((D, ROWS), F32),
             pltpu.VMEM((1, ROWS), F32),
             pltpu.SMEM((LON,), I32),
             pltpu.VMEM((1, ROWS), F32),
             pltpu.VMEM((1, ROWS), F32),
             pltpu.VMEM((HD, ROWS), F32),
+            pltpu.VMEM((LON, 2 * ROWS, KVH * HD), BF),
             pltpu.SemaphoreType.DMA((2 + 2 * STEPS,)),
+            pltpu.SemaphoreType.DMA,
         ],
         compiler_params=params(60),
-        cost_estimate=cost(24),
-        name="other_rows_project_update_mlp",
+        cost_estimate=cost(17),
+        name="late_rows_project_update_mlp",
     )(
         head_rate,
         tokens,
@@ -434,6 +491,7 @@
         w_up,
         w_down,
         *blocks,
+        *blocks[LON - sum(LATE) :],
     )
 
 
@@ -493,15 +551,16 @@
     near = [across, up, down, far]
     near_twin = [send(b, 0, 0, 1) for b in near]
     pay = lax.all_to_all(pay, ("lat", "lon"), split_axis=0, concat_axis=0, tiled=True)
-    q, part = first_call(head_rate, normed, w_query, kv)
     late_twin = [send(b, 0, 0, 1) for b in late]
 
     near_moves = [(1, 0, 0), (0, 1, 0), (0, 3, 0), (0, 2, 0)]
     late_moves = [(1, 1, 0), (1, 3, 0), (1, 2, 0)]
-    moves = [(0, 0, 0)] + near_moves + late_moves + [(0, 0, 1)]
-    moves = moves + [(x, z, 1) for x, z, _ in near_moves + late_moves]
+    near_moves = near_moves + [(0, 0, 1)] + [(x, z, 1) for x, z, _ in near_moves]
+    late_moves = late_moves + [(x, z, 1) for x, z, _ in late_moves]
+    near = near + [sibling] + near_twin
+    q, part = first_call(near_moves, head_rate, normed, w_query, kv, near)
     return last_call(
-        moves,
+        [(0, 0, 0)] + near_moves + late_moves,
         head_rate,
         tokens,
         mlp_gain,
@@ -512,7 +571,7 @@
         w_obs_out,
         w_up,
         w_down,
-        [kv] + near + late + [sibling] + near_twin + late_twin,
+        [kv] + near + late + late_twin,
     )
 
 

time: 185 us -> 199 us (1.076)
  Pallas kernels: 157 us -> 173 us
  waiting for transfers between devices: 3.72 us -> 0.04 us
    pallas_call x1, Pallas kernels: 8.08 us -> 19.6 us  [first_call(): pl.pallas_call(functools.partial(first_kernel, moves), out_shape=(jax.Sha...]
    pallas_call x1, Pallas kernels: 130 us -> 135 us  [last_call(): pl.pallas_call(functools.partial(last_kernel, moves), out_shape=jax.Shape...]
    all_to_all x1, waiting for transfers between devices: 3.68 us -> 0.01 us  [shards(): lax.all_to_all(pay, ('lat', 'lon'), split_axis=0, concat_axis=0, tiled=True)]
  transfers between devices with their start and end apart: 16 -> 16, of which waited for: 1 -> 0; matrix products, arithmetic and copies ran while one was open for 0% -> 0% of each run, Pallas kernels for 13% -> 18%
where the time goes in v4:
time: 199 us; the launch traced here: 198 us
  Pallas kernels  173 us (87%)
  starting transfers between devices  21.4 us (11%)
  local copies, waits for them, and re-layouts  2.89 us (1%)
    pallas_call x1, Pallas kernels, last_call(): pl.pallas_call(functools.partial(last_kernel, moves), out_shape=jax.Shape...  135 us
    pallas_call x1, Pallas kernels, first_call(): pl.pallas_call(functools.partial(first_kernel, moves), out_shape=(jax.Sha...  19.6 us
    pallas_call x1, Pallas kernels, pool_call(): pl.pallas_call(pool_kernel, out_shape=jax.ShapeDtypeStruct((SLOTS // 2, 2...  16.4 us
    ppermute x15, starting transfers between devices, send(): return lax.ppermute(block, 'lon', pairs)  13.3 us
    all_to_all x1, starting transfers between devices, shards(): lax.all_to_all(pay, ('lat', 'lon'), split_axis=0, concat_axis=0, tiled=True)  8.14 us
  transfers between devices with their start and end apart: 16, of which 0 were waited for; matrix products, arithmetic and copies ran while one was open for 0% of the time, Pallas kernels for 18%

profile of v4, /device:TPU:0, one launch (start us, length us, event | category | flops | bytes accessed | tf_op | source)
XLA Modules:
  0.0 198.1 jit_solution(890184766030975960)
XLA Ops:
  0.0 2.7 %norm_keys_values.1 = (bf16[256,1024]{1,0:T(8,128)(2,1)}, bf16[512,256]{1,0:T(8,128)(2,1)}) custom-call(bf16[256,1024]{1,0:T(8,128)(2,1)} %tok_ref.3, f32[1,1024]{1,0:T(1,128)} %bitcast.9, bf16[1024,256]{1,0:T(8,128)(2,1)} %wk_ref.1, bf16[1024,256]{1,0:T(8,128)(2,1)} %wv_ref.1), custom_call_target="tpu_custom_call" | custom-call | flops 3000000000 | bytes 3000000 | tf_op jit(solution)/shard_map/norm_keys_values/pallas_call | solution.py:74
  2.7 2.0 %collective-permute-start = (bf16[512,256]{1,0:T(8,128)(2,1)}, bf16[512,256]{1,0:T(8,128)(2,1)S(1)}, u32[]{:S(2)}, u32[]{:S(2)}) collective-permute-start(bf16[512,256]{1,0:T(8,128)(2,1)} %get-tuple-element.17.kv_ref.rest_0_), channel_id=1, source_target_pairs={{0,2},{1,3},{2,4},{3,5},{4,6},{5,7},{6,0},{7,1},{8,10},{9,11},{10,... | collective-permute-start | bytes 786440 | tf_op jit(solution)/shard_map/ppermute | solution.py:509
  4.7 2.1 %collective-permute-start.1 = (bf16[512,256]{1,0:T(8,128)(2,1)}, bf16[512,256]{1,0:T(8,128)(2,1)S(1)}, u32[]{:S(2)}, u32[]{:S(2)}) collective-permute-start(bf16[512,256]{1,0:T(8,128)(2,1)} %get-tuple-element.17.kv_ref.rest_0_), channel_id=1, source_target_pairs={{0,6},{1,7},{2,0},{3,1},{4,2},{5,3},{6,4},{7,5},{8,14},{9,15},{10,... | collective-permute-start | bytes 786440 | tf_op jit(solution)/shard_map/ppermute | solution.py:509
  6.8 1.5 collective-permute-start.2
  8.3 1.9 collective-permute-start.3
  10.2 0.0 collective-permute-start.4
  10.2 16.4 %pool_tiles.1 = bf16[128,2,1152]{2,1,0:T(2,128)(2,1)} custom-call(s32[128]{0:T(128)} %cnt_s.1, bf16[4096,128]{1,0:T(8,128)(2,1)} %bitcast.8, s32[1,128]{1,0:T(1,128)} %bitcast.11, s32[1,128]{1,0:T(1,128)} %bitcast.12, s32[1,128]{1,0:T(1,128)} %bitcast.13, bf16[32,1024]{1,0:T(8,128)(2,1)} %w_ref.1), custom_call_target="tpu_custom_call" | custom-call | flops 15000000512 | bytes 15000000 | tf_op jit(solution)/shard_map/pool_tiles/pallas_call | solution.py:163
  26.6 0.0 collective-permute-done.rest_1_.rest_2_
  26.6 0.6 collective-permute-start.5
  27.2 0.1 collective-permute-start.6
  27.3 0.9 collective-permute-start.9
  28.2 2.3 %collective-permute-start.10 = (bf16[512,256]{1,0:T(8,128)(2,1)S(1)}, bf16[512,256]{1,0:T(8,128)(2,1)S(1)}, u32[]{:S(2)}, u32[]{:S(2)}) collective-permute-start(bf16[512,256]{1,0:T(8,128)(2,1)S(1)} %collective-permute-done.2.rest_0_.rest_1_), channel_id=1, source_target_pairs={{0,6},{1,7},{2,0},{3,1},{4,2},{5,3},{6,4},{7,5},{8,14},{9,15},{10,... | collective-permute-start | bytes 786440 | tf_op jit(solution)/shard_map/ppermute | solution.py:509
  30.6 0.5 collective-permute-start.11
  31.1 0.5 collective-permute-start.8
  31.6 8.1 %all-to-all-start = ((bf16[128,2,1152]{2,1,0:T(2,128)(2,1)}), bf16[128,2,1152]{2,1,0:T(2,128)(2,1)S(1)}, u32[]{:S(2)}, u32[]{:S(2)}) async-start(bf16[128,2,1152]{2,1,0:T(2,128)(2,1)} %pool_tiles.1), calls=%async_computation | async-start | bytes 1179648 | tf_op jit(solution)/shard_map/all_to_all | solution.py:553
  39.8 0.1 collective-permute-start.12
  39.9 0.5 collective-permute-start.13
  40.4 0.3 collective-permute-start.14
  40.7 0.6 copy-done.11
  41.4 19.6 %queries_near_rows.1 = (bf16[16,128,256]{2,1,0:T(8,128)(2,1)}, f32[16,80,256]{2,1,0:T(8,128)}) custom-call(f32[16]{0:T(128)} %rate_s.3, bf16[256,1024]{1,0:T(8,128)(2,1)} %get-tuple-element.18.normed_ref, bf16[1024,1024]{1,0:T(8,128)(2,1)} %wq_ref.1, bf16[512,256]{1,0:T(8,128)(2,1)} %get-tuple-element.17.kv_ref.rest_0_, bf16[512,256]{1,0:T(8,128)(2,1)} %copy-done.3, ...), custom_call_target="tpu_custom_call" | custom-call | flops 17999998976 | bytes 18000000 | tf_op jit(solution)/shard_map/queries_near_rows/pallas_call | solution.py:295
  61.1 0.7 copy-done.12
  61.7 0.7 copy-done.13
  62.5 0.8 copy-done
  63.3 134.7 %late_rows_project_update_mlp.1 = bf16[256,1024]{1,0:T(8,128)(2,1)} custom-call(f32[16]{0:T(128)} %rate_s.3, bf16[256,1024]{1,0:T(8,128)(2,1)} %tok_ref.3, f32[1,1024]{1,0:T(1,128)} %bitcast.10, bf16[16,128,256]{2,1,0:T(8,128)(2,1)} %get-tuple-element.24.q_ref, f32[16,80,256]{2,1,0:T(8,128)} %get-tuple-element.25.part_ref, bf16[128,2,1152]{2,1,0:T(2,128)(2,1)} %copy-done, ...), custom_call_target="tpu_custom_call" | custom-call | flops 16999999488 | bytes 17000000 | tf_op jit(solution)/shard_map/late_rows_project_update_mlp/pallas_call | solution.py:457
  (40 shorter events, 0.1 us)
Async XLA Ops:
  2.7 23.9 %collective-permute-start = (bf16[512,256]{1,0:T(8,128)(2,1)}, bf16[512,256]{1,0:T(8,128)(2,1)S(1)}, u32[]{:S(2)}, u32[]{:S(2)}) collective-permute-start(bf16[512,256]{1,0:T(8,128)(2,1)} %get-tuple-element.17.kv_ref.rest_0_), channel_id=1, source_target_pairs={{0,2},{1,3},{2,4},{3,5},{4,6},{5,7},{6,0},{7,1},{8,10},{9,11},{10,... | collective-permute-start | bytes 786440 | tf_op jit(solution)/shard_map/ppermute | solution.py:509
  4.7 21.9 %collective-permute-start.1 = (bf16[512,256]{1,0:T(8,128)(2,1)}, bf16[512,256]{1,0:T(8,128)(2,1)S(1)}, u32[]{:S(2)}, u32[]{:S(2)}) collective-permute-start(bf16[512,256]{1,0:T(8,128)(2,1)} %get-tuple-element.17.kv_ref.rest_0_), channel_id=1, source_target_pairs={{0,6},{1,7},{2,0},{3,1},{4,2},{5,3},{6,4},{7,5},{8,14},{9,15},{10,... | collective-permute-start | bytes 786440 | tf_op jit(solution)/shard_map/ppermute | solution.py:509
  6.8 19.8 %collective-permute-start.2 = (bf16[512,256]{1,0:T(8,128)(2,1)}, bf16[512,256]{1,0:T(8,128)(2,1)S(1)}, u32[]{:S(2)}, u32[]{:S(2)}) collective-permute-start(bf16[512,256]{1,0:T(8,128)(2,1)} %get-tuple-element.17.kv_ref.rest_0_), channel_id=1, source_target_pairs={{0,8},{1,9},{2,10},{3,11},{4,12},{5,13},{6,14},{7,15},{8,0},{9,1},... | collective-permute-start | bytes 786440 | tf_op jit(solution)/shard_map/ppermute | solution.py:509
  8.3 18.3 %collective-permute-start.3 = (bf16[512,256]{1,0:T(8,128)(2,1)}, bf16[512,256]{1,0:T(8,128)(2,1)S(1)}, u32[]{:S(2)}, u32[]{:S(2)}) collective-permute-start(bf16[512,256]{1,0:T(8,128)(2,1)} %get-tuple-element.17.kv_ref.rest_0_), channel_id=1, source_target_pairs={{0,4},{1,5},{2,6},{3,7},{4,0},{5,1},{6,2},{7,3},{8,12},{9,13},{10,... | collective-permute-start | bytes 786440 | tf_op jit(solution)/shard_map/ppermute | solution.py:509
  10.2 16.4 %collective-permute-start.4 = (bf16[512,256]{1,0:T(8,128)(2,1)}, bf16[512,256]{1,0:T(8,128)(2,1)S(1)}, u32[]{:S(2)}, u32[]{:S(2)}) collective-permute-start(bf16[512,256]{1,0:T(8,128)(2,1)} %get-tuple-element.17.kv_ref.rest_0_), channel_id=1, source_target_pairs={{0,1},{1,0},{2,3},{3,2},{4,5},{5,4},{6,7},{7,6},{8,9},{9,8},{10,11... | collective-permute-start | bytes 786440 | tf_op jit(solution)/shard_map/ppermute | solution.py:509
  26.6 14.1 %copy-start.1 = (bf16[512,256]{1,0:T(8,128)(2,1)}, bf16[512,256]{1,0:T(8,128)(2,1)S(1)}, u32[]{:S(2)}) copy-start(bf16[512,256]{1,0:T(8,128)(2,1)S(1)} %collective-permute-done.rest_1_.rest_2_) | copy-start | bytes 786436
  26.6 14.1 %copy-start.2 = (bf16[512,256]{1,0:T(8,128)(2,1)}, bf16[512,256]{1,0:T(8,128)(2,1)S(1)}, u32[]{:S(2)}) copy-start(bf16[512,256]{1,0:T(8,128)(2,1)S(1)} %collective-permute-done.1.rest_2_.rest_3_) | copy-start | bytes 786436
  26.6 14.1 %copy-start.3 = (bf16[512,256]{1,0:T(8,128)(2,1)}, bf16[512,256]{1,0:T(8,128)(2,1)S(1)}, u32[]{:S(2)}) copy-start(bf16[512,256]{1,0:T(8,128)(2,1)S(1)} %collective-permute-done.2.rest_0_.rest_1_) | copy-start | bytes 786436
  26.6 14.1 %copy-start.4 = (bf16[512,256]{1,0:T(8,128)(2,1)}, bf16[512,256]{1,0:T(8,128)(2,1)S(1)}, u32[]{:S(2)}) copy-start(bf16[512,256]{1,0:T(8,128)(2,1)S(1)} %collective-permute-done.3.rest_3_.rest_4_) | copy-start | bytes 786436
  26.6 14.1 %copy-start.5 = (bf16[512,256]{1,0:T(8,128)(2,1)}, bf16[512,256]{1,0:T(8,128)(2,1)S(1)}, u32[]{:S(2)}) copy-start(bf16[512,256]{1,0:T(8,128)(2,1)S(1)} %collective-permute-done.4.rest_4_.rest_5_) | copy-start | bytes 786436
  26.6 4.4 %collective-permute-start.5 = (bf16[512,256]{1,0:T(8,128)(2,1)S(1)}, bf16[512,256]{1,0:T(8,128)(2,1)S(1)}, u32[]{:S(2)}, u32[]{:S(2)}) collective-permute-start(bf16[512,256]{1,0:T(8,128)(2,1)S(1)} %collective-permute-done.2.rest_0_.rest_1_), channel_id=1, source_target_pairs={{0,1},{1,0},{2,3},{3,2},{4,5},{5,4},{6,7},{7,6},{8,9},{9,8},{10,11... | collective-permute-start | bytes 786440 | tf_op jit(solution)/shard_map/ppermute | solution.py:509
  27.2 3.9 %collective-permute-start.6 = (bf16[512,256]{1,0:T(8,128)(2,1)S(1)}, bf16[512,256]{1,0:T(8,128)(2,1)S(1)}, u32[]{:S(2)}, u32[]{:S(2)}) collective-permute-start(bf16[512,256]{1,0:T(8,128)(2,1)S(1)} %collective-permute-done.rest_1_.rest_2_), channel_id=1, source_target_pairs={{0,1},{1,0},{2,3},{3,2},{4,5},{5,4},{6,7},{7,6},{8,9},{9,8},{10,11... | collective-permute-start | bytes 786440 | tf_op jit(solution)/shard_map/ppermute | solution.py:509
  27.3 12.4 %collective-permute-start.9 = (bf16[512,256]{1,0:T(8,128)(2,1)S(1)}, bf16[512,256]{1,0:T(8,128)(2,1)S(1)}, u32[]{:S(2)}, u32[]{:S(2)}) collective-permute-start(bf16[512,256]{1,0:T(8,128)(2,1)S(1)} %collective-permute-done.2.rest_0_.rest_1_), channel_id=1, source_target_pairs={{0,2},{1,3},{2,4},{3,5},{4,6},{5,7},{6,0},{7,1},{8,10},{9,11},{10,... | collective-permute-start | bytes 786440 | tf_op jit(solution)/shard_map/ppermute | solution.py:509
  28.2 11.6 %collective-permute-start.10 = (bf16[512,256]{1,0:T(8,128)(2,1)S(1)}, bf16[512,256]{1,0:T(8,128)(2,1)S(1)}, u32[]{:S(2)}, u32[]{:S(2)}) collective-permute-start(bf16[512,256]{1,0:T(8,128)(2,1)S(1)} %collective-permute-done.2.rest_0_.rest_1_), channel_id=1, source_target_pairs={{0,6},{1,7},{2,0},{3,1},{4,2},{5,3},{6,4},{7,5},{8,14},{9,15},{10,... | collective-permute-start | bytes 786440 | tf_op jit(solution)/shard_map/ppermute | solution.py:509
  30.6 9.8 %collective-permute-start.11 = (bf16[512,256]{1,0:T(8,128)(2,1)S(1)}, bf16[512,256]{1,0:T(8,128)(2,1)S(1)}, u32[]{:S(2)}, u32[]{:S(2)}) collective-permute-start(bf16[512,256]{1,0:T(8,128)(2,1)S(1)} %collective-permute-done.3.rest_3_.rest_4_), channel_id=1, source_target_pairs={{0,8},{1,9},{2,10},{3,11},{4,12},{5,13},{6,14},{7,15},{8,0},{9,1},... | collective-permute-start | bytes 786440 | tf_op jit(solution)/shard_map/ppermute | solution.py:509
  31.1 9.6 %collective-permute-start.7 = (bf16[512,256]{1,0:T(8,128)(2,1)S(1)}, bf16[512,256]{1,0:T(8,128)(2,1)S(1)}, u32[]{:S(2)}, u32[]{:S(2)}) collective-permute-start(bf16[512,256]{1,0:T(8,128)(2,1)S(1)} %collective-permute-done.1.rest_2_.rest_3_), channel_id=1, source_target_pairs={{0,1},{1,0},{2,3},{3,2},{4,5},{5,4},{6,7},{7,6},{8,9},{9,8},{10,11... | collective-permute-start | bytes 786440 | tf_op jit(solution)/shard_map/ppermute | solution.py:509
  31.1 9.5 %collective-permute-start.8 = (bf16[512,256]{1,0:T(8,128)(2,1)S(1)}, bf16[512,256]{1,0:T(8,128)(2,1)}, u32[]{:S(2)}, u32[]{:S(2)}) collective-permute-start(bf16[512,256]{1,0:T(8,128)(2,1)S(1)} %collective-permute-done.3.rest_3_.rest_4_), channel_id=1, source_target_pairs={{0,1},{1,0},{2,3},{3,2},{4,5},{5,4},{6,7},{7,6},{8,9},{9,8},{10,11... | collective-permute-start | bytes 786440 | tf_op jit(solution)/shard_map/ppermute | solution.py:509
  31.6 30.8 %all-to-all-start = ((bf16[128,2,1152]{2,1,0:T(2,128)(2,1)}), bf16[128,2,1152]{2,1,0:T(2,128)(2,1)S(1)}, u32[]{:S(2)}, u32[]{:S(2)}) async-start(bf16[128,2,1152]{2,1,0:T(2,128)(2,1)} %pool_tiles.1), calls=%async_computation | async-start | bytes 1179648 | tf_op jit(solution)/shard_map/all_to_all | solution.py:553
  39.8 21.2 %copy-start.8 = (bf16[512,256]{1,0:T(8,128)(2,1)}, bf16[512,256]{1,0:T(8,128)(2,1)S(1)}, u32[]{:S(2)}) copy-start(bf16[512,256]{1,0:T(8,128)(2,1)S(1)} %collective-permute-done.9.rest_10_.rest_16_) | copy-start | bytes 786436
  39.8 21.2 %collective-permute-start.12 = (bf16[512,256]{1,0:T(8,128)(2,1)S(1)}, bf16[512,256]{1,0:T(8,128)(2,1)S(1)}, u32[]{:S(2)}, u32[]{:S(2)}) collective-permute-start(bf16[512,256]{1,0:T(8,128)(2,1)S(1)} %collective-permute-done.9.rest_10_.rest_16_), channel_id=1, source_target_pairs={{0,1},{1,0},{2,3},{3,2},{4,5},{5,4},{6,7},{7,6},{8,9},{9,8},{10,11... | collective-permute-start | bytes 786440 | tf_op jit(solution)/shard_map/ppermute | solution.py:509
  39.9 21.1 %copy-start.9 = (bf16[512,256]{1,0:T(8,128)(2,1)}, bf16[512,256]{1,0:T(8,128)(2,1)S(1)}, u32[]{:S(2)}) copy-start(bf16[512,256]{1,0:T(8,128)(2,1)S(1)} %collective-permute-done.10.rest_11_.rest_17_) | copy-start | bytes 786436
  39.9 21.2 %collective-permute-start.13 = (bf16[512,256]{1,0:T(8,128)(2,1)S(1)}, bf16[512,256]{1,0:T(8,128)(2,1)S(1)}, u32[]{:S(2)}, u32[]{:S(2)}) collective-permute-start(bf16[512,256]{1,0:T(8,128)(2,1)S(1)} %collective-permute-done.10.rest_11_.rest_17_), channel_id=1, source_target_pairs={{0,1},{1,0},{2,3},{3,2},{4,5},{5,4},{6,7},{7,6},{8,9},{9,8},{10,11... | collective-permute-start | bytes 786440 | tf_op jit(solution)/shard_map/ppermute | solution.py:509
  40.4 20.6 %copy-start.10 = (bf16[512,256]{1,0:T(8,128)(2,1)}, bf16[512,256]{1,0:T(8,128)(2,1)S(1)}, u32[]{:S(2)}) copy-start(bf16[512,256]{1,0:T(8,128)(2,1)S(1)} %collective-permute-done.11.rest_12_.rest_18_) | copy-start | bytes 786436
  40.4 22.1 %collective-permute-start.14 = (bf16[512,256]{1,0:T(8,128)(2,1)S(1)}, bf16[512,256]{1,0:T(8,128)(2,1)}, u32[]{:S(2)}, u32[]{:S(2)}) collective-permute-start(bf16[512,256]{1,0:T(8,128)(2,1)S(1)} %collective-permute-done.11.rest_12_.rest_18_), channel_id=1, source_target_pairs={{0,1},{1,0},{2,3},{3,2},{4,5},{5,4},{6,7},{7,6},{8,9},{9,8},{10,11... | collective-permute-start | bytes 786440 | tf_op jit(solution)/shard_map/ppermute | solution.py:509
  (6 other events, 22.2 us)

commit v5 on v4

--- a/solution.py
+++ b/solution.py
@@ -94,22 +94,22 @@
     cnt_s, obs_ref, cnt_ref, own_ref, cell_ref, w_ref, pay_ref, live_ref, acc_ref, act_ref, member_ref
 ):
     square = (TILES, TILES)
-    source = iota(square, 1) // F_OBS
-    row = iota(square, 0)
+    lanes = [(iota(square, 1) // F_OBS == k).astype(F32).astype(BF) for k in range(4)]
+    column = iota(square, 1)
 
     def put(step, first):
-        for u in range(2):
-            four = step * 2 + u
-            rows = obs_ref[pl.ds(pl.multiple_of(four * TILES, TILES), TILES), :].T
-            for k in range(4):
-                count = cnt_s[four * 4 + k]
-                live_ref[pl.ds(pl.multiple_of(first, 32), TROWS), :] = jnp.where(
-                    (source == k) & (row < count), rows, jnp.zeros_like(rows)
-                )
+        for u in range(4):
+            four = step * 4 + u
+            counts = [cnt_s[four * 4 + k] for k in range(4)]
+            limit = jnp.concatenate([jnp.full((F_OBS, TROWS), c, I32) for c in counts], axis=0)
+            rows = obs_ref[pl.ds(pl.multiple_of(four * TILES, TILES), TILES), :]
+            rows = jnp.where(column < limit, rows, jnp.zeros_like(rows)).T
+            for k, count in enumerate(counts):
+                live_ref[pl.ds(pl.multiple_of(first, 32), TROWS), :] = rows * lanes[k]
                 first = first + ((count + 31) // 32) * 32
         return first
 
-    total = lax.fori_loop(0, TILES // 8, put, jnp.int32(0))
+    total = lax.fori_loop(0, TILES // 16, put, jnp.int32(0))
     for i in range(0, 2 * BLOCK, 128):
         live_ref[pl.ds(pl.multiple_of(total + i, 32), 128), :] = jnp.zeros(square, BF)
 

time: 199 us -> 198 us (level)
  no operation moved by 1% of the time
where the time goes in v5:
time: 198 us; the launch traced here: 196 us
  Pallas kernels  172 us (87%)
  starting transfers between devices  20.8 us (11%)
  local copies, waits for them, and re-layouts  2.89 us (1%)
    pallas_call x1, Pallas kernels, last_call(): pl.pallas_call(functools.partial(last_kernel, moves), out_shape=jax.Shape...  135 us
    pallas_call x1, Pallas kernels, first_call(): pl.pallas_call(functools.partial(first_kernel, moves), out_shape=(jax.Sha...  19.6 us
    pallas_call x1, Pallas kernels, pool_call(): pl.pallas_call(pool_kernel, out_shape=jax.ShapeDtypeStruct((SLOTS // 2, 2...  14.7 us
    ppermute x15, starting transfers between devices, send(): return lax.ppermute(block, 'lon', pairs)  12.7 us
    all_to_all x1, starting transfers between devices, shards(): lax.all_to_all(pay, ('lat', 'lon'), split_axis=0, concat_axis=0, tiled=True)  8.13 us
  transfers between devices with their start and end apart: 16, of which 0 were waited for; matrix products, arithmetic and copies ran while one was open for 0% of the time, Pallas kernels for 18%

profile of v5, /device:TPU:0, one launch (start us, length us, event | category | flops | bytes accessed | tf_op | source)
XLA Modules:
  0.0 195.9 jit_solution(10724483860078195693)
XLA Ops:
  0.0 2.7 %norm_keys_values.1 = (bf16[256,1024]{1,0:T(8,128)(2,1)}, bf16[512,256]{1,0:T(8,128)(2,1)}) custom-call(bf16[256,1024]{1,0:T(8,128)(2,1)} %tok_ref.3, f32[1,1024]{1,0:T(1,128)} %bitcast.9, bf16[1024,256]{1,0:T(8,128)(2,1)} %wk_ref.1, bf16[1024,256]{1,0:T(8,128)(2,1)} %wv_ref.1), custom_call_target="tpu_custom_call" | custom-call | flops 3000000000 | bytes 3000000 | tf_op jit(solution)/shard_map/norm_keys_values/pallas_call | solution.py:74
  2.7 2.0 %collective-permute-start = (bf16[512,256]{1,0:T(8,128)(2,1)}, bf16[512,256]{1,0:T(8,128)(2,1)S(1)}, u32[]{:S(2)}, u32[]{:S(2)}) collective-permute-start(bf16[512,256]{1,0:T(8,128)(2,1)} %get-tuple-element.17.kv_ref.rest_0_), channel_id=1, source_target_pairs={{0,2},{1,3},{2,4},{3,5},{4,6},{5,7},{6,0},{7,1},{8,10},{9,11},{10,... | collective-permute-start | bytes 786440 | tf_op jit(solution)/shard_map/ppermute | solution.py:509
  4.7 2.1 %collective-permute-start.1 = (bf16[512,256]{1,0:T(8,128)(2,1)}, bf16[512,256]{1,0:T(8,128)(2,1)S(1)}, u32[]{:S(2)}, u32[]{:S(2)}) collective-permute-start(bf16[512,256]{1,0:T(8,128)(2,1)} %get-tuple-element.17.kv_ref.rest_0_), channel_id=1, source_target_pairs={{0,6},{1,7},{2,0},{3,1},{4,2},{5,3},{6,4},{7,5},{8,14},{9,15},{10,... | collective-permute-start | bytes 786440 | tf_op jit(solution)/shard_map/ppermute | solution.py:509
  6.8 1.5 collective-permute-start.2
  8.3 1.9 collective-permute-start.3
  10.2 0.0 collective-permute-start.4
  10.2 14.7 %pool_tiles.1 = bf16[128,2,1152]{2,1,0:T(2,128)(2,1)} custom-call(s32[128]{0:T(128)} %cnt_s.1, bf16[4096,128]{1,0:T(8,128)(2,1)} %bitcast.8, s32[1,128]{1,0:T(1,128)} %bitcast.11, s32[1,128]{1,0:T(1,128)} %bitcast.12, s32[1,128]{1,0:T(1,128)} %bitcast.13, bf16[32,1024]{1,0:T(8,128)(2,1)} %w_ref.1), custom_call_target="tpu_custom_call" | custom-call | flops 15000000512 | bytes 15000000 | tf_op jit(solution)/shard_map/pool_tiles/pallas_call | solution.py:163
  24.9 0.0 collective-permute-done.rest_1_.rest_2_
  25.0 0.1 collective-permute-start.5
  25.1 0.5 collective-permute-start.6
  25.6 1.1 collective-permute-start.9
  26.7 2.1 %collective-permute-start.10 = (bf16[512,256]{1,0:T(8,128)(2,1)S(1)}, bf16[512,256]{1,0:T(8,128)(2,1)S(1)}, u32[]{:S(2)}, u32[]{:S(2)}) collective-permute-start(bf16[512,256]{1,0:T(8,128)(2,1)S(1)} %collective-permute-done.2.rest_0_.rest_1_), channel_id=1, source_target_pairs={{0,6},{1,7},{2,0},{3,1},{4,2},{5,3},{6,4},{7,5},{8,14},{9,15},{10,... | collective-permute-start | bytes 786440 | tf_op jit(solution)/shard_map/ppermute | solution.py:509
  28.8 0.1 collective-permute-start.7
  28.9 0.5 collective-permute-start.8
  29.4 8.1 %all-to-all-start = ((bf16[128,2,1152]{2,1,0:T(2,128)(2,1)}), bf16[128,2,1152]{2,1,0:T(2,128)(2,1)S(1)}, u32[]{:S(2)}, u32[]{:S(2)}) async-start(bf16[128,2,1152]{2,1,0:T(2,128)(2,1)} %pool_tiles.1), calls=%async_computation | async-start | bytes 1179648 | tf_op jit(solution)/shard_map/all_to_all | solution.py:553
  37.6 0.1 collective-permute-start.12
  37.7 0.5 collective-permute-start.13
  38.2 0.3 collective-permute-start.14
  38.5 0.6 copy-done.11
  39.2 19.6 %queries_near_rows.1 = (bf16[16,128,256]{2,1,0:T(8,128)(2,1)}, f32[16,80,256]{2,1,0:T(8,128)}) custom-call(f32[16]{0:T(128)} %rate_s.3, bf16[256,1024]{1,0:T(8,128)(2,1)} %get-tuple-element.18.normed_ref, bf16[1024,1024]{1,0:T(8,128)(2,1)} %wq_ref.1, bf16[512,256]{1,0:T(8,128)(2,1)} %get-tuple-element.17.kv_ref.rest_0_, bf16[512,256]{1,0:T(8,128)(2,1)} %copy-done.3, ...), custom_call_target="tpu_custom_call" | custom-call | flops 17999998976 | bytes 18000000 | tf_op jit(solution)/shard_map/queries_near_rows/pallas_call | solution.py:295
  58.9 0.7 copy-done.12
  59.5 0.7 copy-done.13
  60.3 0.8 copy-done
  61.1 134.7 %late_rows_project_update_mlp.1 = bf16[256,1024]{1,0:T(8,128)(2,1)} custom-call(f32[16]{0:T(128)} %rate_s.3, bf16[256,1024]{1,0:T(8,128)(2,1)} %tok_ref.3, f32[1,1024]{1,0:T(1,128)} %bitcast.10, bf16[16,128,256]{2,1,0:T(8,128)(2,1)} %get-tuple-element.24.q_ref, f32[16,80,256]{2,1,0:T(8,128)} %get-tuple-element.25.part_ref, bf16[128,2,1152]{2,1,0:T(2,128)(2,1)} %copy-done, ...), custom_call_target="tpu_custom_call" | custom-call | flops 16999999488 | bytes 17000000 | tf_op jit(solution)/shard_map/late_rows_project_update_mlp/pallas_call | solution.py:457
  (40 shorter events, 0.1 us)
Async XLA Ops:
  2.7 22.2 %collective-permute-start = (bf16[512,256]{1,0:T(8,128)(2,1)}, bf16[512,256]{1,0:T(8,128)(2,1)S(1)}, u32[]{:S(2)}, u32[]{:S(2)}) collective-permute-start(bf16[512,256]{1,0:T(8,128)(2,1)} %get-tuple-element.17.kv_ref.rest_0_), channel_id=1, source_target_pairs={{0,2},{1,3},{2,4},{3,5},{4,6},{5,7},{6,0},{7,1},{8,10},{9,11},{10,... | collective-permute-start | bytes 786440 | tf_op jit(solution)/shard_map/ppermute | solution.py:509
  4.7 20.2 %collective-permute-start.1 = (bf16[512,256]{1,0:T(8,128)(2,1)}, bf16[512,256]{1,0:T(8,128)(2,1)S(1)}, u32[]{:S(2)}, u32[]{:S(2)}) collective-permute-start(bf16[512,256]{1,0:T(8,128)(2,1)} %get-tuple-element.17.kv_ref.rest_0_), channel_id=1, source_target_pairs={{0,6},{1,7},{2,0},{3,1},{4,2},{5,3},{6,4},{7,5},{8,14},{9,15},{10,... | collective-permute-start | bytes 786440 | tf_op jit(solution)/shard_map/ppermute | solution.py:509
  6.8 18.1 %collective-permute-start.2 = (bf16[512,256]{1,0:T(8,128)(2,1)}, bf16[512,256]{1,0:T(8,128)(2,1)S(1)}, u32[]{:S(2)}, u32[]{:S(2)}) collective-permute-start(bf16[512,256]{1,0:T(8,128)(2,1)} %get-tuple-element.17.kv_ref.rest_0_), channel_id=1, source_target_pairs={{0,8},{1,9},{2,10},{3,11},{4,12},{5,13},{6,14},{7,15},{8,0},{9,1},... | collective-permute-start | bytes 786440 | tf_op jit(solution)/shard_map/ppermute | solution.py:509
  8.3 16.6 %collective-permute-start.3 = (bf16[512,256]{1,0:T(8,128)(2,1)}, bf16[512,256]{1,0:T(8,128)(2,1)S(1)}, u32[]{:S(2)}, u32[]{:S(2)}) collective-permute-start(bf16[512,256]{1,0:T(8,128)(2,1)} %get-tuple-element.17.kv_ref.rest_0_), channel_id=1, source_target_pairs={{0,4},{1,5},{2,6},{3,7},{4,0},{5,1},{6,2},{7,3},{8,12},{9,13},{10,... | collective-permute-start | bytes 786440 | tf_op jit(solution)/shard_map/ppermute | solution.py:509
  10.2 14.8 %collective-permute-start.4 = (bf16[512,256]{1,0:T(8,128)(2,1)}, bf16[512,256]{1,0:T(8,128)(2,1)S(1)}, u32[]{:S(2)}, u32[]{:S(2)}) collective-permute-start(bf16[512,256]{1,0:T(8,128)(2,1)} %get-tuple-element.17.kv_ref.rest_0_), channel_id=1, source_target_pairs={{0,1},{1,0},{2,3},{3,2},{4,5},{5,4},{6,7},{7,6},{8,9},{9,8},{10,11... | collective-permute-start | bytes 786440 | tf_op jit(solution)/shard_map/ppermute | solution.py:509
  24.9 13.6 %copy-start.1 = (bf16[512,256]{1,0:T(8,128)(2,1)}, bf16[512,256]{1,0:T(8,128)(2,1)S(1)}, u32[]{:S(2)}) copy-start(bf16[512,256]{1,0:T(8,128)(2,1)S(1)} %collective-permute-done.rest_1_.rest_2_) | copy-start | bytes 786436
  24.9 13.6 %copy-start.2 = (bf16[512,256]{1,0:T(8,128)(2,1)}, bf16[512,256]{1,0:T(8,128)(2,1)S(1)}, u32[]{:S(2)}) copy-start(bf16[512,256]{1,0:T(8,128)(2,1)S(1)} %collective-permute-done.1.rest_2_.rest_3_) | copy-start | bytes 786436
  24.9 13.6 %copy-start.3 = (bf16[512,256]{1,0:T(8,128)(2,1)}, bf16[512,256]{1,0:T(8,128)(2,1)S(1)}, u32[]{:S(2)}) copy-start(bf16[512,256]{1,0:T(8,128)(2,1)S(1)} %collective-permute-done.2.rest_0_.rest_1_) | copy-start | bytes 786436
  25.0 13.5 %copy-start.4 = (bf16[512,256]{1,0:T(8,128)(2,1)}, bf16[512,256]{1,0:T(8,128)(2,1)S(1)}, u32[]{:S(2)}) copy-start(bf16[512,256]{1,0:T(8,128)(2,1)S(1)} %collective-permute-done.3.rest_3_.rest_4_) | copy-start | bytes 786436
  25.0 13.5 %copy-start.5 = (bf16[512,256]{1,0:T(8,128)(2,1)}, bf16[512,256]{1,0:T(8,128)(2,1)S(1)}, u32[]{:S(2)}) copy-start(bf16[512,256]{1,0:T(8,128)(2,1)S(1)} %collective-permute-done.4.rest_4_.rest_5_) | copy-start | bytes 786436
  25.0 3.8 %collective-permute-start.5 = (bf16[512,256]{1,0:T(8,128)(2,1)S(1)}, bf16[512,256]{1,0:T(8,128)(2,1)S(1)}, u32[]{:S(2)}, u32[]{:S(2)}) collective-permute-start(bf16[512,256]{1,0:T(8,128)(2,1)S(1)} %collective-permute-done.2.rest_0_.rest_1_), channel_id=1, source_target_pairs={{0,1},{1,0},{2,3},{3,2},{4,5},{5,4},{6,7},{7,6},{8,9},{9,8},{10,11... | collective-permute-start | bytes 786440 | tf_op jit(solution)/shard_map/ppermute | solution.py:509
  25.1 3.8 %collective-permute-start.6 = (bf16[512,256]{1,0:T(8,128)(2,1)S(1)}, bf16[512,256]{1,0:T(8,128)(2,1)S(1)}, u32[]{:S(2)}, u32[]{:S(2)}) collective-permute-start(bf16[512,256]{1,0:T(8,128)(2,1)S(1)} %collective-permute-done.rest_1_.rest_2_), channel_id=1, source_target_pairs={{0,1},{1,0},{2,3},{3,2},{4,5},{5,4},{6,7},{7,6},{8,9},{9,8},{10,11... | collective-permute-start | bytes 786440 | tf_op jit(solution)/shard_map/ppermute | solution.py:509
  25.6 12.0 %collective-permute-start.9 = (bf16[512,256]{1,0:T(8,128)(2,1)S(1)}, bf16[512,256]{1,0:T(8,128)(2,1)S(1)}, u32[]{:S(2)}, u32[]{:S(2)}) collective-permute-start(bf16[512,256]{1,0:T(8,128)(2,1)S(1)} %collective-permute-done.2.rest_0_.rest_1_), channel_id=1, source_target_pairs={{0,2},{1,3},{2,4},{3,5},{4,6},{5,7},{6,0},{7,1},{8,10},{9,11},{10,... | collective-permute-start | bytes 786440 | tf_op jit(solution)/shard_map/ppermute | solution.py:509
  26.7 11.0 %collective-permute-start.10 = (bf16[512,256]{1,0:T(8,128)(2,1)S(1)}, bf16[512,256]{1,0:T(8,128)(2,1)S(1)}, u32[]{:S(2)}, u32[]{:S(2)}) collective-permute-start(bf16[512,256]{1,0:T(8,128)(2,1)S(1)} %collective-permute-done.2.rest_0_.rest_1_), channel_id=1, source_target_pairs={{0,6},{1,7},{2,0},{3,1},{4,2},{5,3},{6,4},{7,5},{8,14},{9,15},{10,... | collective-permute-start | bytes 786440 | tf_op jit(solution)/shard_map/ppermute | solution.py:509
  28.8 9.4 %collective-permute-start.11 = (bf16[512,256]{1,0:T(8,128)(2,1)S(1)}, bf16[512,256]{1,0:T(8,128)(2,1)S(1)}, u32[]{:S(2)}, u32[]{:S(2)}) collective-permute-start(bf16[512,256]{1,0:T(8,128)(2,1)S(1)} %collective-permute-done.3.rest_3_.rest_4_), channel_id=1, source_target_pairs={{0,8},{1,9},{2,10},{3,11},{4,12},{5,13},{6,14},{7,15},{8,0},{9,1},... | collective-permute-start | bytes 786440 | tf_op jit(solution)/shard_map/ppermute | solution.py:509
  28.8 9.6 %collective-permute-start.7 = (bf16[512,256]{1,0:T(8,128)(2,1)S(1)}, bf16[512,256]{1,0:T(8,128)(2,1)S(1)}, u32[]{:S(2)}, u32[]{:S(2)}) collective-permute-start(bf16[512,256]{1,0:T(8,128)(2,1)S(1)} %collective-permute-done.1.rest_2_.rest_3_), channel_id=1, source_target_pairs={{0,1},{1,0},{2,3},{3,2},{4,5},{5,4},{6,7},{7,6},{8,9},{9,8},{10,11... | collective-permute-start | bytes 786440 | tf_op jit(solution)/shard_map/ppermute | solution.py:509
  28.9 9.5 %collective-permute-start.8 = (bf16[512,256]{1,0:T(8,128)(2,1)S(1)}, bf16[512,256]{1,0:T(8,128)(2,1)}, u32[]{:S(2)}, u32[]{:S(2)}) collective-permute-start(bf16[512,256]{1,0:T(8,128)(2,1)S(1)} %collective-permute-done.3.rest_3_.rest_4_), channel_id=1, source_target_pairs={{0,1},{1,0},{2,3},{3,2},{4,5},{5,4},{6,7},{7,6},{8,9},{9,8},{10,11... | collective-permute-start | bytes 786440 | tf_op jit(solution)/shard_map/ppermute | solution.py:509
  29.4 30.8 %all-to-all-start = ((bf16[128,2,1152]{2,1,0:T(2,128)(2,1)}), bf16[128,2,1152]{2,1,0:T(2,128)(2,1)S(1)}, u32[]{:S(2)}, u32[]{:S(2)}) async-start(bf16[128,2,1152]{2,1,0:T(2,128)(2,1)} %pool_tiles.1), calls=%async_computation | async-start | bytes 1179648 | tf_op jit(solution)/shard_map/all_to_all | solution.py:553
  37.6 21.2 %copy-start.8 = (bf16[512,256]{1,0:T(8,128)(2,1)}, bf16[512,256]{1,0:T(8,128)(2,1)S(1)}, u32[]{:S(2)}) copy-start(bf16[512,256]{1,0:T(8,128)(2,1)S(1)} %collective-permute-done.9.rest_10_.rest_16_) | copy-start | bytes 786436
  37.6 21.3 %collective-permute-start.12 = (bf16[512,256]{1,0:T(8,128)(2,1)S(1)}, bf16[512,256]{1,0:T(8,128)(2,1)S(1)}, u32[]{:S(2)}, u32[]{:S(2)}) collective-permute-start(bf16[512,256]{1,0:T(8,128)(2,1)S(1)} %collective-permute-done.9.rest_10_.rest_16_), channel_id=1, source_target_pairs={{0,1},{1,0},{2,3},{3,2},{4,5},{5,4},{6,7},{7,6},{8,9},{9,8},{10,11... | collective-permute-start | bytes 786440 | tf_op jit(solution)/shard_map/ppermute | solution.py:509
  37.7 21.1 %copy-start.9 = (bf16[512,256]{1,0:T(8,128)(2,1)}, bf16[512,256]{1,0:T(8,128)(2,1)S(1)}, u32[]{:S(2)}) copy-start(bf16[512,256]{1,0:T(8,128)(2,1)S(1)} %collective-permute-done.10.rest_11_.rest_17_) | copy-start | bytes 786436
  37.7 21.2 %collective-permute-start.13 = (bf16[512,256]{1,0:T(8,128)(2,1)S(1)}, bf16[512,256]{1,0:T(8,128)(2,1)S(1)}, u32[]{:S(2)}, u32[]{:S(2)}) collective-permute-start(bf16[512,256]{1,0:T(8,128)(2,1)S(1)} %collective-permute-done.10.rest_11_.rest_17_), channel_id=1, source_target_pairs={{0,1},{1,0},{2,3},{3,2},{4,5},{5,4},{6,7},{7,6},{8,9},{9,8},{10,11... | collective-permute-start | bytes 786440 | tf_op jit(solution)/shard_map/ppermute | solution.py:509
  38.2 20.6 %copy-start.10 = (bf16[512,256]{1,0:T(8,128)(2,1)}, bf16[512,256]{1,0:T(8,128)(2,1)S(1)}, u32[]{:S(2)}) copy-start(bf16[512,256]{1,0:T(8,128)(2,1)S(1)} %collective-permute-done.11.rest_12_.rest_18_) | copy-start | bytes 786436
  38.2 22.1 %collective-permute-start.14 = (bf16[512,256]{1,0:T(8,128)(2,1)S(1)}, bf16[512,256]{1,0:T(8,128)(2,1)}, u32[]{:S(2)}, u32[]{:S(2)}) collective-permute-start(bf16[512,256]{1,0:T(8,128)(2,1)S(1)} %collective-permute-done.11.rest_12_.rest_18_), channel_id=1, source_target_pairs={{0,1},{1,0},{2,3},{3,2},{4,5},{5,4},{6,7},{7,6},{8,9},{9,8},{10,11... | collective-permute-start | bytes 786440 | tf_op jit(solution)/shard_map/ppermute | solution.py:509
  (6 other events, 22.3 us)

commit v6 on v5

--- a/solution.py
+++ b/solution.py
@@ -350,7 +350,7 @@
 
 STEP = 2048
 STEPS = FF // STEP
-LATE = (3, 3)
+LATE = (4, 2)
 
 
 def last_kernel(

time: 198 us -> 197 us (level)
  no operation moved by 1% of the time
where the time goes in v6:
time: 197 us; the launch traced here: 195 us
  Pallas kernels  171 us (87%)
  starting transfers between devices  20.9 us (11%)
  local copies, waits for them, and re-layouts  2.89 us (1%)
    pallas_call x1, Pallas kernels, last_call(): pl.pallas_call(functools.partial(last_kernel, moves), out_shape=jax.Shape...  134 us
    pallas_call x1, Pallas kernels, first_call(): pl.pallas_call(functools.partial(first_kernel, moves), out_shape=(jax.Sha...  19.6 us
    pallas_call x1, Pallas kernels, pool_call(): pl.pallas_call(pool_kernel, out_shape=jax.ShapeDtypeStruct((SLOTS // 2, 2...  14.7 us
    ppermute x15, starting transfers between devices, send(): return lax.ppermute(block, 'lon', pairs)  13.2 us
    all_to_all x1, starting transfers between devices, shards(): lax.all_to_all(pay, ('lat', 'lon'), split_axis=0, concat_axis=0, tiled=True)  7.68 us
  transfers between devices with their start and end apart: 16, of which 0 were waited for; matrix products, arithmetic and copies ran while one was open for 0% of the time, Pallas kernels for 18%

profile of v6, /device:TPU:0, one launch (start us, length us, event | category | flops | bytes accessed | tf_op | source)
XLA Modules:
  0.0 195.1 jit_solution(12757725920202205188)
XLA Ops:
  0.0 2.7 %norm_keys_values.1 = (bf16[256,1024]{1,0:T(8,128)(2,1)}, bf16[512,256]{1,0:T(8,128)(2,1)}) custom-call(bf16[256,1024]{1,0:T(8,128)(2,1)} %tok_ref.3, f32[1,1024]{1,0:T(1,128)} %bitcast.9, bf16[1024,256]{1,0:T(8,128)(2,1)} %wk_ref.1, bf16[1024,256]{1,0:T(8,128)(2,1)} %wv_ref.1), custom_call_target="tpu_custom_call" | custom-call | flops 3000000000 | bytes 3000000 | tf_op jit(solution)/shard_map/norm_keys_values/pallas_call | solution.py:74
  2.7 2.0 %collective-permute-start = (bf16[512,256]{1,0:T(8,128)(2,1)}, bf16[512,256]{1,0:T(8,128)(2,1)S(1)}, u32[]{:S(2)}, u32[]{:S(2)}) collective-permute-start(bf16[512,256]{1,0:T(8,128)(2,1)} %get-tuple-element.17.kv_ref.rest_0_), channel_id=1, source_target_pairs={{0,2},{1,3},{2,4},{3,5},{4,6},{5,7},{6,0},{7,1},{8,10},{9,11},{10,... | collective-permute-start | bytes 786440 | tf_op jit(solution)/shard_map/ppermute | solution.py:509
  4.7 2.1 %collective-permute-start.1 = (bf16[512,256]{1,0:T(8,128)(2,1)}, bf16[512,256]{1,0:T(8,128)(2,1)S(1)}, u32[]{:S(2)}, u32[]{:S(2)}) collective-permute-start(bf16[512,256]{1,0:T(8,128)(2,1)} %get-tuple-element.17.kv_ref.rest_0_), channel_id=1, source_target_pairs={{0,6},{1,7},{2,0},{3,1},{4,2},{5,3},{6,4},{7,5},{8,14},{9,15},{10,... | collective-permute-start | bytes 786440 | tf_op jit(solution)/shard_map/ppermute | solution.py:509
  6.8 1.5 collective-permute-start.2
  8.3 1.9 collective-permute-start.3
  10.2 0.0 collective-permute-start.4
  10.2 14.7 %pool_tiles.1 = bf16[128,2,1152]{2,1,0:T(2,128)(2,1)} custom-call(s32[128]{0:T(128)} %cnt_s.1, bf16[4096,128]{1,0:T(8,128)(2,1)} %bitcast.8, s32[1,128]{1,0:T(1,128)} %bitcast.11, s32[1,128]{1,0:T(1,128)} %bitcast.12, s32[1,128]{1,0:T(1,128)} %bitcast.13, bf16[32,1024]{1,0:T(8,128)(2,1)} %w_ref.1), custom_call_target="tpu_custom_call" | custom-call | flops 15000000512 | bytes 15000000 | tf_op jit(solution)/shard_map/pool_tiles/pallas_call | solution.py:163
  24.9 0.0 collective-permute-done.rest_1_.rest_2_
  25.0 0.1 collective-permute-start.5
  25.1 0.5 collective-permute-start.6
  25.6 1.1 collective-permute-start.9
  26.7 2.1 %collective-permute-start.10 = (bf16[512,256]{1,0:T(8,128)(2,1)S(1)}, bf16[512,256]{1,0:T(8,128)(2,1)S(1)}, u32[]{:S(2)}, u32[]{:S(2)}) collective-permute-start(bf16[512,256]{1,0:T(8,128)(2,1)S(1)} %collective-permute-done.2.rest_0_.rest_1_), channel_id=1, source_target_pairs={{0,6},{1,7},{2,0},{3,1},{4,2},{5,3},{6,4},{7,5},{8,14},{9,15},{10,... | collective-permute-start | bytes 786440 | tf_op jit(solution)/shard_map/ppermute | solution.py:509
  28.8 0.5 collective-permute-start.11
  29.4 0.5 collective-permute-start.8
  29.9 7.7 %all-to-all-start = ((bf16[128,2,1152]{2,1,0:T(2,128)(2,1)}), bf16[128,2,1152]{2,1,0:T(2,128)(2,1)S(1)}, u32[]{:S(2)}, u32[]{:S(2)}) async-start(bf16[128,2,1152]{2,1,0:T(2,128)(2,1)} %pool_tiles.1), calls=%async_computation | async-start | bytes 1179648 | tf_op jit(solution)/shard_map/all_to_all | solution.py:553
  37.6 0.1 collective-permute-start.12
  37.7 0.5 collective-permute-start.13
  38.2 0.3 collective-permute-start.14
  38.5 0.6 copy-done.11
  39.2 19.6 %queries_near_rows.1 = (bf16[16,128,256]{2,1,0:T(8,128)(2,1)}, f32[16,80,256]{2,1,0:T(8,128)}) custom-call(f32[16]{0:T(128)} %rate_s.3, bf16[256,1024]{1,0:T(8,128)(2,1)} %get-tuple-element.18.normed_ref, bf16[1024,1024]{1,0:T(8,128)(2,1)} %wq_ref.1, bf16[512,256]{1,0:T(8,128)(2,1)} %get-tuple-element.17.kv_ref.rest_0_, bf16[512,256]{1,0:T(8,128)(2,1)} %copy-done.3, ...), custom_call_target="tpu_custom_call" | custom-call | flops 17999998976 | bytes 18000000 | tf_op jit(solution)/shard_map/queries_near_rows/pallas_call | solution.py:295
  58.9 0.7 copy-done.12
  59.5 0.7 copy-done.13
  60.3 0.8 copy-done
  61.1 133.8 %late_rows_project_update_mlp.1 = bf16[256,1024]{1,0:T(8,128)(2,1)} custom-call(f32[16]{0:T(128)} %rate_s.3, bf16[256,1024]{1,0:T(8,128)(2,1)} %tok_ref.3, f32[1,1024]{1,0:T(1,128)} %bitcast.10, bf16[16,128,256]{2,1,0:T(8,128)(2,1)} %get-tuple-element.24.q_ref, f32[16,80,256]{2,1,0:T(8,128)} %get-tuple-element.25.part_ref, bf16[128,2,1152]{2,1,0:T(2,128)(2,1)} %copy-done, ...), custom_call_target="tpu_custom_call" | custom-call | flops 16999999488 | bytes 17000000 | tf_op jit(solution)/shard_map/late_rows_project_update_mlp/pallas_call | solution.py:457
  (40 shorter events, 0.1 us)
Async XLA Ops:
  2.7 22.2 %collective-permute-start = (bf16[512,256]{1,0:T(8,128)(2,1)}, bf16[512,256]{1,0:T(8,128)(2,1)S(1)}, u32[]{:S(2)}, u32[]{:S(2)}) collective-permute-start(bf16[512,256]{1,0:T(8,128)(2,1)} %get-tuple-element.17.kv_ref.rest_0_), channel_id=1, source_target_pairs={{0,2},{1,3},{2,4},{3,5},{4,6},{5,7},{6,0},{7,1},{8,10},{9,11},{10,... | collective-permute-start | bytes 786440 | tf_op jit(solution)/shard_map/ppermute | solution.py:509
  4.7 20.2 %collective-permute-start.1 = (bf16[512,256]{1,0:T(8,128)(2,1)}, bf16[512,256]{1,0:T(8,128)(2,1)S(1)}, u32[]{:S(2)}, u32[]{:S(2)}) collective-permute-start(bf16[512,256]{1,0:T(8,128)(2,1)} %get-tuple-element.17.kv_ref.rest_0_), channel_id=1, source_target_pairs={{0,6},{1,7},{2,0},{3,1},{4,2},{5,3},{6,4},{7,5},{8,14},{9,15},{10,... | collective-permute-start | bytes 786440 | tf_op jit(solution)/shard_map/ppermute | solution.py:509
  6.8 18.1 %collective-permute-start.2 = (bf16[512,256]{1,0:T(8,128)(2,1)}, bf16[512,256]{1,0:T(8,128)(2,1)S(1)}, u32[]{:S(2)}, u32[]{:S(2)}) collective-permute-start(bf16[512,256]{1,0:T(8,128)(2,1)} %get-tuple-element.17.kv_ref.rest_0_), channel_id=1, source_target_pairs={{0,8},{1,9},{2,10},{3,11},{4,12},{5,13},{6,14},{7,15},{8,0},{9,1},... | collective-permute-start | bytes 786440 | tf_op jit(solution)/shard_map/ppermute | solution.py:509
  8.3 16.6 %collective-permute-start.3 = (bf16[512,256]{1,0:T(8,128)(2,1)}, bf16[512,256]{1,0:T(8,128)(2,1)S(1)}, u32[]{:S(2)}, u32[]{:S(2)}) collective-permute-start(bf16[512,256]{1,0:T(8,128)(2,1)} %get-tuple-element.17.kv_ref.rest_0_), channel_id=1, source_target_pairs={{0,4},{1,5},{2,6},{3,7},{4,0},{5,1},{6,2},{7,3},{8,12},{9,13},{10,... | collective-permute-start | bytes 786440 | tf_op jit(solution)/shard_map/ppermute | solution.py:509
  10.2 14.8 %collective-permute-start.4 = (bf16[512,256]{1,0:T(8,128)(2,1)}, bf16[512,256]{1,0:T(8,128)(2,1)S(1)}, u32[]{:S(2)}, u32[]{:S(2)}) collective-permute-start(bf16[512,256]{1,0:T(8,128)(2,1)} %get-tuple-element.17.kv_ref.rest_0_), channel_id=1, source_target_pairs={{0,1},{1,0},{2,3},{3,2},{4,5},{5,4},{6,7},{7,6},{8,9},{9,8},{10,11... | collective-permute-start | bytes 786440 | tf_op jit(solution)/shard_map/ppermute | solution.py:509
  24.9 13.6 %copy-start.1 = (bf16[512,256]{1,0:T(8,128)(2,1)}, bf16[512,256]{1,0:T(8,128)(2,1)S(1)}, u32[]{:S(2)}) copy-start(bf16[512,256]{1,0:T(8,128)(2,1)S(1)} %collective-permute-done.rest_1_.rest_2_) | copy-start | bytes 786436
  24.9 13.6 %copy-start.2 = (bf16[512,256]{1,0:T(8,128)(2,1)}, bf16[512,256]{1,0:T(8,128)(2,1)S(1)}, u32[]{:S(2)}) copy-start(bf16[512,256]{1,0:T(8,128)(2,1)S(1)} %collective-permute-done.1.rest_2_.rest_3_) | copy-start | bytes 786436
  24.9 13.6 %copy-start.3 = (bf16[512,256]{1,0:T(8,128)(2,1)}, bf16[512,256]{1,0:T(8,128)(2,1)S(1)}, u32[]{:S(2)}) copy-start(bf16[512,256]{1,0:T(8,128)(2,1)S(1)} %collective-permute-done.2.rest_0_.rest_1_) | copy-start | bytes 786436
  25.0 13.5 %copy-start.4 = (bf16[512,256]{1,0:T(8,128)(2,1)}, bf16[512,256]{1,0:T(8,128)(2,1)S(1)}, u32[]{:S(2)}) copy-start(bf16[512,256]{1,0:T(8,128)(2,1)S(1)} %collective-permute-done.3.rest_3_.rest_4_) | copy-start | bytes 786436
  25.0 13.5 %copy-start.5 = (bf16[512,256]{1,0:T(8,128)(2,1)}, bf16[512,256]{1,0:T(8,128)(2,1)S(1)}, u32[]{:S(2)}) copy-start(bf16[512,256]{1,0:T(8,128)(2,1)S(1)} %collective-permute-done.4.rest_4_.rest_5_) | copy-start | bytes 786436
  25.0 4.4 %collective-permute-start.5 = (bf16[512,256]{1,0:T(8,128)(2,1)S(1)}, bf16[512,256]{1,0:T(8,128)(2,1)S(1)}, u32[]{:S(2)}, u32[]{:S(2)}) collective-permute-start(bf16[512,256]{1,0:T(8,128)(2,1)S(1)} %collective-permute-done.2.rest_0_.rest_1_), channel_id=1, source_target_pairs={{0,1},{1,0},{2,3},{3,2},{4,5},{5,4},{6,7},{7,6},{8,9},{9,8},{10,11... | collective-permute-start | bytes 786440 | tf_op jit(solution)/shard_map/ppermute | solution.py:509
  25.1 4.3 %collective-permute-start.6 = (bf16[512,256]{1,0:T(8,128)(2,1)S(1)}, bf16[512,256]{1,0:T(8,128)(2,1)S(1)}, u32[]{:S(2)}, u32[]{:S(2)}) collective-permute-start(bf16[512,256]{1,0:T(8,128)(2,1)S(1)} %collective-permute-done.rest_1_.rest_2_), channel_id=1, source_target_pairs={{0,1},{1,0},{2,3},{3,2},{4,5},{5,4},{6,7},{7,6},{8,9},{9,8},{10,11... | collective-permute-start | bytes 786440 | tf_op jit(solution)/shard_map/ppermute | solution.py:509
  25.6 12.0 %collective-permute-start.9 = (bf16[512,256]{1,0:T(8,128)(2,1)S(1)}, bf16[512,256]{1,0:T(8,128)(2,1)S(1)}, u32[]{:S(2)}, u32[]{:S(2)}) collective-permute-start(bf16[512,256]{1,0:T(8,128)(2,1)S(1)} %collective-permute-done.2.rest_0_.rest_1_), channel_id=1, source_target_pairs={{0,2},{1,3},{2,4},{3,5},{4,6},{5,7},{6,0},{7,1},{8,10},{9,11},{10,... | collective-permute-start | bytes 786440 | tf_op jit(solution)/shard_map/ppermute | solution.py:509
  26.7 11.0 %collective-permute-start.10 = (bf16[512,256]{1,0:T(8,128)(2,1)S(1)}, bf16[512,256]{1,0:T(8,128)(2,1)S(1)}, u32[]{:S(2)}, u32[]{:S(2)}) collective-permute-start(bf16[512,256]{1,0:T(8,128)(2,1)S(1)} %collective-permute-done.2.rest_0_.rest_1_), channel_id=1, source_target_pairs={{0,6},{1,7},{2,0},{3,1},{4,2},{5,3},{6,4},{7,5},{8,14},{9,15},{10,... | collective-permute-start | bytes 786440 | tf_op jit(solution)/shard_map/ppermute | solution.py:509
  28.8 9.4 %collective-permute-start.11 = (bf16[512,256]{1,0:T(8,128)(2,1)S(1)}, bf16[512,256]{1,0:T(8,128)(2,1)S(1)}, u32[]{:S(2)}, u32[]{:S(2)}) collective-permute-start(bf16[512,256]{1,0:T(8,128)(2,1)S(1)} %collective-permute-done.3.rest_3_.rest_4_), channel_id=1, source_target_pairs={{0,8},{1,9},{2,10},{3,11},{4,12},{5,13},{6,14},{7,15},{8,0},{9,1},... | collective-permute-start | bytes 786440 | tf_op jit(solution)/shard_map/ppermute | solution.py:509
  29.4 9.1 %collective-permute-start.7 = (bf16[512,256]{1,0:T(8,128)(2,1)S(1)}, bf16[512,256]{1,0:T(8,128)(2,1)S(1)}, u32[]{:S(2)}, u32[]{:S(2)}) collective-permute-start(bf16[512,256]{1,0:T(8,128)(2,1)S(1)} %collective-permute-done.1.rest_2_.rest_3_), channel_id=1, source_target_pairs={{0,1},{1,0},{2,3},{3,2},{4,5},{5,4},{6,7},{7,6},{8,9},{9,8},{10,11... | collective-permute-start | bytes 786440 | tf_op jit(solution)/shard_map/ppermute | solution.py:509
  29.4 9.1 %collective-permute-start.8 = (bf16[512,256]{1,0:T(8,128)(2,1)S(1)}, bf16[512,256]{1,0:T(8,128)(2,1)}, u32[]{:S(2)}, u32[]{:S(2)}) collective-permute-start(bf16[512,256]{1,0:T(8,128)(2,1)S(1)} %collective-permute-done.3.rest_3_.rest_4_), channel_id=1, source_target_pairs={{0,1},{1,0},{2,3},{3,2},{4,5},{5,4},{6,7},{7,6},{8,9},{9,8},{10,11... | collective-permute-start | bytes 786440 | tf_op jit(solution)/shard_map/ppermute | solution.py:509
  29.9 30.4 %all-to-all-start = ((bf16[128,2,1152]{2,1,0:T(2,128)(2,1)}), bf16[128,2,1152]{2,1,0:T(2,128)(2,1)S(1)}, u32[]{:S(2)}, u32[]{:S(2)}) async-start(bf16[128,2,1152]{2,1,0:T(2,128)(2,1)} %pool_tiles.1), calls=%async_computation | async-start | bytes 1179648 | tf_op jit(solution)/shard_map/all_to_all | solution.py:553
  37.6 21.2 %copy-start.8 = (bf16[512,256]{1,0:T(8,128)(2,1)}, bf16[512,256]{1,0:T(8,128)(2,1)S(1)}, u32[]{:S(2)}) copy-start(bf16[512,256]{1,0:T(8,128)(2,1)S(1)} %collective-permute-done.9.rest_10_.rest_16_) | copy-start | bytes 786436
  37.6 21.3 %collective-permute-start.12 = (bf16[512,256]{1,0:T(8,128)(2,1)S(1)}, bf16[512,256]{1,0:T(8,128)(2,1)S(1)}, u32[]{:S(2)}, u32[]{:S(2)}) collective-permute-start(bf16[512,256]{1,0:T(8,128)(2,1)S(1)} %collective-permute-done.9.rest_10_.rest_16_), channel_id=1, source_target_pairs={{0,1},{1,0},{2,3},{3,2},{4,5},{5,4},{6,7},{7,6},{8,9},{9,8},{10,11... | collective-permute-start | bytes 786440 | tf_op jit(solution)/shard_map/ppermute | solution.py:509
  37.7 21.1 %copy-start.9 = (bf16[512,256]{1,0:T(8,128)(2,1)}, bf16[512,256]{1,0:T(8,128)(2,1)S(1)}, u32[]{:S(2)}) copy-start(bf16[512,256]{1,0:T(8,128)(2,1)S(1)} %collective-permute-done.10.rest_11_.rest_17_) | copy-start | bytes 786436
  37.7 21.2 %collective-permute-start.13 = (bf16[512,256]{1,0:T(8,128)(2,1)S(1)}, bf16[512,256]{1,0:T(8,128)(2,1)S(1)}, u32[]{:S(2)}, u32[]{:S(2)}) collective-permute-start(bf16[512,256]{1,0:T(8,128)(2,1)S(1)} %collective-permute-done.10.rest_11_.rest_17_), channel_id=1, source_target_pairs={{0,1},{1,0},{2,3},{3,2},{4,5},{5,4},{6,7},{7,6},{8,9},{9,8},{10,11... | collective-permute-start | bytes 786440 | tf_op jit(solution)/shard_map/ppermute | solution.py:509
  38.2 20.6 %copy-start.10 = (bf16[512,256]{1,0:T(8,128)(2,1)}, bf16[512,256]{1,0:T(8,128)(2,1)S(1)}, u32[]{:S(2)}) copy-start(bf16[512,256]{1,0:T(8,128)(2,1)S(1)} %collective-permute-done.11.rest_12_.rest_18_) | copy-start | bytes 786436
  38.2 22.1 %collective-permute-start.14 = (bf16[512,256]{1,0:T(8,128)(2,1)S(1)}, bf16[512,256]{1,0:T(8,128)(2,1)}, u32[]{:S(2)}, u32[]{:S(2)}) collective-permute-start(bf16[512,256]{1,0:T(8,128)(2,1)S(1)} %collective-permute-done.11.rest_12_.rest_18_), channel_id=1, source_target_pairs={{0,1},{1,0},{2,3},{3,2},{4,5},{5,4},{6,7},{7,6},{8,9},{9,8},{10,11... | collective-permute-start | bytes 786440 | tf_op jit(solution)/shard_map/ppermute | solution.py:509
  (6 other events, 21.3 us)
